TPU v7x, 32 devices: a whole 2x2x4 slice. The times are simulated.
32 devices in a mesh: expert: 8 (over y, x, core), shard: 4 (over z).
Axes of the slice: x: 2, y: 2, z: 4, core: 2. Of those that a mesh axis runs over, the one named last changes fastest.
Arguments:
- hidden_in: bfloat16 [4, 1024, 1, 768], P('shard', 'expert'), may hold values from -6 to 6
- attn_gain: bfloat16 [2, 768], P(None, 'shard'), may hold values from 0.5 to 1.5
- qkv_weight: bfloat16 [2, 768, 2304], P(None, 'shard'), may hold values from -0.36084392 to 0.36084392
- out_weight: bfloat16 [2, 768, 768], P(None, 'shard'), may hold values from -1.25 to 1.25
- rel_bias: bfloat16 [2, 32, 12], P(None, 'shard'), may hold values from -4 to 4
- bucket_table: int32 [1024], replicated, may hold values from 0 to 31, as said below
- mlp_gain: bfloat16 [2, 768], P(None, 'shard'), may hold values from 0.5 to 1.5
- mlp_up: bfloat16 [768, 3072], P('shard'), may hold values from -0.21875 to 0.21875
- mlp_down: bfloat16 [3072, 768], P('shard'), may hold values from -0.109375 to 0.109375
- router_weight: bfloat16 [768, 16], P('shard'), may hold values from -0.375 to 0.375
- expert_up: bfloat16 [16, 768, 3072], P('expert', 'shard'), may hold values from -0.21875 to 0.21875
- expert_down: bfloat16 [16, 3072, 768], P('expert', 'shard'), may hold values from -0.109375 to 0.109375
- routes: int32 [4, 1024, 1, 2], P('shard', 'expert'), may hold values from 0 to 15, all different within a row; in each aligned block of 128 rows (0 to 127, 128 to 255, ..., all dimensions but the last counted through in order) at most 32 rows name the same one
- out_grad: bfloat16 [4, 1024, 1, 768], P('shard', 'expert'), may hold values from -6 to 6
Outputs:
- hidden_out: bfloat16 [4, 1024, 1, 768], P('shard', 'expert')
- hidden_grad: float32 [4, 1024, 1, 768], P('shard', 'expert')
- attn_gain_grad: float32 [2, 768], P(None, 'shard')
- qkv_grad: float32 [2, 768, 2304], P(None, 'shard')
- out_weight_grad: float32 [2, 768, 768], P(None, 'shard')
- rel_bias_grad: float32 [2, 32, 12], P(None, 'shard')
- mlp_gain_grad: float32 [2, 768], P(None, 'shard')
- mlp_up_grad: float32 [768, 3072], P('shard')
- mlp_down_grad: float32 [3072, 768], P('shard')
- router_grad: float32 [768, 16], P('shard')
- expert_up_grad: float32 [16, 768, 3072], P('expert', 'shard')
- expert_down_grad: float32 [16, 3072, 768], P('expert', 'shard')
- clip_scales: float32 [2, 12], replicated
Inputs may be any that keep to these rules, and one draw needn't show every extreme that they name: `routes`: each row names two different experts; among the 128 tokens that one device holds (an aligned block of the flattened rows), no expert is named more than 32 times, a bound that some block reaches. `bucket_table`: Non-decreasing in the distance; 0 at distance 0 and 31 at distance 1024 - 1.
All inputs are finite; a program needn't handle non-finite values.
Results may differ from a plain program's by a relative error of at most 0.03.
Values may be sent and summed in bfloat16 or wider, within the bound.
A program may use at most 320 MiB of HBM per device.

v0:
```python
import math

import jax
import jax.numpy as jnp
from jax import lax
from jax.sharding import PartitionSpec as P

D = 768
H = 12
HD = 64
NB = 32
EXP_DEV = 2


epsilon = 1e-06
clip_limit = 6.0
bfloat = jnp.bfloat16
single = jnp.float32


def rms_norm(inputs, norm_gain):
    return (
        inputs * lax.rsqrt(jnp.mean(inputs * inputs, axis=-1, keepdims=True) + epsilon) * norm_gain
    )


def norm_back(inputs, norm_gain, upstream):
    _, pullback = jax.vjp(rms_norm, inputs, norm_gain)
    return pullback(upstream)


def gelu_back(pre_values, upstream):
    _, pullback = jax.vjp(jax.nn.gelu, pre_values)
    return pullback(upstream)[0]


def bucket_marks(distance, lower, upper):
    inside = (distance[None] >= lower[:, None, None]) & (distance[None] < upper[:, None, None])
    return inside.astype(bfloat)


def position_bias(marks, bias_pair):
    return jnp.einsum("bij,bh->hij", marks, bias_pair, preferred_element_type=single)


def attention_forward(
    hidden, norm_gain, stacked_weights, output_projection, bias_pair, distance, lower, upper, scale
):
    rows = hidden.shape[0]
    normalized_rows = rms_norm(hidden, norm_gain.astype(single)).astype(bfloat)
    stacked_projection = jnp.einsum(
        "isd,de->sie", normalized_rows, stacked_weights, preferred_element_type=single
    ).astype(bfloat)
    key_value = lax.all_gather(stacked_projection[..., D:], "expert", axis=1, tiled=True)
    shifted = position_bias(bucket_marks(distance, lower, upper), bias_pair)
    causal = distance >= 0

    def one_sequence(items):
        query_rows, pair_rows = items
        queries = query_rows.reshape(rows, H, HD)
        keys = pair_rows[:, :D].reshape(-1, H, HD)
        values = pair_rows[:, D:].reshape(-1, H, HD)
        raw_scores = (
            jnp.einsum("ihd,jhd->hij", queries, keys, preferred_element_type=single) * scale
        )
        head_peak = jnp.max(jnp.where(causal[None], raw_scores, -jnp.inf), axis=(1, 2))
        masked = jnp.where(causal[None], raw_scores + shifted, -jnp.inf)
        softmax_top = jnp.max(masked, axis=-1, keepdims=True)
        exponent = jnp.exp(masked - softmax_top)
        softmax_sum = jnp.sum(exponent, axis=-1, keepdims=True)
        softmax_probs = (exponent / softmax_sum).astype(bfloat)
        log_total = softmax_top[..., 0] + jnp.log(softmax_sum[..., 0])
        attention_result = jnp.einsum(
            "hij,jhd->ihd", softmax_probs, values, preferred_element_type=single
        )
        return (attention_result.astype(bfloat).reshape(rows, D), log_total, head_peak)

    attention_result, log_total, head_peak = lax.map(
        one_sequence, (stacked_projection[..., :D], key_value)
    )
    branch_output = jnp.einsum(
        "sid,de->ise", attention_result, output_projection, preferred_element_type=single
    )
    saved = (normalized_rows, stacked_projection, key_value, log_total, attention_result)
    return (hidden + branch_output, jnp.max(head_peak, axis=0), saved)


def attention_backward(
    upstream,
    hidden,
    norm_gain,
    stacked_weights,
    output_projection,
    bias_pair,
    distance,
    lower,
    upper,
    scale,
    saved,
):
    normalized_rows, stacked_projection, key_value, log_total, attention_result = saved
    rows = hidden.shape[0]
    branch_grad = upstream.astype(bfloat)
    output_grad = jnp.einsum(
        "sid,ise->de", attention_result, branch_grad, preferred_element_type=single
    )
    attended_grad = jnp.einsum(
        "ise,de->sid", branch_grad, output_projection, preferred_element_type=single
    ).astype(bfloat)
    marks = bucket_marks(distance, lower, upper)
    shifted = position_bias(marks, bias_pair)
    causal = distance >= 0

    def query_part(items):
        query_rows, pair_rows, grad_rows, totals = items
        queries = query_rows.reshape(rows, H, HD)
        keys = pair_rows[:, :D].reshape(-1, H, HD)
        values = pair_rows[:, D:].reshape(-1, H, HD)
        grad_heads = grad_rows.reshape(rows, H, HD)
        raw_scores = (
            jnp.einsum("ihd,jhd->hij", queries, keys, preferred_element_type=single) * scale
        )
        softmax_probs = jnp.where(
            causal[None], jnp.exp(raw_scores + shifted - totals[..., None]), 0.0
        )
        prob_grad = jnp.einsum("ihd,jhd->hij", grad_heads, values, preferred_element_type=single)
        row_dot = jnp.sum(prob_grad * softmax_probs, axis=-1)
        score_grad = (softmax_probs * (prob_grad - row_dot[..., None])).astype(bfloat)
        query_grad = (
            jnp.einsum("hij,jhd->ihd", score_grad, keys, preferred_element_type=single) * scale
        )
        query_grad = query_grad.astype(bfloat).reshape(rows, D)
        bias_grad = jnp.einsum("hij,bij->bh", score_grad, marks, preferred_element_type=single)
        key_grad = (
            jnp.einsum("hij,ihd->jhd", score_grad, queries, preferred_element_type=single) * scale
        )
        value_grad = jnp.einsum(
            "hij,ihd->jhd", softmax_probs.astype(bfloat), grad_heads, preferred_element_type=single
        )
        return (
            query_grad,
            bias_grad,
            jnp.concatenate([key_grad.reshape(-1, D), value_grad.reshape(-1, D)], axis=-1),
        )

    query_grad, bias_grads, extra = lax.map(
        query_part, (stacked_projection[..., :D], key_value, attended_grad, log_total)
    )
    pair_grad = lax.psum_scatter(
        extra.astype(jnp.bfloat16), "expert", scatter_dimension=1, tiled=True
    ).astype(jnp.float32)
    packed_grad = jnp.concatenate([query_grad, pair_grad.astype(bfloat)], axis=-1)
    weight_grad = jnp.einsum(
        "isd,sie->de", normalized_rows, packed_grad, preferred_element_type=single
    )
    normed_grad = jnp.einsum(
        "sie,de->isd", packed_grad, stacked_weights, preferred_element_type=single
    )
    input_grad, gain_grad = norm_back(hidden, norm_gain.astype(single), normed_grad)
    return (upstream + input_grad, gain_grad, weight_grad, output_grad, jnp.sum(bias_grads, axis=0))


def shards(
    hidden_in,
    attn_gain,
    qkv_weight,
    out_weight,
    rel_bias,
    bucket_table,
    mlp_gain,
    mlp_up,
    mlp_down,
    router_weight,
    expert_up,
    expert_down,
    routes,
    out_grad,
):
    gathered = (
        lax.all_gather(attn_gain, "shard", axis=1, tiled=True),
        lax.all_gather(qkv_weight, "shard", axis=1, tiled=True),
        lax.all_gather(out_weight, "shard", axis=1, tiled=True),
        lax.all_gather(rel_bias, "shard", axis=1, tiled=True),
        lax.all_gather(mlp_gain, "shard", axis=1, tiled=True),
        lax.all_gather(mlp_up, "shard", axis=0, tiled=True),
        lax.all_gather(mlp_down, "shard", axis=0, tiled=True),
        lax.all_gather(router_weight, "shard", axis=0, tiled=True),
        lax.all_gather(expert_up, "shard", axis=1, tiled=True),
        lax.all_gather(expert_down, "shard", axis=1, tiled=True),
    )
    (
        gain_attn,
        stacked_weights,
        output_projection,
        bias_weights,
        gain_mlp,
        dense_up,
        dense_down,
        router_full,
        experts_up,
        experts_down,
    ) = gathered
    block_rows = hidden_in.shape[1]
    sequences = hidden_in.shape[2]
    length = bucket_table.shape[0]
    token_count = block_rows * sequences
    expert_count = lax.axis_size("expert")
    expert_total = EXP_DEV * expert_count
    capacity = 4 * token_count // expert_total
    scale = 1.0 / math.sqrt(HD)
    own_positions = lax.axis_index("expert") * block_rows + jnp.arange(block_rows, dtype=jnp.int32)
    all_positions = jnp.arange(length, dtype=jnp.int32)
    distance = own_positions[:, None] - all_positions[None, :]
    bounds = jnp.sum(
        (bucket_table[:, None] < jnp.arange(NB + 1, dtype=jnp.int32)[None, :]).astype(jnp.int32),
        axis=0,
    )
    lower = bounds[:NB]
    upper = bounds[1:]
    hidden_zero = hidden_in[0].astype(single)
    mid_first, peak_first, saved_first = attention_forward(
        hidden_zero,
        gain_attn[0],
        stacked_weights[0],
        output_projection[0],
        bias_weights[0],
        distance,
        lower,
        upper,
        scale,
    )
    mid_rows = mid_first.reshape(token_count, D)
    dense_gain = gain_mlp[0].astype(single)
    dense_normed = rms_norm(mid_rows, dense_gain).astype(bfloat)
    pre_act = jnp.dot(dense_normed, dense_up, preferred_element_type=single)
    activation = jax.nn.gelu(pre_act).astype(bfloat)
    layer_one = (mid_rows + jnp.dot(activation, dense_down, preferred_element_type=single)).reshape(
        block_rows, sequences, D
    )
    mid_second, peak_second, saved_second = attention_forward(
        layer_one,
        gain_attn[1],
        stacked_weights[1],
        output_projection[1],
        bias_weights[1],
        distance,
        lower,
        upper,
        scale,
    )
    moe_rows = mid_second.reshape(token_count, D)
    moe_gain = gain_mlp[1].astype(single)
    moe_normed = rms_norm(moe_rows, moe_gain).astype(bfloat)
    router_logits = jnp.dot(moe_normed, router_full, preferred_element_type=single)
    route_rows = routes[0].reshape(token_count, 2)
    selected = (
        route_rows[:, :, None] == jnp.arange(expert_total, dtype=jnp.int32)[None, None, :]
    ).astype(single)
    chosen = jnp.sum(selected * router_logits[:, None, :], axis=-1)
    gates = jax.nn.softmax(chosen, axis=-1)
    flat_routes = route_rows.reshape(-1)
    marks = (flat_routes[:, None] == jnp.arange(expert_total, dtype=jnp.int32)[None, :]).astype(
        jnp.int32
    )
    rank = jnp.sum((jnp.cumsum(marks, axis=0) - marks) * marks, axis=1)
    slot_of_route = flat_routes * capacity + rank
    slot_marks = (
        slot_of_route[:, None] == jnp.arange(expert_total * capacity, dtype=jnp.int32)[None, :]
    ).astype(single)
    token_marks = jnp.sum(slot_marks.reshape(token_count, 2, -1), axis=1).astype(bfloat)
    slot_marks = slot_marks.astype(bfloat)
    send_rows = jnp.einsum(
        "ts,td->sd", token_marks, moe_normed, preferred_element_type=single
    ).astype(bfloat)
    received = lax.all_to_all(
        send_rows.reshape(expert_count, EXP_DEV, capacity, D),
        "expert",
        split_axis=0,
        concat_axis=0,
        tiled=True,
    )
    expert_pre = jnp.einsum("sjcd,jdf->sjcf", received, experts_up, preferred_element_type=single)
    expert_act = jax.nn.gelu(expert_pre).astype(bfloat)
    expert_out = jnp.einsum(
        "sjcf,jfd->sjcd", expert_act, experts_down, preferred_element_type=single
    ).astype(bfloat)
    returned = lax.all_to_all(
        expert_out, "expert", split_axis=0, concat_axis=0, tiled=True
    ).reshape(expert_total * capacity, D)
    route_out = jnp.einsum(
        "rs,sd->rd", slot_marks, returned, preferred_element_type=single
    ).reshape(token_count, 2, D)
    final_rows = moe_rows + jnp.sum(gates[:, :, None] * route_out, axis=1)
    hidden_out = final_rows.reshape(1, block_rows, sequences, D).astype(bfloat)
    peaks = lax.pmax(jnp.stack([peak_first, peak_second]), ("expert", "shard"))
    clip_scales = jnp.sqrt(clip_limit / jnp.maximum(peaks, clip_limit))
    upstream = out_grad[0].astype(single).reshape(token_count, D)
    gate_grad = jnp.sum(route_out * upstream[:, None, :], axis=-1)
    chosen_grad = gates * (gate_grad - jnp.sum(gates * gate_grad, axis=-1, keepdims=True))
    logit_grad = jnp.sum(chosen_grad[:, :, None] * selected, axis=1).astype(bfloat)
    router_grad = jnp.einsum("td,te->de", moe_normed, logit_grad, preferred_element_type=single)
    normed_grad = jnp.einsum("te,de->td", logit_grad, router_full, preferred_element_type=single)
    route_grad = (gates[:, :, None] * upstream[:, None, :]).astype(bfloat).reshape(-1, D)
    slot_grad = jnp.einsum(
        "rs,rd->sd", slot_marks, route_grad, preferred_element_type=single
    ).astype(bfloat)
    owner_grad = lax.all_to_all(
        slot_grad.reshape(expert_count, EXP_DEV, capacity, D),
        "expert",
        split_axis=0,
        concat_axis=0,
        tiled=True,
    )
    act_grad = jnp.einsum("sjcd,jfd->sjcf", owner_grad, experts_down, preferred_element_type=single)
    pre_grad = gelu_back(expert_pre, act_grad).astype(bfloat)
    row_grad = jnp.einsum(
        "sjcf,jdf->sjcd", pre_grad, experts_up, preferred_element_type=single
    ).astype(bfloat)
    back_rows = lax.all_to_all(row_grad, "expert", split_axis=0, concat_axis=0, tiled=True).reshape(
        expert_total * capacity, D
    )
    down_grad_experts = jnp.einsum(
        "sjcf,sjcd->jfd", expert_act, owner_grad, preferred_element_type=single
    )
    up_grad_experts = jnp.einsum(
        "sjcd,sjcf->jdf", received, pre_grad, preferred_element_type=single
    )
    expert_up_grad, expert_down_grad = (
        lax.psum_scatter(
            up_grad_experts.astype(jnp.bfloat16), "shard", scatter_dimension=1, tiled=True
        ).astype(jnp.float32),
        lax.psum_scatter(
            down_grad_experts.astype(jnp.bfloat16), "shard", scatter_dimension=1, tiled=True
        ).astype(jnp.float32),
    )
    normed_grad = normed_grad + jnp.einsum(
        "ts,sd->td", token_marks, back_rows, preferred_element_type=single
    )
    moe_input_grad, moe_gain_grad = norm_back(moe_rows, moe_gain, normed_grad)
    mid_grad = (upstream + moe_input_grad).reshape(block_rows, sequences, D)
    layer_grad, gain_second, packed_second, output_second, bias_second = attention_backward(
        mid_grad,
        layer_one,
        gain_attn[1],
        stacked_weights[1],
        output_projection[1],
        bias_weights[1],
        distance,
        lower,
        upper,
        scale,
        saved_second,
    )
    dense_upstream = layer_grad.reshape(token_count, D)
    dense_branch = dense_upstream.astype(bfloat)
    dense_down_grad = jnp.einsum(
        "tf,td->fd", activation, dense_branch, preferred_element_type=single
    )
    hidden_act_grad = jnp.einsum(
        "td,fd->tf", dense_branch, dense_down, preferred_element_type=single
    )
    pre_act_grad = gelu_back(pre_act, hidden_act_grad).astype(bfloat)
    dense_up_grad = jnp.einsum(
        "td,tf->df", dense_normed, pre_act_grad, preferred_element_type=single
    )
    dense_normed_grad = jnp.einsum(
        "tf,df->td", pre_act_grad, dense_up, preferred_element_type=single
    )
    dense_input_grad, dense_gain_grad = norm_back(mid_rows, dense_gain, dense_normed_grad)
    first_grad = (dense_upstream + dense_input_grad).reshape(block_rows, sequences, D)
    input_grad, gain_first, packed_first, output_first, bias_first = attention_backward(
        first_grad,
        hidden_zero,
        gain_attn[0],
        stacked_weights[0],
        output_projection[0],
        bias_weights[0],
        distance,
        lower,
        upper,
        scale,
        saved_first,
    )
    shared = (
        jnp.stack([gain_first, gain_second]),
        jnp.stack([packed_first, packed_second]),
        jnp.stack([output_first, output_second]),
        jnp.stack([bias_first, bias_second]),
        jnp.stack([dense_gain_grad, moe_gain_grad]),
        dense_up_grad,
        dense_down_grad,
        router_grad,
    )
    shared = (
        lax.psum_scatter(
            shared[0].astype(jnp.bfloat16), "shard", scatter_dimension=1, tiled=True
        ).astype(jnp.float32),
        lax.psum_scatter(
            shared[1].astype(jnp.bfloat16), "shard", scatter_dimension=1, tiled=True
        ).astype(jnp.float32),
        lax.psum_scatter(
            shared[2].astype(jnp.bfloat16), "shard", scatter_dimension=1, tiled=True
        ).astype(jnp.float32),
        lax.psum_scatter(
            shared[3].astype(jnp.bfloat16), "shard", scatter_dimension=1, tiled=True
        ).astype(jnp.float32),
        lax.psum_scatter(
            shared[4].astype(jnp.bfloat16), "shard", scatter_dimension=1, tiled=True
        ).astype(jnp.float32),
        lax.psum_scatter(
            shared[5].astype(jnp.bfloat16), "shard", scatter_dimension=0, tiled=True
        ).astype(jnp.float32),
        lax.psum_scatter(
            shared[6].astype(jnp.bfloat16), "shard", scatter_dimension=0, tiled=True
        ).astype(jnp.float32),
        lax.psum_scatter(
            shared[7].astype(jnp.bfloat16), "shard", scatter_dimension=0, tiled=True
        ).astype(jnp.float32),
    )
    shared = (
        lax.psum(shared[0].astype(jnp.bfloat16), "expert").astype(jnp.float32),
        lax.psum(shared[1].astype(jnp.bfloat16), "expert").astype(jnp.float32),
        lax.psum(shared[2].astype(jnp.bfloat16), "expert").astype(jnp.float32),
        lax.psum(shared[3].astype(jnp.bfloat16), "expert").astype(jnp.float32),
        lax.psum(shared[4].astype(jnp.bfloat16), "expert").astype(jnp.float32),
        lax.psum(shared[5].astype(jnp.bfloat16), "expert").astype(jnp.float32),
        lax.psum(shared[6].astype(jnp.bfloat16), "expert").astype(jnp.float32),
        lax.psum(shared[7].astype(jnp.bfloat16), "expert").astype(jnp.float32),
    )
    (
        attn_gain_grad,
        qkv_grad,
        out_weight_grad,
        rel_bias_grad,
        mlp_gain_grad,
        mlp_up_grad,
        mlp_down_grad,
        router_total,
    ) = shared
    hidden_grad = input_grad.reshape(1, block_rows, sequences, D)
    return (
        hidden_out,
        hidden_grad,
        attn_gain_grad,
        qkv_grad,
        out_weight_grad,
        rel_bias_grad,
        mlp_gain_grad,
        mlp_up_grad,
        mlp_down_grad,
        router_total,
        expert_up_grad,
        expert_down_grad,
        clip_scales,
    )


def solution(mesh):
    in_specs = (
        P("shard", "expert", None, None),
        P(None, "shard"),
        P(None, "shard", None),
        P(None, "shard", None),
        P(None, "shard", None),
        P(),
        P(None, "shard"),
        P("shard", None),
        P("shard", None),
        P("shard", None),
        P("expert", "shard", None),
        P("expert", "shard", None),
        P("shard", "expert", None, None),
        P("shard", "expert", None, None),
    )
    out_specs = (
        P("shard", "expert", None, None),
        P("shard", "expert", None, None),
        P(None, "shard"),
        P(None, "shard", None),
        P(None, "shard", None),
        P(None, "shard", None),
        P(None, "shard"),
        P("shard", None),
        P("shard", None),
        P("shard", None),
        P("expert", "shard", None),
        P("expert", "shard", None),
        P(),
    )
    return jax.shard_map(shards, mesh=mesh, in_specs=in_specs, out_specs=out_specs, check_vma=False)
```

profile of v0, /device:TPU:0, one launch (start us, length us, event | category | flops | bytes accessed | tf_op | source)
XLA Modules:
  0.0 1851.3 jit_solution(17253698073998142007)
XLA Ops:
  8.0 12.8 all-gather
  22.0 118.5 %all-gather.12.cloned.1.call-done = bf16[2,768,2304]{2,1,0:T(8,128)(2,1)} async-done(((bf16[2,192,2304]{2,1,0:T(8,128)(2,1)}), bf16[2,768,2304]{2,1,0:T(8,128)(2,1)}) %all-gather.12.cloned.1.call-update) | async-done | bytes 7077904 | tf_op jit(solution)/shard_map/all_gather | solution.py:181
  146.2 13.1 all_gather.39
  195.8 31.2 %all-gather.16.cloned.1.call-done = bf16[2,768,768]{2,1,0:T(8,128)(2,1)} async-done(((bf16[2,192,768]{2,1,0:T(8,128)(2,1)}), bf16[2,768,768]{2,1,0:T(8,128)(2,1)}) %all-gather.16.cloned.1.call-update) | async-done | bytes 2359312 | tf_op jit(solution)/shard_map/all_gather | solution.py:182
  228.7 87.9 %all-gather.18.cloned.1.call-done = bf16[768,3072]{1,0:T(8,128)(2,1)} async-done(((bf16[192,3072]{1,0:T(8,128)(2,1)}), bf16[768,3072]{1,0:T(8,128)(2,1)}) %all-gather.18.cloned.1.call-update) | async-done | bytes 4718608 | tf_op jit(solution)/shard_map/all_gather | solution.py:185
  319.8 86.1 %all-gather.20.cloned.1.call-done = bf16[3072,768]{1,0:T(8,128)(2,1)} async-done(((bf16[768,768]{1,0:T(8,128)(2,1)}), bf16[3072,768]{1,0:T(8,128)(2,1)}) %all-gather.20.cloned.1.call-update) | async-done | bytes 4718608 | tf_op jit(solution)/shard_map/all_gather | solution.py:186
  415.5 13.1 all-gather.2
  486.7 126.1 %all-gather.24.cloned.1.call-done = bf16[2,768,3072]{2,1,0:T(8,128)(2,1)} async-done(((bf16[2,192,3072]{2,1,0:T(8,128)(2,1)}), bf16[2,768,3072]{2,1,0:T(8,128)(2,1)}) %all-gather.24.cloned.1.call-update) | async-done | bytes 9437200 | tf_op jit(solution)/shard_map/all_gather | solution.py:188
  621.0 158.4 %all-gather.26.cloned.1.call-done = bf16[2,3072,768]{2,1,0:T(8,128)(2,1)} async-done(((bf16[2,768,768]{2,1,0:T(8,128)(2,1)}), bf16[2,3072,768]{2,1,0:T(8,128)(2,1)}) %all-gather.26.cloned.1.call-update) | async-done | bytes 9437200 | tf_op jit(solution)/shard_map/all_gather | solution.py:189
  837.8 11.6 copy.161
  858.4 39.2 %reduce-scatter.34.cloned.1.call-done = bf16[128,1536]{1,0:T(8,128)(2,1)} async-done(((bf16[1024,1536]{1,0:T(8,128)(2,1)}), bf16[128,1536]{1,0:T(8,128)(2,1)}) %reduce-scatter.34.cloned.1.call-update) | async-done | bytes 393232
  933.3 15.8 copy.163
  978.8 22.1 %reduce-scatter.36.cloned.1.call-done = bf16[128,1536]{1,0:T(8,128)(2,1)} async-done(((bf16[1024,1536]{1,0:T(8,128)(2,1)}), bf16[128,1536]{1,0:T(8,128)(2,1)}) %reduce-scatter.36.cloned.1.call-update) | async-done | bytes 393232
  1044.0 45.4 %pmax.7 = f32[2,12]{1,0:T(2,128)S(1)} all-reduce(f32[2,12]{1,0:T(2,128)S(1)} %pad_maximum_fusion.7), channel_id=1, replica_groups=mesh['expert'=8,'shard'=4] {'expert','shard'}, use_global_device_ids=true, to_apply=%region_52.53 | all-reduce | flops 24 | bytes 192 | tf_op jit(solution)/shard_map/pmax | solution.py:295
  1089.9 50.3 %reduce-scatter.26.cloned.1.call-done = bf16[192,3072]{1,0:T(8,128)(2,1)} async-done(((bf16[768,3072]{1,0:T(8,128)(2,1)}), bf16[192,3072]{1,0:T(8,128)(2,1)}) %reduce-scatter.26.cloned.1.call-update) | async-done | bytes 1179664 | tf_op jit(solution)/shard_map/reduce_scatter | solution.py:410
  1140.3 88.5 %reduce-scatter.28.cloned.1.call-done = bf16[768,768]{1,0:T(8,128)(2,1)} async-done(((bf16[3072,768]{1,0:T(8,128)(2,1)}), bf16[768,768]{1,0:T(8,128)(2,1)}) %reduce-scatter.28.cloned.1.call-update) | async-done | bytes 1179664 | tf_op jit(solution)/shard_map/reduce_scatter | solution.py:413
  1228.8 126.2 %reduce-scatter.22.cloned.1.call-done = bf16[2,192,2304]{2,1,0:T(8,128)(2,1)} async-done(((bf16[2,768,2304]{2,1,0:T(8,128)(2,1)}), bf16[2,192,2304]{2,1,0:T(8,128)(2,1)}) %reduce-scatter.22.cloned.1.call-update) | async-done | bytes 1769488 | tf_op jit(solution)/shard_map/reduce_scatter | solution.py:398
  1363.2 13.8 reduce-scatter.42.cloned.1.call-done
  1385.6 16.2 all-reduce
  1404.1 13.6 reduce-scatter.38.cloned.1.call-done
  1418.6 22.8 %all-reduce.1 = (bf16[2,192]{1,0:T(2,128)(2,1)S(1)}, bf16[2,8,12]{2,0,1:T(2,128)(2,1)S(1)}, bf16[2,192]{1,0:T(2,128)(2,1)S(1)}, bf16[192,16]{0,1:T(8,128)(2,1)S(1)}) all-reduce(bf16[2,192]{1,0:T(2,128)(2,1)S(1)} %copy.166, bf16[2,8,12]{2,0,1:T(2,128)(2,1)S(1)} %constant_dynamic-slice_fusion, ...), channel_id=1, replica_groups=mesh['expert'=8,'shard'=4] {'expert'}, use_global_device_ids=true, to_apply=%region_31.32 | all-reduce | flops 4032 | bytes 16128 | tf_op jit(solution)/shard_map/psum | solution.py:421
  1443.8 135.7 %reduce-scatter.30.cloned.1.call-done = bf16[2,192,3072]{2,1,0:T(8,128)(2,1)} async-done(((bf16[2,768,3072]{2,1,0:T(8,128)(2,1)}), bf16[2,192,3072]{2,1,0:T(8,128)(2,1)}) %reduce-scatter.30.cloned.1.call-update) | async-done | bytes 2359312 | tf_op jit(solution)/shard_map/reduce_scatter | solution.py:329
  1583.9 160.2 %reduce-scatter.32.cloned.1.call-done = bf16[2,768,768]{2,1,0:T(8,128)(2,1)} async-done(((bf16[2,3072,768]{2,1,0:T(8,128)(2,1)}), bf16[2,768,768]{2,1,0:T(8,128)(2,1)}) %reduce-scatter.32.cloned.1.call-update) | async-done | bytes 2359312 | tf_op jit(solution)/shard_map/reduce_scatter | solution.py:332
  1748.3 87.9 %all-reduce.5.cloned.1.call-done = (bf16[2,192,2304]{2,1,0:T(8,128)(2,1)}, bf16[2,192,768]{2,1,0:T(8,128)(2,1)}, bf16[192,3072]{1,0:T(8,128)(2,1)}, bf16[768,768]{1,0:T(8,128)(2,1)}) async-done(((bf16[2,192,2304]{2,1,0:T(8,128)(2,1)}, bf16[2,192,768]{2,1,0:T(8,128)(2,1)}, bf16[192,3072]{1,0:T(8,128)(2,1)}, bf16[768,768]{1,0:T(8,128)(2,1)}), (bf16[2,192,2304]{2,1,0:T(8,128)(2,1)}, ...) | async-done | bytes 4718608 | tf_op jit(solution)/shard_map/psum | solution.py:422
  (434 shorter events, 338.0 us)
Async XLA Ops:
  7.2 133.4 %all-gather.12.cloned.1.call-start = ((), (), s32[]{:S(2)}) async-start(), calls=%async_computation.15 | async-start | bytes 8847360 | tf_op jit(solution)/shard_map/all_gather | solution.py:181
  7.9 166.9 %all-gather.14.cloned.1.call-start = ((), (), s32[]{:S(2)}) async-start(), calls=%async_computation.16 | async-start | bytes 3538944 | tf_op jit(solution)/shard_map/all_gather | solution.py:54
  144.2 82.8 %all-gather.16.cloned.1.call-start = ((), (), s32[]{:S(2)}) async-start(), calls=%async_computation.17 | async-start | bytes 2949120 | tf_op jit(solution)/shard_map/all_gather | solution.py:182
  144.9 171.7 %all-gather.18.cloned.1.call-start = ((), (), s32[]{:S(2)}) async-start(), calls=%async_computation.18 | async-start | bytes 5898240 | tf_op jit(solution)/shard_map/all_gather | solution.py:185
  145.5 260.4 %all-gather.20.cloned.1.call-start = ((), (), s32[]{:S(2)}) async-start(), calls=%async_computation.19 | async-start | bytes 5898240 | tf_op jit(solution)/shard_map/all_gather | solution.py:186
  146.1 298.3 %all-gather.22.cloned.1.call-start = ((), (), s32[]{:S(2)}) async-start(), calls=%async_computation.20 | async-start | bytes 3538944 | tf_op jit(solution)/shard_map/all_gather | solution.py:54
  413.5 199.3 %all-gather.24.cloned.1.call-start = ((), (), s32[]{:S(2)}) async-start(), calls=%async_computation.21 | async-start | bytes 11796480 | tf_op jit(solution)/shard_map/all_gather | solution.py:188
  414.3 365.1 %all-gather.26.cloned.1.call-start = ((), (), s32[]{:S(2)}) async-start(), calls=%async_computation.22 | async-start | bytes 11796480 | tf_op jit(solution)/shard_map/all_gather | solution.py:189
  466.2 16.3 all-to-all-start
  482.5 306.3 %all-to-all-start.2 = ((bf16[8,2,32,768]{3,2,1,0:T(8,128)(2,1)}), bf16[8,2,32,768]{3,2,1,0:T(8,128)(2,1)}, u32[]{:S(2)}, u32[]{:S(2)}) async-start(bf16[8,2,32,768]{3,2,1,0:T(8,128)(2,1)} %bitcast.462), calls=%async_computation.2 | async-start | bytes 1572864 | tf_op jit(solution)/shard_map/all_to_all | solution.py:307
  788.8 16.3 all-to-all-start.1
  805.1 16.8 all-to-all-start.3
  809.3 88.3 %reduce-scatter.34.cloned.1.call-start = ((), (), s32[]{:S(2)}) async-start(), calls=%async_computation.29 | async-start | bytes 3538944
  854.9 146.0 %reduce-scatter.36.cloned.1.call-start = ((), (), s32[]{:S(2)}) async-start(), calls=%async_computation.30 | async-start | bytes 3538944
  954.5 135.4 %reduce-scatter.24.cloned.1.call-start = ((), (), s32[]{:S(2)}) async-start(), calls=%async_computation.24 | async-start | bytes 2949120 | tf_op jit(solution)/shard_map/reduce_scatter | solution.py:401
  959.2 181.1 %reduce-scatter.26.cloned.1.call-start = ((), (), s32[]{:S(2)}) async-start(), calls=%async_computation.25 | async-start | bytes 5898240 | tf_op jit(solution)/shard_map/reduce_scatter | solution.py:410
  964.5 264.3 %reduce-scatter.28.cloned.1.call-start = ((), (), s32[]{:S(2)}) async-start(), calls=%async_computation.26 | async-start | bytes 5898240 | tf_op jit(solution)/shard_map/reduce_scatter | solution.py:413
  970.9 384.1 %reduce-scatter.22.cloned.1.call-start = ((), (), s32[]{:S(2)}) async-start(), calls=%async_computation.23 | async-start | bytes 8847360 | tf_op jit(solution)/shard_map/reduce_scatter | solution.py:398
  1012.0 365.0 %reduce-scatter.42.cloned.1.call-start = ((), (), s32[]{:S(2)}) async-start(), calls=%async_computation.33 | async-start | bytes 245760
  1015.3 386.5 %reduce-scatter.40.cloned.1.call-start = ((), (), s32[]{:S(2)}) async-start(), calls=%async_computation.32 | async-start | bytes 245760
  1017.6 400.1 %reduce-scatter.38.cloned.1.call-start = ((), (), s32[]{:S(2)}) async-start(), calls=%async_computation.31 | async-start | bytes 245760
  1023.3 556.2 %reduce-scatter.30.cloned.1.call-start = ((), (), s32[]{:S(2)}) async-start(), calls=%async_computation.27 | async-start | bytes 11796480 | tf_op jit(solution)/shard_map/reduce_scatter | solution.py:329
  1031.9 712.3 %reduce-scatter.32.cloned.1.call-start = ((), (), s32[]{:S(2)}) async-start(), calls=%async_computation.28 | async-start | bytes 11796480 | tf_op jit(solution)/shard_map/reduce_scatter | solution.py:332
  1042.1 794.1 %all-reduce.5.cloned.1.call-start = ((), (), s32[]{:S(2)}) async-start(), calls=%async_computation.34 | async-start | bytes 9437184 | tf_op jit(solution)/shard_map/psum | solution.py:422
  (105 other events, 3005.5 us)
Sparse Core Ops, SparseCore 0:
  9.6 130.8 all-gather.11
  144.3 30.4 all-gather.13
  176.4 50.4 all-gather.15
  228.3 88.2 all-gather.17
  318.0 87.8 all-gather.19
  413.6 30.7 all-gather.21
  446.0 166.7 all-gather.23
  614.3 164.9 all-gather.25
  855.0 42.5 reduce-scatter.33
  954.6 46.2 reduce-scatter.35
  1003.8 48.0 reduce-scatter.23
  1054.6 85.6 reduce-scatter.25
  1143.1 85.5 reduce-scatter.27
  1230.9 124.0 reduce-scatter.21
  1357.1 19.8 reduce-scatter.41
  1379.8 17.5 reduce-scatter.39
  1400.0 17.5 reduce-scatter.37
  1420.0 159.4 reduce-scatter.29
  1582.0 162.1 reduce-scatter.31
  1748.0 88.2 all-reduce.4
where the time goes:
time: 1860 us; the launch traced here: 1850 us
  waiting for transfers between devices  1380 us (74%)
  matrix products  181 us (10%)
  blocking collectives  131 us (7%)
  local copies, waits for them, and re-layouts  88.7 us (5%)
  other arithmetic  40.7 us (2%)
    reduce_scatter x1, waiting for transfers between devices, shards(): lax.psum_scatter(down_grad_experts.astype(jnp.bfloat16), 'shard', scatter...  160 us
    all_gather x1, waiting for transfers between devices, shards(): lax.all_gather(expert_down, 'shard', axis=1, tiled=True)  158 us
    reduce_scatter x1, waiting for transfers between devices, shards(): lax.psum_scatter(up_grad_experts.astype(jnp.bfloat16), 'shard', scatter_d...  136 us
    reduce_scatter x1, waiting for transfers between devices, shards(): lax.psum_scatter(shared[1].astype(jnp.bfloat16), 'shard', scatter_dimensi...  126 us
    all_gather x1, waiting for transfers between devices, shards(): lax.all_gather(expert_up, 'shard', axis=1, tiled=True)  126 us
    all_gather x1, waiting for transfers between devices, shards(): lax.all_gather(qkv_weight, 'shard', axis=1, tiled=True)  118 us
    unnamed x25, waiting for transfers between devices  92.7 us
    reduce_scatter x1, waiting for transfers between devices, shards(): lax.psum_scatter(shared[6].astype(jnp.bfloat16), 'shard', scatter_dimensi...  88.5 us
  transfers between devices with their start and end apart: 24, of which 20 were waited for; matrix products, arithmetic and copies ran while one was open for 11% of the time, Pallas kernels for 0%

commit v1 on v0

v1 whole, which is shorter than its diff:
```python
import math

import jax
import jax.numpy as jnp
from jax import lax
from jax.sharding import PartitionSpec as P

D = 768
H = 12
HD = 64
NB = 32
EXP_DEV = 2

epsilon = 1e-06
clip_limit = 6.0
bfloat = jnp.bfloat16
single = jnp.float32


def rms_norm(inputs, norm_gain):
    return (
        inputs * lax.rsqrt(jnp.mean(inputs * inputs, axis=-1, keepdims=True) + epsilon) * norm_gain
    )


def norm_back(inputs, norm_gain, upstream):
    _, pullback = jax.vjp(rms_norm, inputs, norm_gain)
    return pullback(upstream)


def gelu_back(pre_values, upstream):
    _, pullback = jax.vjp(jax.nn.gelu, pre_values)
    return pullback(upstream)[0]


def matmul(left, right):
    return jnp.dot(left, right, preferred_element_type=single)


def shard_shift(block, amount):
    count = lax.axis_size("shard")
    return lax.ppermute(block, "shard", [(i, (i + amount) % count) for i in range(count)])


def gather_shard(block):
    count = lax.axis_size("shard")
    here = lax.axis_index("shard")
    result = jnp.zeros((count,) + block.shape, block.dtype)
    for step in range(count):
        piece = block if step == 0 else shard_shift(block, step)
        result = lax.dynamic_update_slice_in_dim(result, piece[None], (here - step) % count, 0)
    return result


def scatter_shard(blocks, sent=bfloat):
    count = lax.axis_size("shard")
    here = lax.axis_index("shard")
    total = lax.dynamic_index_in_dim(blocks, here, 0, keepdims=False).astype(single)
    for step in range(1, count):
        part = lax.dynamic_index_in_dim(blocks, (here + step) % count, 0, keepdims=False)
        total = total + shard_shift(part.astype(sent), step).astype(single)
    return total


def spread(columns):
    experts, shard_count = lax.axis_size("expert"), lax.axis_size("shard")
    rows, width = columns.shape
    cut = columns.reshape(rows, shard_count, experts, width // (shard_count * experts))
    return cut.transpose(0, 2, 1, 3).reshape(rows, width)


def unspread(columns):
    experts, shard_count = lax.axis_size("expert"), lax.axis_size("shard")
    rows, width = columns.shape
    cut = columns.reshape(rows, experts, shard_count, width // (shard_count * experts))
    return cut.transpose(0, 2, 1, 3).reshape(rows, width)


def gather_weight(block):
    part = block.shape[0] // lax.axis_size("expert")
    own = lax.dynamic_slice_in_dim(block, lax.axis_index("expert") * part, part, 0)
    column = gather_shard(own).reshape(-1, block.shape[1])
    return lax.all_gather(column, "expert", axis=0, tiled=True)


def reduce_weight(grad):
    part = lax.psum_scatter(grad.astype(bfloat), "expert", scatter_dimension=0, tiled=True)
    blocks = part.reshape((lax.axis_size("shard"), -1) + part.shape[1:])
    own = scatter_shard(blocks).astype(bfloat)
    return lax.all_gather(own, "expert", axis=0, tiled=True).astype(single)


def bucket_marks(distance, lower, upper):
    inside = (distance[None] >= lower[:, None, None]) & (distance[None] < upper[:, None, None])
    return inside.astype(bfloat)


def position_bias(marks, bias_pair):
    return jnp.einsum("bij,bh->hij", marks, bias_pair, preferred_element_type=single)


def attention_forward(hidden, norm_gain, qkv, projection, bias_pair, geometry):
    distance, marks, scale = geometry
    rows = hidden.shape[0]
    normalized = spread(rms_norm(hidden, norm_gain).astype(bfloat))
    packed = matmul(normalized, qkv).astype(bfloat)
    key_value = lax.all_gather(packed[:, D:], "expert", axis=0, tiled=True)
    shifted = position_bias(marks, bias_pair)
    causal = distance >= 0
    queries = packed[:, :D].reshape(rows, H, HD)
    keys = key_value[:, :D].reshape(-1, H, HD)
    values = key_value[:, D:].reshape(-1, H, HD)
    raw_scores = jnp.einsum("ihd,jhd->hij", queries, keys, preferred_element_type=single) * scale
    head_peak = jnp.max(jnp.where(causal[None], raw_scores, -jnp.inf), axis=(1, 2))
    masked = jnp.where(causal[None], raw_scores + shifted, -jnp.inf)
    softmax_top = jnp.max(masked, axis=-1, keepdims=True)
    exponent = jnp.exp(masked - softmax_top)
    softmax_sum = jnp.sum(exponent, axis=-1, keepdims=True)
    probs = (exponent / softmax_sum).astype(bfloat)
    log_total = softmax_top[..., 0] + jnp.log(softmax_sum[..., 0])
    attended = jnp.einsum("hij,jhd->ihd", probs, values, preferred_element_type=single)
    attended = spread(attended.astype(bfloat).reshape(rows, D))
    saved = (normalized, packed, key_value, log_total, attended)
    return hidden + matmul(attended, projection), head_peak, saved


def attention_backward(
    upstream, hidden, norm_gain, qkv, projection, bias_pair, geometry, saved
):
    distance, marks, scale = geometry
    normalized, packed, key_value, log_total, attended = saved
    rows = hidden.shape[0]
    branch_grad = upstream.astype(bfloat)
    projection_grad = matmul(attended.T, branch_grad)
    attended_grad = unspread(matmul(branch_grad, projection.T).astype(bfloat))
    shifted = position_bias(marks, bias_pair)
    causal = distance >= 0
    queries = packed[:, :D].reshape(rows, H, HD)
    keys = key_value[:, :D].reshape(-1, H, HD)
    values = key_value[:, D:].reshape(-1, H, HD)
    grad_heads = attended_grad.reshape(rows, H, HD)
    raw_scores = jnp.einsum("ihd,jhd->hij", queries, keys, preferred_element_type=single) * scale
    probs = jnp.where(causal[None], jnp.exp(raw_scores + shifted - log_total[..., None]), 0.0)
    prob_grad = jnp.einsum("ihd,jhd->hij", grad_heads, values, preferred_element_type=single)
    row_dot = jnp.sum(prob_grad * probs, axis=-1)
    score_grad = (probs * (prob_grad - row_dot[..., None])).astype(bfloat)
    query_grad = jnp.einsum("hij,jhd->ihd", score_grad, keys, preferred_element_type=single) * scale
    query_grad = query_grad.astype(bfloat).reshape(rows, D)
    bias_grad = jnp.einsum("hij,bij->bh", score_grad, marks, preferred_element_type=single)
    key_grad = (
        jnp.einsum("hij,ihd->jhd", score_grad, queries, preferred_element_type=single) * scale
    )
    value_grad = jnp.einsum(
        "hij,ihd->jhd", probs.astype(bfloat), grad_heads, preferred_element_type=single
    )
    pair = jnp.concatenate([key_grad.reshape(-1, D), value_grad.reshape(-1, D)], axis=-1)
    pair_grad = lax.psum_scatter(pair.astype(bfloat), "expert", scatter_dimension=0, tiled=True)
    packed_grad = jnp.concatenate([query_grad, pair_grad], axis=-1)
    qkv_grad = matmul(normalized.T, packed_grad)
    normed_grad = unspread(matmul(packed_grad, qkv.T))
    input_grad, gain_grad = norm_back(hidden, norm_gain, normed_grad)
    return upstream + input_grad, gain_grad, qkv_grad, projection_grad, bias_grad


def exchange(blocks):
    return lax.all_to_all(blocks, "expert", split_axis=0, concat_axis=0, tiled=True)


def shards(
    hidden_in,
    attn_gain,
    qkv_weight,
    out_weight,
    rel_bias,
    bucket_table,
    mlp_gain,
    mlp_up,
    mlp_down,
    router_weight,
    expert_up,
    expert_down,
    routes,
    out_grad,
):
    block_rows = hidden_in.shape[1]
    length = bucket_table.shape[0]
    experts = lax.axis_size("expert")
    groups = lax.axis_size("shard")
    here = lax.axis_index("shard")
    expert_total = EXP_DEV * experts
    capacity = 4 * block_rows // expert_total
    width = expert_down.shape[1]
    scale = 1.0 / math.sqrt(HD)

    small = jnp.concatenate(
        [attn_gain.reshape(-1), mlp_gain.reshape(-1), rel_bias.reshape(-1), router_weight.reshape(-1)]
    )
    small = gather_shard(small)
    part = D // groups
    cuts = [0, 2 * part, 4 * part, 4 * part + 2 * (NB // groups) * H, small.shape[1]]
    gain_attn, gain_mlp, bias_weights, router_full = (
        small[:, cuts[i] : cuts[i + 1]] for i in range(4)
    )
    gain_attn = gain_attn.reshape(groups, 2, part).transpose(1, 0, 2).reshape(2, D).astype(single)
    gain_mlp = gain_mlp.reshape(groups, 2, part).transpose(1, 0, 2).reshape(2, D).astype(single)
    bias_weights = (
        bias_weights.reshape(groups, 2, NB // groups, H).transpose(1, 0, 2, 3).reshape(2, NB, H)
    )
    router_full = router_full.reshape(D, expert_total)

    first = gather_weight(jnp.concatenate([qkv_weight[0], out_weight[0]], axis=1))
    dense_up = gather_weight(mlp_up)
    dense_down = gather_weight(mlp_down)
    second = gather_weight(jnp.concatenate([qkv_weight[1], out_weight[1]], axis=1))
    qkv = (first[:, : 3 * D], second[:, : 3 * D])
    projection = (first[:, 3 * D :], second[:, 3 * D :])

    up_own = jnp.zeros((EXP_DEV, groups, part, width), bfloat)
    for step in range(groups):
        target = (here + step) % groups
        piece = lax.dynamic_slice_in_dim(expert_up, target * width, width, 2)
        if step:
            piece = shard_shift(piece, step)
        up_own = lax.dynamic_update_slice_in_dim(up_own, piece[:, None], (here - step) % groups, 1)
    up_own = up_own.reshape(EXP_DEV, D, width)

    route_rows = gather_shard(routes.reshape(block_rows, 2))
    upstream_all = gather_shard(out_grad.reshape(block_rows, D))
    expert_ids = jnp.arange(expert_total, dtype=jnp.int32)
    flat_routes = route_rows.reshape(groups, -1)
    marks = (flat_routes[:, :, None] == expert_ids).astype(jnp.int32)
    rank = jnp.sum((jnp.cumsum(marks, axis=1) - marks) * marks, axis=2)
    slot_of_route = flat_routes * capacity + rank
    slot_ids = jnp.arange(expert_total * capacity, dtype=jnp.int32)
    slot_marks = (slot_of_route[:, :, None] == slot_ids).astype(bfloat)
    token_marks = jnp.sum(
        slot_marks.reshape(groups, block_rows, 2, -1).astype(single), axis=2
    ).astype(bfloat)

    def dispatch(rows):
        slots = jnp.einsum("gts,gtd->gsd", token_marks, rows, preferred_element_type=single)
        slots = slots.astype(bfloat).reshape(groups, experts, EXP_DEV, capacity, D)
        return exchange(slots.transpose(1, 2, 0, 3, 4)).reshape(
            experts, EXP_DEV, groups * capacity, D
        )

    def collect(blocks):
        back = exchange(blocks.astype(bfloat)).reshape(experts, EXP_DEV, groups, capacity, D)
        return back.transpose(2, 0, 1, 3, 4).reshape(groups, expert_total * capacity, D)

    owner_rows = dispatch(upstream_all)

    own_positions = lax.axis_index("expert") * block_rows + jnp.arange(block_rows, dtype=jnp.int32)
    distance = own_positions[:, None] - jnp.arange(length, dtype=jnp.int32)[None, :]
    bounds = jnp.sum(
        (bucket_table[:, None] < jnp.arange(NB + 1, dtype=jnp.int32)[None, :]).astype(jnp.int32),
        axis=0,
    )
    geometry = (distance, bucket_marks(distance, bounds[:NB], bounds[1:]), scale)

    hidden_zero = hidden_in.reshape(block_rows, D).astype(single)
    mid_first, peak_first, saved_first = attention_forward(
        hidden_zero, gain_attn[0], qkv[0], projection[0], bias_weights[0], geometry
    )
    dense_normed = spread(rms_norm(mid_first, gain_mlp[0]).astype(bfloat))
    pre_act = matmul(dense_normed, dense_up)
    activation = spread(jax.nn.gelu(pre_act).astype(bfloat))
    layer_one = mid_first + matmul(activation, dense_down)
    mid_second, peak_second, saved_second = attention_forward(
        layer_one, gain_attn[1], qkv[1], projection[1], bias_weights[1], geometry
    )

    moe_normed = rms_norm(mid_second, gain_mlp[1]).astype(bfloat)
    normed_all = gather_shard(moe_normed)
    received = dispatch(normed_all)
    router_logits = jnp.einsum("gtd,de->gte", normed_all, router_full, preferred_element_type=single)
    selected = (route_rows[..., None] == expert_ids).astype(single)
    gates_all = jax.nn.softmax(jnp.sum(selected * router_logits[:, :, None, :], axis=-1), axis=-1)
    slot_gates = jnp.sum(
        gates_all.reshape(groups, -1)[:, :, None] * (slot_of_route[:, :, None] == slot_ids), axis=1
    )
    owner_gates = exchange(
        slot_gates.reshape(groups, experts, EXP_DEV, capacity).transpose(1, 2, 0, 3)
    ).reshape(experts, EXP_DEV, groups * capacity)

    expert_pre = jnp.einsum("sjcd,jdf->sjcf", received, up_own, preferred_element_type=single)
    expert_act = jax.nn.gelu(expert_pre).astype(bfloat)
    expert_out = jnp.einsum(
        "sjcf,jfd->sjcd", expert_act, expert_down, preferred_element_type=single
    )
    owner_grad = (owner_gates[..., None] * owner_rows.astype(single)).astype(bfloat)
    act_grad = jnp.einsum("sjcd,jfd->sjcf", owner_grad, expert_down, preferred_element_type=single)
    pre_grad = gelu_back(expert_pre, act_grad).astype(bfloat)
    row_grad = jnp.einsum("sjcf,jdf->sjcd", pre_grad, up_own, preferred_element_type=single)

    returned = collect(expert_out)
    back_rows = collect(row_grad)
    expert_down_grad = jnp.einsum(
        "sjcf,sjcd->jfd", expert_act, owner_grad, preferred_element_type=single
    )
    up_grad = jnp.einsum(
        "sjcd,sjcf->jdf", received, pre_grad, preferred_element_type=single
    ).astype(bfloat)

    route_out = jnp.einsum("grs,gsd->grd", slot_marks, returned, preferred_element_type=single)
    route_out = route_out.reshape(groups, block_rows, 2, D)
    gate_grad = scatter_shard(
        jnp.sum(route_out * upstream_all[:, :, None, :].astype(single), axis=-1), single
    )
    mixed = scatter_shard(jnp.sum(gates_all[..., None] * route_out, axis=2))
    hidden_out = (mid_second + mixed).astype(bfloat).reshape(hidden_in.shape)

    gates = lax.dynamic_index_in_dim(gates_all, here, 0, keepdims=False)
    own_selected = lax.dynamic_index_in_dim(selected, here, 0, keepdims=False)
    upstream = out_grad.reshape(block_rows, D).astype(single)
    chosen_grad = gates * (gate_grad - jnp.sum(gates * gate_grad, axis=-1, keepdims=True))
    logit_grad = jnp.sum(chosen_grad[:, :, None] * own_selected, axis=1).astype(bfloat)
    router_grad = matmul(moe_normed.T, logit_grad)
    row_terms = jnp.einsum("gts,gsd->gtd", token_marks, back_rows, preferred_element_type=single)
    normed_grad = matmul(logit_grad, router_full.T) + scatter_shard(row_terms)
    moe_input_grad, moe_gain_grad = norm_back(mid_second, gain_mlp[1], normed_grad)
    mid_grad = upstream + moe_input_grad

    up_grad = up_grad.reshape(EXP_DEV, groups, part, width)
    expert_up_grad = jnp.zeros((EXP_DEV, part, groups * width), single)
    for step in range(groups):
        piece = lax.dynamic_index_in_dim(up_grad, (here + step) % groups, 1, keepdims=False)
        if step:
            piece = shard_shift(piece, step)
        expert_up_grad = lax.dynamic_update_slice_in_dim(
            expert_up_grad, piece.astype(single), ((here - step) % groups) * width, 2
        )

    layer_grad, gain_second, qkv_second, projection_second, bias_second = attention_backward(
        mid_grad, layer_one, gain_attn[1], qkv[1], projection[1], bias_weights[1], geometry,
        saved_second,
    )
    second_grad = reduce_weight(jnp.concatenate([qkv_second, projection_second], axis=1))
    dense_branch = layer_grad.astype(bfloat)
    mlp_down_grad = reduce_weight(matmul(activation.T, dense_branch))
    hidden_act_grad = unspread(matmul(dense_branch, dense_down.T))
    pre_act_grad = gelu_back(pre_act, hidden_act_grad).astype(bfloat)
    mlp_up_grad = reduce_weight(matmul(dense_normed.T, pre_act_grad))
    dense_normed_grad = unspread(matmul(pre_act_grad, dense_up.T))
    dense_input_grad, dense_gain_grad = norm_back(mid_first, gain_mlp[0], dense_normed_grad)
    first_grad = layer_grad + dense_input_grad
    input_grad, gain_first, qkv_first, projection_first, bias_first = attention_backward(
        first_grad, hidden_zero, gain_attn[0], qkv[0], projection[0], bias_weights[0], geometry,
        saved_first,
    )
    first_weight_grad = reduce_weight(jnp.concatenate([qkv_first, projection_first], axis=1))

    gains = jnp.stack([gain_first, gain_second, dense_gain_grad, moe_gain_grad])
    biases = jnp.stack([bias_first, bias_second])
    small_grad = jnp.concatenate(
        [
            gains.reshape(4, groups, part).transpose(1, 0, 2).reshape(groups, -1),
            biases.reshape(2, groups, NB // groups, H).transpose(1, 0, 2, 3).reshape(groups, -1),
            router_grad.reshape(groups, -1),
        ],
        axis=1,
    )
    small_grad = lax.psum(scatter_shard(small_grad, single), "expert")
    gain_cut = 4 * part
    bias_cut = gain_cut + 2 * (NB // groups) * H
    own_gains = small_grad[:gain_cut].reshape(4, part)
    peaks = lax.pmax(jnp.stack([peak_first, peak_second]), ("expert", "shard"))
    clip_scales = jnp.sqrt(clip_limit / jnp.maximum(peaks, clip_limit))
    return (
        hidden_out,
        input_grad.reshape(hidden_in.shape),
        own_gains[:2],
        jnp.stack([first_weight_grad[:, : 3 * D], second_grad[:, : 3 * D]]),
        jnp.stack([first_weight_grad[:, 3 * D :], second_grad[:, 3 * D :]]),
        small_grad[gain_cut:bias_cut].reshape(2, NB // groups, H),
        own_gains[2:],
        mlp_up_grad,
        mlp_down_grad,
        small_grad[bias_cut:].reshape(part, expert_total),
        expert_up_grad,
        expert_down_grad,
        clip_scales,
    )


def solution(mesh):
    tokens = P("shard", "expert", None, None)
    columns = P(None, "shard")
    layers = P(None, "shard", None)
    rows = P("shard", None)
    owned = P("expert", "shard", None)
    in_specs = (
        tokens, columns, layers, layers, layers, P(), columns, rows, rows, rows, owned, owned,
        tokens, tokens,
    )
    out_specs = (
        tokens, tokens, columns, layers, layers, layers, columns, rows, rows, rows, owned, owned,
        P(),
    )
    return jax.shard_map(shards, mesh=mesh, in_specs=in_specs, out_specs=out_specs, check_vma=False)
```

time: 1860 us -> 1140 us (0.61)
  waiting for transfers between devices: 1380 us -> 447 us
  starting transfers between devices: 17.6 us -> 152 us
  local copies, waits for them, and re-layouts: 88.7 us -> 190 us
  blocking collectives: 131 us -> 61.9 us
  other arithmetic: 40.7 us -> 86 us
    reduce_scatter x6 -> x4, waiting for transfers between devices: 561 us -> 59.3 us  [reduce_weight(): lax.psum_scatter(grad.astype(bfloat), 'expert', scatter_dimension=0, tile...]
    all_gather x8 -> x10, waiting for transfers between devices: 613 us -> 141 us  [the longest x4 90.6 us: gather_weight(): return lax.all_gather(column, 'expert', axis=0, tiled=True)]
    ppermute x0 -> x54, waiting for transfers between devices: none -> 144 us  [shard_shift(): lax.ppermute(block, 'shard', [(i, (i + amount) % count) for i in range(co...]
    ppermute x0 -> x54, starting transfers between devices: none -> 128 us  [shard_shift(): lax.ppermute(block, 'shard', [(i, (i + amount) % count) for i in range(co...]
    psum x1 -> x0, waiting for transfers between devices: 87.9 us -> none  [shards(): lax.psum(shared[1].astype(jnp.bfloat16), 'expert').astype(jnp.float32)]
    dynamic_update_slice x0 -> x35, local copies, waits for them, and re-layouts: none -> 58 us  [the longest x30 49.6 us: gather_shard(): lax.dynamic_update_slice_in_dim(result, piece[None], (here - step) % coun...]
    all_gather x4 -> x0, blocking collectives: 47 us -> none  [the longest x1 13.1 us: shards(): lax.all_gather(rel_bias, 'shard', axis=1, tiled=True)]
    unnamed x235 -> x228, local copies, waits for them, and re-layouts: 68.1 us -> 34 us
  transfers between devices with their start and end apart: 24 -> 75, of which waited for: 20 -> 37; matrix products, arithmetic and copies ran while one was open for 11% -> 29% of each run, Pallas kernels for 0% -> 0%
where the time goes in v1:
time: 1140 us; the launch traced here: 1130 us
  waiting for transfers between devices  447 us (39%)
  local copies, waits for them, and re-layouts  190 us (17%)
  matrix products  175 us (15%)
  starting transfers between devices  152 us (13%)
  other arithmetic  86 us (8%)
  blocking collectives  61.9 us (5%)
  between operations  16.7 us (1%)
    ppermute x54, waiting for transfers between devices, shard_shift(): lax.ppermute(block, 'shard', [(i, (i + amount) % count) for i in range(co...  144 us
    ppermute x54, starting transfers between devices, shard_shift(): lax.ppermute(block, 'shard', [(i, (i + amount) % count) for i in range(co...  128 us
    all_gather x4, waiting for transfers between devices, gather_weight(): return lax.all_gather(column, 'expert', axis=0, tiled=True)  90.6 us
    unnamed x18, waiting for transfers between devices  68.9 us
    reduce_scatter x4, waiting for transfers between devices, reduce_weight(): lax.psum_scatter(grad.astype(bfloat), 'expert', scatter_dimension=0, tile...  59.3 us
    all_gather x4, waiting for transfers between devices, reduce_weight(): return lax.all_gather(own, 'expert', axis=0, tiled=True).astype(single)  50 us
    dynamic_update_slice x30, local copies, waits for them, and re-layouts, gather_shard(): lax.dynamic_update_slice_in_dim(result, piece[None], (here - step) % coun...  49.6 us
    dot_general x20, matrix products, matmul(): return jnp.dot(left, right, preferred_element_type=single)  47.8 us
  transfers between devices with their start and end apart: 75, of which 37 were waited for; matrix products, arithmetic and copies ran while one was open for 29% of the time, Pallas kernels for 0%

profile of v1, /device:TPU:0, one launch (start us, length us, event | category | flops | bytes accessed | tf_op | source)
XLA Modules:
  0.0 1129.1 jit_solution(15714809447100085138)
XLA Ops:
  41.5 31.2 %all-gather.11.cloned.1.call-done = bf16[768,3072]{1,0:T(8,128)(2,1)} async-done(((bf16[96,3072]{1,0:T(8,128)(2,1)}), bf16[768,3072]{1,0:T(8,128)(2,1)}) %all-gather.11.cloned.1.call-update) | async-done | bytes 4718608 | tf_op jit(solution)/shard_map/all_gather | solution.py:83
  143.8 11.2 select_reduce_fusion.3
  169.7 22.5 %all-gather.17.cloned.1.call-done = bf16[3072,768]{1,0:T(8,128)(2,1)} async-done(((bf16[384,768]{1,0:T(8,128)(2,1)}), bf16[3072,768]{1,0:T(8,128)(2,1)}) %all-gather.17.cloned.1.call-update) | async-done | bytes 4718608 | tf_op jit(solution)/shard_map/all_gather | solution.py:83
  196.6 36.8 %all-gather.19.cloned.1.call-done = bf16[768,3072]{1,0:T(8,128)(2,1)} async-done(((bf16[96,3072]{1,0:T(8,128)(2,1)}), bf16[768,3072]{1,0:T(8,128)(2,1)}) %all-gather.19.cloned.1.call-update) | async-done | bytes 4718608 | tf_op jit(solution)/shard_map/all_gather | solution.py:83
  249.3 11.4 %collective-permute-start.29 = (bf16[128,768]{1,0:T(8,128)(2,1)}, bf16[128,768]{1,0:T(8,128)(2,1)}, u32[]{:S(2)}, u32[]{:S(2)}) collective-permute-start(bf16[128,768]{1,0:T(8,128)(2,1)} %bitcast.97), channel_id=1, source_target_pairs={{0,3},{1,0},{2,1},{3,2},{4,7},{5,4},{6,5},{7,6},{8,11},{9,8},{10,9... | collective-permute-start | bytes 589832 | tf_op jit(solution)/shard_map/ppermute | solution.py:42
  261.2 10.8 dynamic_update_slice.141
  272.0 10.8 dynamic_update_slice.142
  282.8 10.8 dynamic_update_slice.143
  327.1 11.8 %select_reduce_fusion.1 = (f32[12]{0:T(128)}, f32[12,128]{1,0:T(8,128)S(1)}, f32[12]{0:T(128)}, f32[12,128,1024]{2,1,0:T(8,128)S(1)}) fusion(f32[12,128,1024]{2,1,0:T(8,128)} %get-tuple-element.193, pred[128,1024]{1,0:T(8,128)(4,1)S(1)} %broadcast_compare_fusion, f32[12,128,1024]{2,0,1:T(8,128)} %fusion.133, bf16[128,12,64]{0,2,1:T(8,128)(2,1)S(1)} %bitcast.535, ...), kind=kOutput, calls=%fused_computation.23 | convolution fusion | flops 215480800 | bytes 20781152 | tf_op jit(solution)/shard_map/ihd,jhd->hij/dot_general | solution.py:113
  407.3 23.1 %collective-permute-done.22 = bf16[2,192,768]{2,1,0:T(8,128)(2,1)} collective-permute-done((bf16[2,192,768]{2,1,0:T(8,128)(2,1)}, bf16[2,192,768]{2,1,0:T(8,128)(2,1)}, u32[]{:S(2)}, u32[]{:S(2)}) %collective-permute-start.22) | collective-permute-done | bytes 589856 | tf_op jit(solution)/shard_map/ppermute | solution.py:42
  478.7 29.3 %all-to-all-done.4 = bf16[8,2,128,768]{2,3,1,0:T(8,128)(2,1)} async-done(((bf16[8,2,128,768]{2,3,1,0:T(8,128)(2,1)}), bf16[8,2,128,768]{2,3,1,0:T(8,128)(2,1)}, u32[]{:S(2)}, u32[]{:S(2)}) %all-to-all-start.4) | async-done | bytes 3145760 | tf_op jit(solution)/shard_map/all_to_all | solution.py:166
  531.1 14.9 %collective-permute-start.35 = (bf16[128,768]{1,0:T(8,128)(2,1)}, bf16[128,768]{1,0:T(8,128)(2,1)}, u32[]{:S(2)}, u32[]{:S(2)}) collective-permute-start(bf16[128,768]{1,0:T(8,128)(2,1)} %get-tuple-element.158), channel_id=1, source_target_pairs={{0,3},{1,0},{2,1},{3,2},{4,7},{5,4},{6,5},{7,6},{8,11},{9,8},{10,9... | collective-permute-start | bytes 589832 | tf_op jit(solution)/shard_map/ppermute | solution.py:42
  564.4 14.9 %collective-permute-start.32 = (f32[128,2]{0,1:T(2,128)S(1)}, f32[128,2]{0,1:T(2,128)S(1)}, u32[]{:S(2)}, u32[]{:S(2)}) collective-permute-start(f32[128,2]{0,1:T(2,128)S(1)} %bitcast.595), channel_id=1, source_target_pairs={{0,3},{1,0},{2,1},{3,2},{4,7},{5,4},{6,5},{7,6},{8,11},{9,8},{10,9... | collective-permute-start | bytes 3080 | tf_op jit(solution)/shard_map/ppermute | solution.py:42
  580.8 17.4 %multiply_reduce_fusion.3 = f32[4,128,768]{2,1,0:T(8,128)S(1)} fusion(f32[4,128,2,768]{3,2,1,0:T(2,128)} %reshape.587, f32[4,128,2]{2,1,0:T(8,128)S(1)} %copy-done.51), kind=kLoop, calls=%fused_computation.68 | loop fusion | flops 1179648 | bytes 4722688 | tf_op jit(solution)/shard_map/reduce_sum | solution.py:310
  649.3 41.4 %reduce-scatter.19.cloned.1.call-done = bf16[128,1536]{1,0:T(8,128)(2,1)} async-done(((bf16[1024,1536]{1,0:T(8,128)(2,1)}), bf16[128,1536]{1,0:T(8,128)(2,1)}) %reduce-scatter.19.cloned.1.call-update) | async-done | bytes 393232
  752.6 27.3 %reduce-scatter.21.cloned.1.call-done = bf16[128,1536]{1,0:T(8,128)(2,1)} async-done(((bf16[1024,1536]{1,0:T(8,128)(2,1)}), bf16[128,1536]{1,0:T(8,128)(2,1)}) %reduce-scatter.21.cloned.1.call-update) | async-done | bytes 393232
  785.8 39.5 %pmax.7 = f32[2,12]{1,0:T(2,128)S(1)} all-reduce(f32[2,12]{1,0:T(2,128)S(1)} %pad_maximum_fusion.12), channel_id=1, replica_groups=mesh['expert'=8,'shard'=4] {'expert','shard'}, use_global_device_ids=true, to_apply=%region_40.41 | all-reduce | flops 24 | bytes 192 | tf_op jit(solution)/shard_map/pmax | solution.py:367
  848.5 32.5 %collective-permute-done.43 = bf16[24,3072]{1,0:T(8,128)(2,1)S(1)} collective-permute-done((bf16[24,3072]{1,0:T(8,128)(2,1)S(1)}, bf16[24,3072]{1,0:T(8,128)(2,1)S(1)}, u32[]{:S(2)}, u32[]{:S(2)}) %collective-permute-start.43) | collective-permute-done | bytes 147488 | tf_op jit(solution)/shard_map/ppermute | solution.py:42
  899.7 11.9 %collective-permute-start.47 = (bf16[24,3072]{1,0:T(8,128)(2,1)S(1)}, bf16[24,3072]{1,0:T(8,128)(2,1)S(1)}, u32[]{:S(2)}, u32[]{:S(2)}) collective-permute-start(bf16[24,3072]{1,0:T(8,128)(2,1)S(1)} %get-tuple-element.167), channel_id=1, source_target_pairs={{0,3},{1,0},{2,1},{3,2},{4,7},{5,4},{6,5},{7,6},{8,11},{9,8},{10,9... | collective-permute-start | bytes 442376 | tf_op jit(solution)/shard_map/ppermute | solution.py:42
  933.6 19.4 %reduce-scatter.17.cloned.1.call-done = bf16[384,768]{1,0:T(8,128)(2,1)} async-done(((bf16[3072,768]{1,0:T(8,128)(2,1)}), bf16[384,768]{1,0:T(8,128)(2,1)}) %reduce-scatter.17.cloned.1.call-update) | async-done | bytes 589840 | tf_op jit(solution)/shard_map/reduce_scatter | solution.py:87
  975.6 35.1 %reduce-scatter.11.cloned.1.call-done = bf16[96,3072]{1,0:T(8,128)(2,1)} async-done(((bf16[768,3072]{1,0:T(8,128)(2,1)}), bf16[96,3072]{1,0:T(8,128)(2,1)}) %reduce-scatter.11.cloned.1.call-update) | async-done | bytes 589840 | tf_op jit(solution)/shard_map/reduce_scatter | solution.py:87
  1032.0 22.4 %psum.7 = f32[4032]{0:T(1024)S(1)} all-reduce(f32[4032]{0:T(1024)S(1)} %add_add_fusion.4), channel_id=1, replica_groups=mesh['expert'=8,'shard'=4] {'expert'}, use_global_device_ids=true, to_apply=%region_33.34 | all-reduce | flops 4032 | bytes 32256 | tf_op jit(solution)/shard_map/psum | solution.py:363
  1066.7 23.4 %all-gather.29.cloned.1.call-done = bf16[768,768]{1,0:T(8,128)(2,1)} async-done(((bf16[96,768]{1,0:T(8,128)(2,1)}), bf16[768,768]{1,0:T(8,128)(2,1)}) %all-gather.29.cloned.1.call-update) | async-done | bytes 1179664 | tf_op jit(solution)/shard_map/all_gather | solution.py:90
  1094.4 21.6 %all-gather.23.cloned.1.call-done = bf16[192,3072]{1,0:T(8,128)(2,1)} async-done(((bf16[24,3072]{1,0:T(8,128)(2,1)}), bf16[192,3072]{1,0:T(8,128)(2,1)}) %all-gather.23.cloned.1.call-update) | async-done | bytes 1179664 | tf_op jit(solution)/shard_map/all_gather | solution.py:90
  (670 shorter events, 581.0 us)
Async XLA Ops:
  7.2 65.6 %all-gather.11.cloned.1.call-start = ((), (), s32[]{:S(2)}) async-start(), calls=%async_computation.11 | async-start | bytes 5308416 | tf_op jit(solution)/shard_map/all_gather | solution.py:83
  31.3 102.4 %all-gather.13.cloned.1.call-start = ((), (), s32[]{:S(2)}) async-start(), calls=%async_computation.12 | async-start | bytes 3538944 | tf_op jit(solution)/shard_map/all_gather | solution.py:107
  77.1 85.6 %all-gather.15.cloned.1.call-start = ((), (), s32[]{:S(2)}) async-start(), calls=%async_computation.13 | async-start | bytes 5308416 | tf_op jit(solution)/shard_map/all_gather | solution.py:83
  93.3 98.9 %all-gather.17.cloned.1.call-start = ((), (), s32[]{:S(2)}) async-start(), calls=%async_computation.14 | async-start | bytes 5308416 | tf_op jit(solution)/shard_map/all_gather | solution.py:83
  109.7 123.7 %all-gather.19.cloned.1.call-start = ((), (), s32[]{:S(2)}) async-start(), calls=%async_computation.15 | async-start | bytes 5308416 | tf_op jit(solution)/shard_map/all_gather | solution.py:83
  126.7 191.5 %all-gather.21.cloned.1.call-start = ((), (), s32[]{:S(2)}) async-start(), calls=%async_computation.16 | async-start | bytes 3538944 | tf_op jit(solution)/shard_map/all_gather | solution.py:107
  243.1 60.9 %collective-permute-start.27 = (bf16[128,768]{1,0:T(8,128)(2,1)}, bf16[128,768]{1,0:T(8,128)(2,1)}, u32[]{:S(2)}, u32[]{:S(2)}) collective-permute-start(bf16[128,768]{1,0:T(8,128)(2,1)} %bitcast.97), channel_id=1, source_target_pairs={{0,1},{1,2},{2,3},{3,0},{4,5},{5,6},{6,7},{7,4},{8,9},{9,10},{10,1... | collective-permute-start | bytes 589832 | tf_op jit(solution)/shard_map/ppermute | solution.py:42
  243.7 62.0 %collective-permute-start.28 = (bf16[128,768]{1,0:T(8,128)(2,1)}, bf16[128,768]{1,0:T(8,128)(2,1)}, u32[]{:S(2)}, u32[]{:S(2)}) collective-permute-start(bf16[128,768]{1,0:T(8,128)(2,1)} %bitcast.97), channel_id=1, source_target_pairs={{0,2},{1,3},{2,0},{3,1},{4,6},{5,7},{6,4},{7,5},{8,10},{9,11},{10,... | collective-permute-start | bytes 589832 | tf_op jit(solution)/shard_map/ppermute | solution.py:42
  249.3 58.0 %collective-permute-start.29 = (bf16[128,768]{1,0:T(8,128)(2,1)}, bf16[128,768]{1,0:T(8,128)(2,1)}, u32[]{:S(2)}, u32[]{:S(2)}) collective-permute-start(bf16[128,768]{1,0:T(8,128)(2,1)} %bitcast.97), channel_id=1, source_target_pairs={{0,3},{1,0},{2,1},{3,2},{4,7},{5,4},{6,5},{7,6},{8,11},{9,8},{10,9... | collective-permute-start | bytes 589832 | tf_op jit(solution)/shard_map/ppermute | solution.py:42
  313.1 57.6 %all-to-all-start.3 = ((bf16[8,2,4,32,768]{4,3,1,2,0:T(8,128)(2,1)}), bf16[8,2,4,32,768]{4,3,1,2,0:T(8,128)(2,1)}, u32[]{:S(2)}, u32[]{:S(2)}) async-start(bf16[8,2,4,32,768]{4,3,1,2,0:T(8,128)(2,1)} %bitcast.499), calls=%async_computation.3 | async-start | bytes 6291456 | tf_op jit(solution)/shard_map/all_to_all | solution.py:166
  379.6 64.0 %all-to-all-start = ((bf16[8,2,4,32,768]{4,3,1,2,0:T(8,128)(2,1)}), bf16[8,2,4,32,768]{4,3,1,2,0:T(8,128)(2,1)}, u32[]{:S(2)}, u32[]{:S(2)}) async-start(bf16[8,2,4,32,768]{4,3,1,2,0:T(8,128)(2,1)} %bitcast.498), calls=%async_computation | async-start | bytes 6291456 | tf_op jit(solution)/shard_map/all_to_all | solution.py:166
  512.4 178.3 %reduce-scatter.19.cloned.1.call-start = ((), (), s32[]{:S(2)}) async-start(), calls=%async_computation.25 | async-start | bytes 3538944
  531.1 75.0 %collective-permute-start.35 = (bf16[128,768]{1,0:T(8,128)(2,1)}, bf16[128,768]{1,0:T(8,128)(2,1)}, u32[]{:S(2)}, u32[]{:S(2)}) collective-permute-start(bf16[128,768]{1,0:T(8,128)(2,1)} %get-tuple-element.158), channel_id=1, source_target_pairs={{0,3},{1,0},{2,1},{3,2},{4,7},{5,4},{6,5},{7,6},{8,11},{9,8},{10,9... | collective-permute-start | bytes 589832 | tf_op jit(solution)/shard_map/ppermute | solution.py:42
  546.0 61.1 %collective-permute-start.34 = (bf16[128,768]{1,0:T(8,128)(2,1)S(1)}, bf16[128,768]{1,0:T(8,128)(2,1)}, u32[]{:S(2)}, u32[]{:S(2)}) collective-permute-start(bf16[128,768]{1,0:T(8,128)(2,1)S(1)} %get-tuple-element.159), channel_id=1, source_target_pairs={{0,2},{1,3},{2,0},{3,1},{4,6},{5,7},{6,4},{7,5},{8,10},{9,11},{10,... | collective-permute-start | bytes 589832 | tf_op jit(solution)/shard_map/ppermute | solution.py:42
  644.8 135.1 %reduce-scatter.21.cloned.1.call-start = ((), (), s32[]{:S(2)}) async-start(), calls=%async_computation.26 | async-start | bytes 3538944
  733.5 104.6 %reduce-scatter.13.cloned.1.call-start = ((), (), s32[]{:S(2)}) async-start(), calls=%async_computation.19 | async-start | bytes 5308416 | tf_op jit(solution)/shard_map/reduce_scatter | solution.py:87
  738.8 159.8 %reduce-scatter.15.cloned.1.call-start = ((), (), s32[]{:S(2)}) async-start(), calls=%async_computation.21 | async-start | bytes 5308416 | tf_op jit(solution)/shard_map/reduce_scatter | solution.py:87
  743.3 209.8 %reduce-scatter.17.cloned.1.call-start = ((), (), s32[]{:S(2)}) async-start(), calls=%async_computation.23 | async-start | bytes 5308416 | tf_op jit(solution)/shard_map/reduce_scatter | solution.py:87
  748.0 262.7 %reduce-scatter.11.cloned.1.call-start = ((), (), s32[]{:S(2)}) async-start(), calls=%async_computation.17 | async-start | bytes 5308416 | tf_op jit(solution)/shard_map/reduce_scatter | solution.py:87
  785.1 272.2 %all-gather.25.cloned.1.call-start = ((), (), s32[]{:S(2)}) async-start(), calls=%async_computation.20 | async-start | bytes 1327104 | tf_op jit(solution)/shard_map/all_gather | solution.py:90
  845.2 50.2 %collective-permute-start.51 = (bf16[2,192,768]{2,1,0:T(8,128)(2,1)S(1)}, bf16[2,192,768]{2,1,0:T(8,128)(2,1)}, u32[]{:S(2)}, u32[]{:S(2)}) collective-permute-start(bf16[2,192,768]{2,1,0:T(8,128)(2,1)S(1)} %get-tuple-element.151), channel_id=1, source_target_pairs={{0,1},{1,2},{2,3},{3,0},{4,5},{5,6},{6,7},{7,4},{8,9},{9,10},{10,1... | collective-permute-start | bytes 1769480 | tf_op jit(solution)/shard_map/ppermute | solution.py:42
  882.7 181.0 %all-gather.27.cloned.1.call-start = ((), (), s32[]{:S(2)}) async-start(), calls=%async_computation.22 | async-start | bytes 1327104 | tf_op jit(solution)/shard_map/all_gather | solution.py:90
  925.0 165.1 %all-gather.29.cloned.1.call-start = ((), (), s32[]{:S(2)}) async-start(), calls=%async_computation.24 | async-start | bytes 1327104 | tf_op jit(solution)/shard_map/all_gather | solution.py:90
  971.9 144.1 %all-gather.23.cloned.1.call-start = ((), (), s32[]{:S(2)}) async-start(), calls=%async_computation.18 | async-start | bytes 1327104 | tf_op jit(solution)/shard_map/all_gather | solution.py:90
  (162 other events, 2902.7 us)
Sparse Core Ops, SparseCore 0:
  31.5 41.2 all-gather.10
  77.2 32.3 all-gather.12
  112.0 38.9 all-gather.14
  153.2 38.9 all-gather.16
  194.5 38.9 all-gather.18
  237.8 32.4 all-gather.20
  644.9 45.6 reduce-scatter.18
  733.6 46.2 reduce-scatter.20
  783.9 54.1 reduce-scatter.12
  841.8 53.8 reduce-scatter.14
  899.1 53.8 reduce-scatter.16
  956.8 53.8 reduce-scatter.10
  1013.1 24.0 all-gather.24
  1039.5 24.2 all-gather.26
  1066.1 24.0 all-gather.28
  1091.9 24.0 all-gather.22

commit v2 on v1

--- a/solution.py
+++ b/solution.py
@@ -1,8 +1,11 @@
+import functools
 import math
 
 import jax
 import jax.numpy as jnp
 from jax import lax
+from jax.experimental import pallas as pl
+from jax.experimental.pallas import tpu as pltpu
 from jax.sharding import PartitionSpec as P
 
 D = 768
@@ -166,6 +169,830 @@
     return lax.all_to_all(blocks, "expert", split_axis=0, concat_axis=0, tiled=True)
 
 
+def plain_shards(
+    hidden_in,
+    attn_gain,
+    qkv_weight,
+    out_weight,
+    rel_bias,
+    bucket_table,
+    mlp_gain,
+    mlp_up,
+    mlp_down,
+    router_weight,
+    expert_up,
+    expert_down,
+    routes,
+    out_grad,
+):
+    block_rows = hidden_in.shape[1]
+    length = bucket_table.shape[0]
+    experts = lax.axis_size("expert")
+    groups = lax.axis_size("shard")
+    here = lax.axis_index("shard")
+    expert_total = EXP_DEV * experts
+    capacity = 4 * block_rows // expert_total
+    width = expert_down.shape[1]
+    scale = 1.0 / math.sqrt(HD)
+
+    small = jnp.concatenate(
+        [attn_gain.reshape(-1), mlp_gain.reshape(-1), rel_bias.reshape(-1), router_weight.reshape(-1)]
+    )
+    small = gather_shard(small)
+    part = D // groups
+    cuts = [0, 2 * part, 4 * part, 4 * part + 2 * (NB // groups) * H, small.shape[1]]
+    gain_attn, gain_mlp, bias_weights, router_full = (
+        small[:, cuts[i] : cuts[i + 1]] for i in range(4)
+    )
+    gain_attn = gain_attn.reshape(groups, 2, part).transpose(1, 0, 2).reshape(2, D).astype(single)
+    gain_mlp = gain_mlp.reshape(groups, 2, part).transpose(1, 0, 2).reshape(2, D).astype(single)
+    bias_weights = (
+        bias_weights.reshape(groups, 2, NB // groups, H).transpose(1, 0, 2, 3).reshape(2, NB, H)
+    )
+    router_full = router_full.reshape(D, expert_total)
+
+    first = gather_weight(jnp.concatenate([qkv_weight[0], out_weight[0]], axis=1))
+    dense_up = gather_weight(mlp_up)
+    dense_down = gather_weight(mlp_down)
+    second = gather_weight(jnp.concatenate([qkv_weight[1], out_weight[1]], axis=1))
+    qkv = (first[:, : 3 * D], second[:, : 3 * D])
+    projection = (first[:, 3 * D :], second[:, 3 * D :])
+
+    up_own = jnp.zeros((EXP_DEV, groups, part, width), bfloat)
+    for step in range(groups):
+        target = (here + step) % groups
+        piece = lax.dynamic_slice_in_dim(expert_up, target * width, width, 2)
+        if step:
+            piece = shard_shift(piece, step)
+        up_own = lax.dynamic_update_slice_in_dim(up_own, piece[:, None], (here - step) % groups, 1)
+    up_own = up_own.reshape(EXP_DEV, D, width)
+
+    route_rows = gather_shard(routes.reshape(block_rows, 2))
+    upstream_all = gather_shard(out_grad.reshape(block_rows, D))
+    expert_ids = jnp.arange(expert_total, dtype=jnp.int32)
+    flat_routes = route_rows.reshape(groups, -1)
+    marks = (flat_routes[:, :, None] == expert_ids).astype(jnp.int32)
+    rank = jnp.sum((jnp.cumsum(marks, axis=1) - marks) * marks, axis=2)
+    slot_of_route = flat_routes * capacity + rank
+    slot_ids = jnp.arange(expert_total * capacity, dtype=jnp.int32)
+    slot_marks = (slot_of_route[:, :, None] == slot_ids).astype(bfloat)
+    token_marks = jnp.sum(
+        slot_marks.reshape(groups, block_rows, 2, -1).astype(single), axis=2
+    ).astype(bfloat)
+
+    def dispatch(rows):
+        slots = jnp.einsum("gts,gtd->gsd", token_marks, rows, preferred_element_type=single)
+        slots = slots.astype(bfloat).reshape(groups, experts, EXP_DEV, capacity, D)
+        return exchange(slots.transpose(1, 2, 0, 3, 4)).reshape(
+            experts, EXP_DEV, groups * capacity, D
+        )
+
+    def collect(blocks):
+        back = exchange(blocks.astype(bfloat)).reshape(experts, EXP_DEV, groups, capacity, D)
+        return back.transpose(2, 0, 1, 3, 4).reshape(groups, expert_total * capacity, D)
+
+    owner_rows = dispatch(upstream_all)
+
+    own_positions = lax.axis_index("expert") * block_rows + jnp.arange(block_rows, dtype=jnp.int32)
+    distance = own_positions[:, None] - jnp.arange(length, dtype=jnp.int32)[None, :]
+    bounds = jnp.sum(
+        (bucket_table[:, None] < jnp.arange(NB + 1, dtype=jnp.int32)[None, :]).astype(jnp.int32),
+        axis=0,
+    )
+    geometry = (distance, bucket_marks(distance, bounds[:NB], bounds[1:]), scale)
+
+    hidden_zero = hidden_in.reshape(block_rows, D).astype(single)
+    mid_first, peak_first, saved_first = attention_forward(
+        hidden_zero, gain_attn[0], qkv[0], projection[0], bias_weights[0], geometry
+    )
+    dense_normed = spread(rms_norm(mid_first, gain_mlp[0]).astype(bfloat))
+    pre_act = matmul(dense_normed, dense_up)
+    activation = spread(jax.nn.gelu(pre_act).astype(bfloat))
+    layer_one = mid_first + matmul(activation, dense_down)
+    mid_second, peak_second, saved_second = attention_forward(
+        layer_one, gain_attn[1], qkv[1], projection[1], bias_weights[1], geometry
+    )
+
+    moe_normed = rms_norm(mid_second, gain_mlp[1]).astype(bfloat)
+    normed_all = gather_shard(moe_normed)
+    received = dispatch(normed_all)
+    router_logits = jnp.einsum("gtd,de->gte", normed_all, router_full, preferred_element_type=single)
+    selected = (route_rows[..., None] == expert_ids).astype(single)
+    gates_all = jax.nn.softmax(jnp.sum(selected * router_logits[:, :, None, :], axis=-1), axis=-1)
+    slot_gates = jnp.sum(
+        gates_all.reshape(groups, -1)[:, :, None] * (slot_of_route[:, :, None] == slot_ids), axis=1
+    )
+    owner_gates = exchange(
+        slot_gates.reshape(groups, experts, EXP_DEV, capacity).transpose(1, 2, 0, 3)
+    ).reshape(experts, EXP_DEV, groups * capacity)
+
+    expert_pre = jnp.einsum("sjcd,jdf->sjcf", received, up_own, preferred_element_type=single)
+    expert_act = jax.nn.gelu(expert_pre).astype(bfloat)
+    expert_out = jnp.einsum(
+        "sjcf,jfd->sjcd", expert_act, expert_down, preferred_element_type=single
+    )
+    owner_grad = (owner_gates[..., None] * owner_rows.astype(single)).astype(bfloat)
+    act_grad = jnp.einsum("sjcd,jfd->sjcf", owner_grad, expert_down, preferred_element_type=single)
+    pre_grad = gelu_back(expert_pre, act_grad).astype(bfloat)
+    row_grad = jnp.einsum("sjcf,jdf->sjcd", pre_grad, up_own, preferred_element_type=single)
+
+    returned = collect(expert_out)
+    back_rows = collect(row_grad)
+    expert_down_grad = jnp.einsum(
+        "sjcf,sjcd->jfd", expert_act, owner_grad, preferred_element_type=single
+    )
+    up_grad = jnp.einsum(
+        "sjcd,sjcf->jdf", received, pre_grad, preferred_element_type=single
+    ).astype(bfloat)
+
+    route_out = jnp.einsum("grs,gsd->grd", slot_marks, returned, preferred_element_type=single)
+    route_out = route_out.reshape(groups, block_rows, 2, D)
+    gate_grad = scatter_shard(
+        jnp.sum(route_out * upstream_all[:, :, None, :].astype(single), axis=-1), single
+    )
+    mixed = scatter_shard(jnp.sum(gates_all[..., None] * route_out, axis=2))
+    hidden_out = (mid_second + mixed).astype(bfloat).reshape(hidden_in.shape)
+
+    gates = lax.dynamic_index_in_dim(gates_all, here, 0, keepdims=False)
+    own_selected = lax.dynamic_index_in_dim(selected, here, 0, keepdims=False)
+    upstream = out_grad.reshape(block_rows, D).astype(single)
+    chosen_grad = gates * (gate_grad - jnp.sum(gates * gate_grad, axis=-1, keepdims=True))
+    logit_grad = jnp.sum(chosen_grad[:, :, None] * own_selected, axis=1).astype(bfloat)
+    router_grad = matmul(moe_normed.T, logit_grad)
+    row_terms = jnp.einsum("gts,gsd->gtd", token_marks, back_rows, preferred_element_type=single)
+    normed_grad = matmul(logit_grad, router_full.T) + scatter_shard(row_terms)
+    moe_input_grad, moe_gain_grad = norm_back(mid_second, gain_mlp[1], normed_grad)
+    mid_grad = upstream + moe_input_grad
+
+    up_grad = up_grad.reshape(EXP_DEV, groups, part, width)
+    expert_up_grad = jnp.zeros((EXP_DEV, part, groups * width), single)
+    for step in range(groups):
+        piece = lax.dynamic_index_in_dim(up_grad, (here + step) % groups, 1, keepdims=False)
+        if step:
+            piece = shard_shift(piece, step)
+        expert_up_grad = lax.dynamic_update_slice_in_dim(
+            expert_up_grad, piece.astype(single), ((here - step) % groups) * width, 2
+        )
+
+    layer_grad, gain_second, qkv_second, projection_second, bias_second = attention_backward(
+        mid_grad, layer_one, gain_attn[1], qkv[1], projection[1], bias_weights[1], geometry,
+        saved_second,
+    )
+    second_grad = reduce_weight(jnp.concatenate([qkv_second, projection_second], axis=1))
+    dense_branch = layer_grad.astype(bfloat)
+    mlp_down_grad = reduce_weight(matmul(activation.T, dense_branch))
+    hidden_act_grad = unspread(matmul(dense_branch, dense_down.T))
+    pre_act_grad = gelu_back(pre_act, hidden_act_grad).astype(bfloat)
+    mlp_up_grad = reduce_weight(matmul(dense_normed.T, pre_act_grad))
+    dense_normed_grad = unspread(matmul(pre_act_grad, dense_up.T))
+    dense_input_grad, dense_gain_grad = norm_back(mid_first, gain_mlp[0], dense_normed_grad)
+    first_grad = layer_grad + dense_input_grad
+    input_grad, gain_first, qkv_first, projection_first, bias_first = attention_backward(
+        first_grad, hidden_zero, gain_attn[0], qkv[0], projection[0], bias_weights[0], geometry,
+        saved_first,
+    )
+    first_weight_grad = reduce_weight(jnp.concatenate([qkv_first, projection_first], axis=1))
+
+    gains = jnp.stack([gain_first, gain_second, dense_gain_grad, moe_gain_grad])
+    biases = jnp.stack([bias_first, bias_second])
+    small_grad = jnp.concatenate(
+        [
+            gains.reshape(4, groups, part).transpose(1, 0, 2).reshape(groups, -1),
+            biases.reshape(2, groups, NB // groups, H).transpose(1, 0, 2, 3).reshape(groups, -1),
+            router_grad.reshape(groups, -1),
+        ],
+        axis=1,
+    )
+    small_grad = lax.psum(scatter_shard(small_grad, single), "expert")
+    gain_cut = 4 * part
+    bias_cut = gain_cut + 2 * (NB // groups) * H
+    own_gains = small_grad[:gain_cut].reshape(4, part)
+    peaks = lax.pmax(jnp.stack([peak_first, peak_second]), ("expert", "shard"))
+    clip_scales = jnp.sqrt(clip_limit / jnp.maximum(peaks, clip_limit))
+    return (
+        hidden_out,
+        input_grad.reshape(hidden_in.shape),
+        own_gains[:2],
+        jnp.stack([first_weight_grad[:, : 3 * D], second_grad[:, : 3 * D]]),
+        jnp.stack([first_weight_grad[:, 3 * D :], second_grad[:, 3 * D :]]),
+        small_grad[gain_cut:bias_cut].reshape(2, NB // groups, H),
+        own_gains[2:],
+        mlp_up_grad,
+        mlp_down_grad,
+        small_grad[bias_cut:].reshape(part, expert_total),
+        expert_up_grad,
+        expert_down_grad,
+        clip_scales,
+    )
+
+
+MESH = pl.DeviceIdType.MESH
+ANY = pl.ANY
+VMEM = pltpu.VMEM
+
+
+def place():
+    return lax.axis_index("expert"), lax.axis_index("shard")
+
+
+def greet(devices):
+    barrier = pltpu.get_barrier_semaphore()
+    for device in devices:
+        pl.semaphore_signal(barrier, inc=1, device_id=device, device_id_type=MESH)
+    pl.semaphore_wait(barrier, len(devices))
+
+
+def push(sent, source, target, send_sem, recv_sem, device):
+    copy = pltpu.make_async_remote_copy(
+        src_ref=source,
+        dst_ref=target,
+        send_sem=send_sem,
+        recv_sem=recv_sem,
+        device_id=device,
+        device_id_type=MESH,
+    )
+    copy.start()
+    sent.append(copy)
+    return copy
+
+
+def small_kernel(groups, small_ref, routes_ref, small_out, routes_out, ssem, rsem, lsem):
+    e, s = place()
+    others = [(e, lax.rem(s + k, groups)) for k in range(1, groups)]
+    local = [
+        pltpu.make_async_copy(small_ref, small_out.at[s], lsem.at[0]),
+        pltpu.make_async_copy(routes_ref, routes_out.at[s], lsem.at[1]),
+    ]
+    for copy in local:
+        copy.start()
+    greet(others)
+    sent = []
+    for k, device in enumerate(others):
+        push(sent, small_ref, small_out.at[s], ssem.at[0, k], rsem.at[0, k], device)
+        push(sent, routes_ref, routes_out.at[s], ssem.at[1, k], rsem.at[1, k], device)
+    for copy in local:
+        copy.wait()
+    for copy in sent:
+        copy.wait()
+
+
+def gather_small(small, routes):
+    groups = lax.axis_size("shard")
+    vmem = pl.BlockSpec(memory_space=VMEM)
+    return pl.pallas_call(
+        functools.partial(small_kernel, groups),
+        name="gather_small",
+        out_shape=(
+            jax.ShapeDtypeStruct((groups,) + small.shape, small.dtype),
+            jax.ShapeDtypeStruct((groups,) + routes.shape, routes.dtype),
+        ),
+        in_specs=[vmem, vmem],
+        out_specs=(vmem, vmem),
+        scratch_shapes=[
+            pltpu.SemaphoreType.DMA((2, groups - 1)),
+            pltpu.SemaphoreType.DMA((2, groups - 1)),
+            pltpu.SemaphoreType.DMA((2,)),
+        ],
+        compiler_params=pltpu.CompilerParams(collective_id=1, has_side_effects=True),
+    )(small, routes)
+
+
+def norm_rows(inputs, gain):
+    return inputs * lax.rsqrt(jnp.mean(inputs * inputs, axis=-1, keepdims=True) + epsilon) * gain
+
+
+def dot_rows(left, right):
+    return lax.dot_general(left, right, (((1,), (1,)), ((), ())), preferred_element_type=single)
+
+
+def loop(count, body):
+    def step(i, carry):
+        body(i)
+        return carry
+
+    lax.fori_loop(0, count, step, 0)
+
+
+def lane_block(i, width):
+    return pl.ds(pl.multiple_of(i * width, 128), width)
+
+
+def row_block(i, height):
+    return pl.ds(pl.multiple_of(i * height, height), height)
+
+
+T = 128
+PAIRS = H // 2
+TOE = 1152
+
+
+def forward_kernel(
+    hidden_ref,
+    gains_ref,
+    table_ref,
+    qkv_hbm,
+    out_hbm,
+    up_hbm,
+    down_hbm,
+    expert_up_hbm,
+    cot_hbm,
+    normed_out,
+    query_out,
+    attended_out,
+    mid_out,
+    dense_normed_out,
+    pre_out,
+    act_out,
+    one_out,
+    peak_out,
+    normed_all,
+    qkv0_out,
+    qkv1_out,
+    proj0_out,
+    proj1_out,
+    up_out,
+    down_out,
+    kv_out,
+    probs_out,
+    up_own,
+    cot_all,
+    w_qkv0,
+    w_qkv1,
+    w_out0,
+    w_out1,
+    w_up,
+    w_down,
+    kv,
+    probs,
+    scores,
+    zs,
+    zr,
+    f1s,
+    f1r,
+    f2s,
+    f2r,
+    cs,
+    cr,
+    locals_sem,
+    k1s,
+    k1r,
+    k2s,
+    k2r,
+    kcs,
+    kcr,
+    us,
+    ur,
+    gs,
+    gr,
+    ns,
+    nr,
+    outs_sem,
+):
+    e, s = place()
+    core = lax.rem(e, 2)
+    quarter = e // 2
+    at_x = e + 2 - 4 * lax.rem(quarter, 2)
+    at_y = lax.rem(e + 4, 8)
+    at_core = e + 1 - 2 * core
+    inward = jnp.where(core == 0, at_x, at_y)
+    onward = jnp.where(core == 0, at_y, at_x)
+    others = [lax.rem(s + k, 4) for k in range(1, 4)]
+    sources = [lax.rem(s + 4 - k, 4) for k in range(1, 4)]
+    sent = []
+    kept = []
+
+    def local(source, target, sem):
+        copy = pltpu.make_async_copy(source, target, sem)
+        copy.start()
+        return copy
+
+    chunks = [
+        (qkv_hbm.at[0], w_qkv0, 48, 1152),
+        (out_hbm.at[0], w_out0, 48, 384),
+        (up_hbm, w_up, 48, 1536),
+        (down_hbm, w_down, 192, 384),
+        (qkv_hbm.at[1], w_qkv1, 48, 1152),
+        (out_hbm.at[1], w_out1, 48, 384),
+    ]
+
+    def block(target, who, position, height, half, width):
+        rows = pl.ds(pl.multiple_of(position * 4 * height + who * height, height), height)
+        return target.at[rows, lane_block(half, width)]
+
+    stage1, stage2, stage3, stage4, own = {}, {}, {}, {}, {}
+
+    def z_send(c):
+        source, target, height, width = chunks[c]
+        piece = source.at[row_block(quarter, height), lane_block(core, width)]
+        mine = block(target, quarter, s, height, core, width)
+        stage1[c] = [
+            push(sent, piece, mine, zs.at[c, k], zr.at[c, k], (e, others[k])) for k in range(3)
+        ]
+        own[c] = local(source, target.at[row_block(s, 4 * height), :], locals_sem.at[c])
+
+    def plane_send(c):
+        _, target, height, width = chunks[c]
+        stage2[c] = []
+        for k in range(3):
+            stage1[c][k].wait_recv()
+            mine = block(target, quarter, sources[k], height, core, width)
+            stage2[c].append(
+                [
+                    push(sent, mine, mine, f1s.at[c, k, i], f1r.at[c, k, i], (partner, s))
+                    for i, partner in enumerate((at_x, at_y))
+                ]
+            )
+
+    def plane_forward(c):
+        _, target, height, width = chunks[c]
+        stage3[c] = []
+        for k in range(3):
+            pltpu.make_async_remote_copy(
+                src_ref=block(target, quarter, sources[k], height, core, width),
+                dst_ref=block(target, quarter, sources[k], height, core, width),
+                send_sem=f1s.at[c, k, core],
+                recv_sem=f1r.at[c, k, core],
+                device_id=(inward, s),
+                device_id_type=MESH,
+            ).wait_recv()
+            theirs = block(target, inward // 2, sources[k], height, core, width)
+            stage3[c].append(
+                push(sent, theirs, theirs, f2s.at[c, k], f2r.at[c, k], (onward, s))
+            )
+
+    def core_send(c):
+        _, target, height, width = chunks[c]
+        stage4[c] = []
+        for k in range(3):
+            pltpu.make_async_remote_copy(
+                src_ref=block(target, quarter, sources[k], height, core, width),
+                dst_ref=block(target, quarter, sources[k], height, core, width),
+                send_sem=f1s.at[c, k, 1 - core],
+                recv_sem=f1r.at[c, k, 1 - core],
+                device_id=(onward, s),
+                device_id_type=MESH,
+            ).wait_recv()
+            stage3[c][k].wait_recv()
+            half = target.at[row_block(sources[k], 4 * height), lane_block(core, width)]
+            stage4[c].append(push(sent, half, half, cs.at[c, k], cr.at[c, k], (at_core, s)))
+
+    weight_outs = [qkv0_out, proj0_out, up_out, down_out, qkv1_out, proj1_out]
+
+    def ready(c):
+        for k in range(3):
+            stage4[c][k].wait_recv()
+        own[c].wait()
+        kept.append(local(chunks[c][1], weight_outs[c], outs_sem.at[c]))
+
+    greet(
+        [(at_core, s), (at_x, s), (at_y, s)] + [(e, other) for other in others]
+    )
+    z_send(0)
+    z_send(1)
+    z_send(2)
+
+    def attention(layer, inputs, w_qkv, w_out, work):
+        normed = norm_rows(inputs, gains_ref[pl.ds(layer, 1), :]).astype(bfloat)
+        normed_out[layer] = normed
+        if layer == 0:
+            plane_send(0)
+            plane_forward(0)
+            core_send(0)
+            ready(0)
+        else:
+            ready(4)
+        own_rows = row_block(e, T)
+        first, second, third = [], [], []
+        for part in range(3):
+            x = normed_out[layer]
+            for i, base in enumerate((D, 2 * D)):
+                columns = w_qkv[:, base + 256 * part : base + 256 * (part + 1)]
+                kv[layer, part, own_rows, 256 * i : 256 * (i + 1)] = jnp.dot(
+                    x, columns, preferred_element_type=single
+                ).astype(bfloat)
+            mine = kv.at[layer, part, own_rows, :]
+            first.append(
+                [
+                    push(sent, mine, mine, k1s.at[layer, part, i], k1r.at[layer, part, i], (p, s))
+                    for i, p in enumerate((at_x, at_y))
+                ]
+            )
+            third.append(
+                [
+                    push(
+                        sent, mine, mine, kcs.at[layer, part, 0], kcr.at[layer, part, 0],
+                        (at_core, s),
+                    )
+                ]
+            )
+        query_out[layer] = jnp.dot(
+            normed_out[layer], w_qkv[:, :D], preferred_element_type=single
+        ).astype(bfloat)
+        if work:
+            work[0]()
+        at_diagonal = inward + onward - e
+        for part in range(3):
+            pltpu.make_async_remote_copy(
+                src_ref=kv.at[layer, part, own_rows, :],
+                dst_ref=kv.at[layer, part, own_rows, :],
+                send_sem=k1s.at[layer, part, core],
+                recv_sem=k1r.at[layer, part, core],
+                device_id=(inward, s),
+                device_id_type=MESH,
+            ).wait_recv()
+            theirs = kv.at[layer, part, row_block(inward, T), :]
+            second.append(
+                push(
+                    sent, theirs, theirs, k2s.at[layer, part], k2r.at[layer, part], (onward, s)
+                )
+            )
+            third[part].append(
+                push(
+                    sent, theirs, theirs, kcs.at[layer, part, 1], kcr.at[layer, part, 1],
+                    (at_core, s),
+                )
+            )
+        if work:
+            work[1]()
+        for part in range(3):
+            pltpu.make_async_remote_copy(
+                src_ref=kv.at[layer, part, own_rows, :],
+                dst_ref=kv.at[layer, part, own_rows, :],
+                send_sem=k1s.at[layer, part, 1 - core],
+                recv_sem=k1r.at[layer, part, 1 - core],
+                device_id=(onward, s),
+                device_id_type=MESH,
+            ).wait_recv()
+            theirs = kv.at[layer, part, row_block(onward, T), :]
+            third[part].append(
+                push(
+                    sent, theirs, theirs, kcs.at[layer, part, 2], kcr.at[layer, part, 2],
+                    (at_core, s),
+                )
+            )
+            second[part].wait_recv()
+            theirs = kv.at[layer, part, row_block(at_diagonal, T), :]
+            third[part].append(
+                push(
+                    sent, theirs, theirs, kcs.at[layer, part, 3], kcr.at[layer, part, 3],
+                    (at_core, s),
+                )
+            )
+        for part in range(3):
+            for i in range(4):
+                third[part][i].wait_recv()
+
+            def one_pair(local_pair):
+                pair = 2 * part + local_pair
+                lanes = lane_block(pair, 128)
+                queries = query_out[layer, :, lanes]
+                lane = lax.broadcasted_iota(jnp.int32, (T, 128), 1)
+                zero = jnp.zeros_like(queries)
+                both = jnp.concatenate(
+                    [jnp.where(lane < HD, queries, zero), jnp.where(lane >= HD, queries, zero)]
+                )
+                keys = kv[layer, part, :, lane_block(local_pair, 128)]
+                scores[...] = dot_rows(both, keys) * (1.0 / math.sqrt(HD))
+                for half in range(2):
+                    head = 2 * pair + half
+                    toeplitz = table_ref[pl.ds(layer * H + head, 1), :]
+                    peak = jnp.full((1, 1), -jnp.inf, single)
+                    for rows in range(0, T, 32):
+                        raw = scores[half * T + rows : half * T + rows + 32, :]
+                        row = e * T + rows + lax.broadcasted_iota(jnp.int32, raw.shape, 0)
+                        causal = row >= lax.broadcasted_iota(jnp.int32, raw.shape, 1)
+                        shifted = pltpu.roll(
+                            jnp.broadcast_to(toeplitz, (32, TOE)),
+                            TOE - (T - 1) + rows,
+                            1,
+                            stride=1,
+                            stride_axis=0,
+                        )[:, : raw.shape[1]]
+                        peak = jnp.maximum(
+                            peak, jnp.max(jnp.where(causal, raw, -jnp.inf), keepdims=True)
+                        )
+                        masked = jnp.where(causal, raw + shifted, -jnp.inf)
+                        top = jnp.max(masked, axis=-1, keepdims=True)
+                        exponent = jnp.exp(masked - top)
+                        total = jnp.sum(exponent, axis=-1, keepdims=True)
+                        probs[layer, pl.ds(pl.multiple_of(head * T + rows, 32), 32), :] = (
+                            exponent / total
+                        ).astype(bfloat)
+                    peak_out[pl.ds(layer * H + head, 1), :] = jnp.broadcast_to(peak, (1, 128))
+                values = kv[layer, part, :, pl.ds(pl.multiple_of(256 + local_pair * 128, 128), 128)]
+                mixed = jnp.dot(
+                    probs[layer, pl.ds(pl.multiple_of(pair * 2 * T, 2 * T), 2 * T), :],
+                    values,
+                    preferred_element_type=single,
+                )
+                attended_out[layer, :, lanes] = jnp.where(
+                    lane < HD, mixed[:T], mixed[T:]
+                ).astype(bfloat)
+
+            loop(2, one_pair)
+            if work:
+                work[2 + part]()
+        kept.append(local(kv.at[layer], kv_out.at[layer], outs_sem.at[6 + layer]))
+        kept.append(local(probs.at[layer], probs_out.at[layer], outs_sem.at[8 + layer]))
+
+    def nothing():
+        pass
+
+    def work0():
+        plane_send(1)
+        z_send(3)
+
+    def work1():
+        plane_forward(1)
+
+    def work2():
+        core_send(1)
+        plane_send(2)
+
+    def work3():
+        plane_forward(2)
+        z_send(4)
+        z_send(5)
+
+    def work4():
+        core_send(2)
+        plane_send(3)
+
+    hidden = hidden_ref[...].astype(single)
+    attention(0, hidden, w_qkv0, w_out0, [work0, work1, work2, work3, work4])
+    ready(1)
+    mid_out[0] = hidden + jnp.dot(
+        attended_out[0], w_out0[...], preferred_element_type=single
+    )
+    dense_normed_out[...] = norm_rows(mid_out[0], gains_ref[pl.ds(2, 1), :]).astype(bfloat)
+    reshard = []
+    for k in range(3):
+        reshard.append(
+            push(
+                sent,
+                expert_up_hbm.at[:, :, lane_block(others[k], 768)],
+                up_own.at[:, row_block(s, 192), :],
+                us.at[k],
+                ur.at[k],
+                (e, others[k]),
+            )
+        )
+        reshard.append(
+            push(sent, cot_hbm, cot_all.at[s], gs.at[k], gr.at[k], (e, others[k]))
+        )
+    kept.append(
+        local(
+            expert_up_hbm.at[:, :, lane_block(s, 768)],
+            up_own.at[:, row_block(s, 192), :],
+            us.at[3],
+        )
+    )
+    kept.append(local(cot_hbm, cot_all.at[s], gs.at[3]))
+    ready(2)
+
+    def up_part(i):
+        lanes = lane_block(i, 512)
+        before = jnp.dot(dense_normed_out[...], w_up[:, lanes], preferred_element_type=single)
+        pre_out[:, lanes] = before
+        act_out[:, lanes] = jax.nn.gelu(before).astype(bfloat)
+
+    plane_forward(3)
+    loop(3, up_part)
+    core_send(3)
+    plane_send(4)
+    plane_send(5)
+
+    def up_later(i):
+        up_part(i + 3)
+
+    loop(3, up_later)
+    plane_forward(4)
+    plane_forward(5)
+    ready(3)
+    one_out[...] = mid_out[0]
+
+    def down_part(i):
+        rows = row_block(i, 768)
+        one_out[...] += jnp.dot(
+            act_out[:, lane_block(i, 768)], w_down[rows, :], preferred_element_type=single
+        )
+
+    loop(4, down_part)
+    core_send(4)
+    core_send(5)
+    attention(1, one_out[...], w_qkv1, w_out1, None)
+    ready(5)
+    mid_out[1] = one_out[...] + jnp.dot(
+        attended_out[1], w_out1[...], preferred_element_type=single
+    )
+    normed_all[s] = norm_rows(mid_out[1], gains_ref[pl.ds(3, 1), :]).astype(bfloat)
+    last = [
+        push(sent, normed_all.at[s], normed_all.at[s], ns.at[k], nr.at[k], (e, others[k]))
+        for k in range(3)
+    ]
+    for copy in last + reshard:
+        copy.wait_recv()
+    for copy in kept:
+        copy.wait()
+    for copy in sent:
+        copy.wait_send()
+
+
+def forward(hidden, gains, table, qkv, out, up, down, expert_up, cotangent):
+    length = T * lax.axis_size("expert")
+    vmem = pl.BlockSpec(memory_space=VMEM)
+    anywhere = pl.BlockSpec(memory_space=ANY)
+    shape = jax.ShapeDtypeStruct
+    ff = up.shape[1]
+    sem = pltpu.SemaphoreType.DMA
+    return pl.pallas_call(
+        forward_kernel,
+        name="forward_layers",
+        out_shape=(
+            shape((2, T, D), bfloat),
+            shape((2, T, D), bfloat),
+            shape((2, T, D), bfloat),
+            shape((2, T, D), single),
+            shape((T, D), bfloat),
+            shape((T, ff), single),
+            shape((T, ff), bfloat),
+            shape((T, D), single),
+            shape((2 * H, 128), single),
+            shape((4, T, D), bfloat),
+            shape((D, 3 * D), bfloat),
+            shape((D, 3 * D), bfloat),
+            shape((D, D), bfloat),
+            shape((D, D), bfloat),
+            shape((D, ff), bfloat),
+            shape((ff, D), bfloat),
+            shape((2, 3, length, 512), bfloat),
+            shape((2, H * T, length), bfloat),
+            shape((EXP_DEV, D, 768), bfloat),
+            shape((4, T, D), bfloat),
+        ),
+        in_specs=[vmem] * 3 + [anywhere] * 6,
+        out_specs=(vmem,) * 10 + (anywhere,) * 10,
+        scratch_shapes=[
+            VMEM((D, 3 * D), bfloat),
+            VMEM((D, 3 * D), bfloat),
+            VMEM((D, D), bfloat),
+            VMEM((D, D), bfloat),
+            VMEM((D, ff), bfloat),
+            VMEM((ff, D), bfloat),
+            VMEM((2, 3, length, 512), bfloat),
+            VMEM((2, H * T, length), bfloat),
+            VMEM((2 * T, length), single),
+            sem((6, 3)), sem((6, 3)),
+            sem((6, 3, 2)), sem((6, 3, 2)),
+            sem((6, 3)), sem((6, 3)),
+            sem((6, 3)), sem((6, 3)),
+            sem((6,)),
+            sem((2, 3, 2)), sem((2, 3, 2)),
+            sem((2, 3)), sem((2, 3)),
+            sem((2, 3, 4)), sem((2, 3, 4)),
+            sem((4,)), sem((3,)),
+            sem((4,)), sem((3,)),
+            sem((3,)), sem((3,)),
+            sem((10,)),
+        ],
+        compiler_params=pltpu.CompilerParams(
+            collective_id=2, has_side_effects=True, vmem_limit_bytes=56 * 2**20
+        ),
+    )(hidden, gains, table, qkv, out, up, down, expert_up, cotangent)
+
+
+def kernel_backward(upstream, hidden, norm_gain, qkv, projection, marks, saved):
+    normalized, queries, kv, probs, attended = saved
+    rows = hidden.shape[0]
+    scale = 1.0 / math.sqrt(HD)
+    branch_grad = upstream.astype(bfloat)
+    projection_grad = matmul(spread(attended).T, branch_grad)
+    attended_grad = matmul(branch_grad, projection.T).astype(bfloat)
+    queries = queries.reshape(rows, H, HD)
+    keys = kv[:, :, :256].transpose(1, 0, 2).reshape(-1, H, HD)
+    values = kv[:, :, 256:].transpose(1, 0, 2).reshape(-1, H, HD)
+    grad_heads = attended_grad.reshape(rows, H, HD)
+    probs_low = probs.reshape(H, rows, -1)
+    probs = probs_low.astype(single)
+    prob_grad = jnp.einsum("ihd,jhd->hij", grad_heads, values, preferred_element_type=single)
+    row_dot = jnp.sum(prob_grad * probs, axis=-1)
+    score_grad = (probs * (prob_grad - row_dot[..., None])).astype(bfloat)
+    query_grad = jnp.einsum("hij,jhd->ihd", score_grad, keys, preferred_element_type=single) * scale
+    query_grad = query_grad.astype(bfloat).reshape(rows, D)
+    bias_grad = jnp.einsum("hij,bij->bh", score_grad, marks, preferred_element_type=single)
+    key_grad = (
+        jnp.einsum("hij,ihd->jhd", score_grad, queries, preferred_element_type=single) * scale
+    )
+    value_grad = jnp.einsum("hij,ihd->jhd", probs_low, grad_heads, preferred_element_type=single)
+    pair = jnp.concatenate([key_grad.reshape(-1, D), value_grad.reshape(-1, D)], axis=-1)
+    pair_grad = lax.psum_scatter(pair.astype(bfloat), "expert", scatter_dimension=0, tiled=True)
+    packed_grad = jnp.concatenate([query_grad, pair_grad], axis=-1)
+    qkv_grad = matmul(spread(normalized).T, packed_grad)
+    normed_grad = matmul(packed_grad, qkv.T)
+    input_grad, gain_grad = norm_back(hidden, norm_gain, normed_grad)
+    return upstream + input_grad, gain_grad, qkv_grad, projection_grad, bias_grad
+
+
 def shards(
     hidden_in,
     attn_gain,
@@ -190,42 +1017,51 @@
     expert_total = EXP_DEV * experts
     capacity = 4 * block_rows // expert_total
     width = expert_down.shape[1]
-    scale = 1.0 / math.sqrt(HD)
 
     small = jnp.concatenate(
         [attn_gain.reshape(-1), mlp_gain.reshape(-1), rel_bias.reshape(-1), router_weight.reshape(-1)]
-    )
-    small = gather_shard(small)
+    ).astype(single)
     part = D // groups
-    cuts = [0, 2 * part, 4 * part, 4 * part + 2 * (NB // groups) * H, small.shape[1]]
-    gain_attn, gain_mlp, bias_weights, router_full = (
-        small[:, cuts[i] : cuts[i + 1]] for i in range(4)
-    )
-    gain_attn = gain_attn.reshape(groups, 2, part).transpose(1, 0, 2).reshape(2, D).astype(single)
-    gain_mlp = gain_mlp.reshape(groups, 2, part).transpose(1, 0, 2).reshape(2, D).astype(single)
+    used = small.shape[0]
+    small = jnp.pad(small, (0, -used % 1024)).reshape(-1, 128)
+    small, route_rows = gather_small(small, routes.reshape(-1, 128))
+    small = small.reshape(groups, -1)
+    route_rows = route_rows.reshape(groups, block_rows, 2)
+    cuts = [0, 4 * part, 4 * part + 2 * (NB // groups) * H, used]
+    gains, bias_weights, router_full = (small[:, cuts[i] : cuts[i + 1]] for i in range(3))
+    gains = gains.reshape(groups, 4, part).transpose(1, 0, 2).reshape(4, D)
+    gain_attn, gain_mlp = gains[:2], gains[2:]
     bias_weights = (
         bias_weights.reshape(groups, 2, NB // groups, H).transpose(1, 0, 2, 3).reshape(2, NB, H)
     )
-    router_full = router_full.reshape(D, expert_total)
-
-    first = gather_weight(jnp.concatenate([qkv_weight[0], out_weight[0]], axis=1))
-    dense_up = gather_weight(mlp_up)
-    dense_down = gather_weight(mlp_down)
-    second = gather_weight(jnp.concatenate([qkv_weight[1], out_weight[1]], axis=1))
-    qkv = (first[:, : 3 * D], second[:, : 3 * D])
-    projection = (first[:, 3 * D :], second[:, 3 * D :])
-
-    up_own = jnp.zeros((EXP_DEV, groups, part, width), bfloat)
-    for step in range(groups):
-        target = (here + step) % groups
-        piece = lax.dynamic_slice_in_dim(expert_up, target * width, width, 2)
-        if step:
-            piece = shard_shift(piece, step)
-        up_own = lax.dynamic_update_slice_in_dim(up_own, piece[:, None], (here - step) % groups, 1)
-    up_own = up_own.reshape(EXP_DEV, D, width)
-
-    route_rows = gather_shard(routes.reshape(block_rows, 2))
-    upstream_all = gather_shard(out_grad.reshape(block_rows, D))
+    router_full = router_full.reshape(D, expert_total).astype(bfloat)
+
+    distances = lax.axis_index("expert") * block_rows + block_rows - 1 - jnp.arange(TOE)
+    buckets = jnp.take(bucket_table, jnp.clip(distances, 0, length - 1))
+    toeplitz_marks = (buckets[None] == jnp.arange(NB, dtype=jnp.int32)[:, None]).astype(bfloat)
+    table = jnp.einsum(
+        "lbh,bm->lhm", bias_weights.astype(bfloat), toeplitz_marks, preferred_element_type=single
+    ).reshape(2 * H, TOE)
+
+    (
+        normed, queries, attended, mid, dense_normed, pre_act, activation, layer_one, peak_rows,
+        normed_all, qkv0, qkv1, projection0, projection1, dense_up, dense_down, kv, probs, up_own,
+        upstream_all,
+    ) = forward(
+        hidden_in.reshape(block_rows, D), gains, table, qkv_weight, out_weight, mlp_up, mlp_down,
+        expert_up, out_grad.reshape(block_rows, D),
+    )
+    mid_first, mid_second = mid[0], mid[1]
+    hidden_zero = hidden_in.reshape(block_rows, D).astype(single)
+    moe_normed = lax.dynamic_index_in_dim(normed_all, here, 0, keepdims=False)
+    own_positions = lax.axis_index("expert") * block_rows + jnp.arange(block_rows, dtype=jnp.int32)
+    distance = own_positions[:, None] - jnp.arange(length, dtype=jnp.int32)[None, :]
+    bounds = jnp.sum(
+        (bucket_table[:, None] < jnp.arange(NB + 1, dtype=jnp.int32)[None, :]).astype(jnp.int32),
+        axis=0,
+    )
+    attention_marks = bucket_marks(distance, bounds[:NB], bounds[1:])
+
     expert_ids = jnp.arange(expert_total, dtype=jnp.int32)
     flat_routes = route_rows.reshape(groups, -1)
     marks = (flat_routes[:, :, None] == expert_ids).astype(jnp.int32)
@@ -249,29 +1085,6 @@
         return back.transpose(2, 0, 1, 3, 4).reshape(groups, expert_total * capacity, D)
 
     owner_rows = dispatch(upstream_all)
-
-    own_positions = lax.axis_index("expert") * block_rows + jnp.arange(block_rows, dtype=jnp.int32)
-    distance = own_positions[:, None] - jnp.arange(length, dtype=jnp.int32)[None, :]
-    bounds = jnp.sum(
-        (bucket_table[:, None] < jnp.arange(NB + 1, dtype=jnp.int32)[None, :]).astype(jnp.int32),
-        axis=0,
-    )
-    geometry = (distance, bucket_marks(distance, bounds[:NB], bounds[1:]), scale)
-
-    hidden_zero = hidden_in.reshape(block_rows, D).astype(single)
-    mid_first, peak_first, saved_first = attention_forward(
-        hidden_zero, gain_attn[0], qkv[0], projection[0], bias_weights[0], geometry
-    )
-    dense_normed = spread(rms_norm(mid_first, gain_mlp[0]).astype(bfloat))
-    pre_act = matmul(dense_normed, dense_up)
-    activation = spread(jax.nn.gelu(pre_act).astype(bfloat))
-    layer_one = mid_first + matmul(activation, dense_down)
-    mid_second, peak_second, saved_second = attention_forward(
-        layer_one, gain_attn[1], qkv[1], projection[1], bias_weights[1], geometry
-    )
-
-    moe_normed = rms_norm(mid_second, gain_mlp[1]).astype(bfloat)
-    normed_all = gather_shard(moe_normed)
     received = dispatch(normed_all)
     router_logits = jnp.einsum("gtd,de->gte", normed_all, router_full, preferred_element_type=single)
     selected = (route_rows[..., None] == expert_ids).astype(single)
@@ -331,22 +1144,22 @@
             expert_up_grad, piece.astype(single), ((here - step) % groups) * width, 2
         )
 
-    layer_grad, gain_second, qkv_second, projection_second, bias_second = attention_backward(
-        mid_grad, layer_one, gain_attn[1], qkv[1], projection[1], bias_weights[1], geometry,
-        saved_second,
+    layer_grad, gain_second, qkv_second, projection_second, bias_second = kernel_backward(
+        mid_grad, layer_one, gain_attn[1], qkv1, projection1, attention_marks,
+        (normed[1], queries[1], kv[1], probs[1], attended[1]),
     )
     second_grad = reduce_weight(jnp.concatenate([qkv_second, projection_second], axis=1))
     dense_branch = layer_grad.astype(bfloat)
-    mlp_down_grad = reduce_weight(matmul(activation.T, dense_branch))
-    hidden_act_grad = unspread(matmul(dense_branch, dense_down.T))
+    mlp_down_grad = reduce_weight(matmul(spread(activation).T, dense_branch))
+    hidden_act_grad = matmul(dense_branch, dense_down.T)
     pre_act_grad = gelu_back(pre_act, hidden_act_grad).astype(bfloat)
-    mlp_up_grad = reduce_weight(matmul(dense_normed.T, pre_act_grad))
-    dense_normed_grad = unspread(matmul(pre_act_grad, dense_up.T))
+    mlp_up_grad = reduce_weight(matmul(spread(dense_normed).T, pre_act_grad))
+    dense_normed_grad = matmul(pre_act_grad, dense_up.T)
     dense_input_grad, dense_gain_grad = norm_back(mid_first, gain_mlp[0], dense_normed_grad)
     first_grad = layer_grad + dense_input_grad
-    input_grad, gain_first, qkv_first, projection_first, bias_first = attention_backward(
-        first_grad, hidden_zero, gain_attn[0], qkv[0], projection[0], bias_weights[0], geometry,
-        saved_first,
+    input_grad, gain_first, qkv_first, projection_first, bias_first = kernel_backward(
+        first_grad, hidden_zero, gain_attn[0], qkv0, projection0, attention_marks,
+        (normed[0], queries[0], kv[0], probs[0], attended[0]),
     )
     first_weight_grad = reduce_weight(jnp.concatenate([qkv_first, projection_first], axis=1))
 
@@ -364,7 +1177,7 @@
     gain_cut = 4 * part
     bias_cut = gain_cut + 2 * (NB // groups) * H
     own_gains = small_grad[:gain_cut].reshape(4, part)
-    peaks = lax.pmax(jnp.stack([peak_first, peak_second]), ("expert", "shard"))
+    peaks = lax.pmax(peak_rows[:, 0].reshape(2, H), ("expert", "shard"))
     clip_scales = jnp.sqrt(clip_limit / jnp.maximum(peaks, clip_limit))
     return (
         hidden_out,
@@ -397,4 +1210,6 @@
         tokens, tokens, columns, layers, layers, layers, columns, rows, rows, rows, owned, owned,
         P(),
     )
-    return jax.shard_map(shards, mesh=mesh, in_specs=in_specs, out_specs=out_specs, check_vma=False)
+    sized = mesh.shape["expert"] == 8 and mesh.shape["shard"] == 4
+    part = shards if sized else plain_shards
+    return jax.shard_map(part, mesh=mesh, in_specs=in_specs, out_specs=out_specs, check_vma=False)

time: 1140 us -> 931 us (0.82)
  Pallas kernels: 0 us -> 165 us
  waiting for transfers between devices: 447 us -> 290 us
  matrix products: 175 us -> 105 us
  starting transfers between devices: 152 us -> 82 us
  local copies, waits for them, and re-layouts: 190 us -> 134 us
  other arithmetic: 86 us -> 66.8 us
    pallas_call x0 -> x2, Pallas kernels: none -> 165 us  [the longest x1 156 us: forward(): pl.pallas_call(forward_kernel, name='forward_layers', out_shape=(shape((2...]
    all_gather x6 -> x0, waiting for transfers between devices: 90.7 us -> none  [the longest x4 90.6 us: gather_weight(): return lax.all_gather(column, 'expert', axis=0, tiled=True)]
    ppermute x54 -> x27, starting transfers between devices: 128 us -> 55.5 us  [shard_shift(): lax.ppermute(block, 'shard', [(i, (i + amount) % count) for i in range(co...]
    ppermute x54 -> x27, waiting for transfers between devices: 144 us -> 74.7 us  [shard_shift(): lax.ppermute(block, 'shard', [(i, (i + amount) % count) for i in range(co...]
    all_to_all x5, waiting for transfers between devices: 34 us -> 94.3 us  [exchange(): lax.all_to_all(blocks, 'expert', split_axis=0, concat_axis=0, tiled=True)]
    dynamic_update_slice x35 -> x0, local copies, waits for them, and re-layouts: 58 us -> none  [the longest x30 49.6 us: gather_shard(): lax.dynamic_update_slice_in_dim(result, piece[None], (here - step) % coun...]
    unnamed x18 -> x12, waiting for transfers between devices: 68.9 us -> 22.1 us
    dot_general x16 -> x11, matrix products: 78.7 us -> 32.8 us  [the longest x2 14.1 us: kernel_backward(): jnp.einsum('hij,bij->bh', score_grad, marks, preferred_element_type=single)]
  transfers between devices with their start and end apart: 75 -> 42, of which waited for: 37 -> 20; matrix products, arithmetic and copies ran while one was open for 29% -> 23% of each run, Pallas kernels for 0% -> 0%
where the time goes in v2:
time: 931 us; the launch traced here: 920 us
  waiting for transfers between devices  290 us (31%)
  Pallas kernels  165 us (18%)
  local copies, waits for them, and re-layouts  134 us (14%)
  matrix products  105 us (11%)
  starting transfers between devices  82 us (9%)
  other arithmetic  66.8 us (7%)
  blocking collectives  62.1 us (7%)
  between operations  16 us (2%)
    pallas_call x1, Pallas kernels, forward(): pl.pallas_call(forward_kernel, name='forward_layers', out_shape=(shape((2...  156 us
    all_to_all x5, waiting for transfers between devices, exchange(): lax.all_to_all(blocks, 'expert', split_axis=0, concat_axis=0, tiled=True)  94.3 us
    ppermute x27, waiting for transfers between devices, shard_shift(): lax.ppermute(block, 'shard', [(i, (i + amount) % count) for i in range(co...  74.7 us
    ppermute x27, starting transfers between devices, shard_shift(): lax.ppermute(block, 'shard', [(i, (i + amount) % count) for i in range(co...  55.5 us
    reduce_scatter x4, waiting for transfers between devices, reduce_weight(): lax.psum_scatter(grad.astype(bfloat), 'expert', scatter_dimension=0, tile...  55 us
    all_gather x4, waiting for transfers between devices, reduce_weight(): return lax.all_gather(own, 'expert', axis=0, tiled=True).astype(single)  43.5 us
    pmax x1, blocking collectives, shards(): peaks = lax.pmax(peak_rows[:, 0].reshape(2, H), ('expert', 'shard'))  39.4 us
    unnamed x138, local copies, waits for them, and re-layouts  30.8 us
  transfers between devices with their start and end apart: 42, of which 20 were waited for; matrix products, arithmetic and copies ran while one was open for 23% of the time, Pallas kernels for 0%

profile of v2, /device:TPU:0, one launch (start us, length us, event | category | flops | bytes accessed | tf_op | source)
XLA Modules:
  0.0 920.1 jit_solution(11246279588139398311)
XLA Ops:
  12.8 9.1 gather_small.1
  34.6 155.7 %forward_layers.1 = (bf16[2,128,768]{2,1,0:T(8,128)(2,1)}, bf16[2,128,768]{2,1,0:T(8,128)(2,1)}, bf16[2,128,768]{2,1,0:T(8,128)(2,1)}, f32[2,128,768]{2,1,0:T(8,...) custom-call(bf16[128,768]{1,0:T(8,128)(2,1)} %bitcast.468, ...), custom_call_target="tpu_custom_call" | custom-call | tf_op jit(solution)/shard_map/forward_layers/pallas_call | solution.py:908
  193.4 7.1 all-to-all-start.2
  213.9 33.7 %all-to-all-done = bf16[8,2,4,32,768]{4,3,1,2,0:T(8,128)(2,1)} async-done(((bf16[8,2,4,32,768]{4,3,1,2,0:T(8,128)(2,1)}), bf16[8,2,4,32,768]{4,3,1,2,0:T(8,128)(2,1)}, u32[]{:S(2)}, u32[]{:S(2)}) %all-to-all-start) | async-done | bytes 3145760 | tf_op jit(solution)/shard_map/all_to_all | solution.py:169
  262.7 27.3 %all-to-all-done.3 = bf16[8,2,4,32,768]{4,3,1,2,0:T(8,128)(2,1)} async-done(((bf16[8,2,4,32,768]{4,3,1,2,0:T(8,128)(2,1)}), bf16[8,2,4,32,768]{4,3,1,2,0:T(8,128)(2,1)}, u32[]{:S(2)}, u32[]{:S(2)}) %all-to-all-start.3) | async-done | bytes 3145760 | tf_op jit(solution)/shard_map/all_to_all | solution.py:169
  329.0 19.6 %all-to-all-done.4 = bf16[8,2,128,768]{2,3,1,0:T(8,128)(2,1)} async-done(((bf16[8,2,128,768]{2,3,1,0:T(8,128)(2,1)}), bf16[8,2,128,768]{2,3,1,0:T(8,128)(2,1)}, u32[]{:S(2)}, u32[]{:S(2)}) %all-to-all-start.4) | async-done | bytes 3145760 | tf_op jit(solution)/shard_map/all_to_all | solution.py:169
  377.3 13.7 %all-to-all-done.1 = bf16[8,2,128,768]{3,2,1,0:T(8,128)(2,1)} async-done(((bf16[8,2,128,768]{3,2,1,0:T(8,128)(2,1)}), bf16[8,2,128,768]{3,2,1,0:T(8,128)(2,1)}, u32[]{:S(2)}, u32[]{:S(2)}) %all-to-all-start.1) | async-done | bytes 3145760 | tf_op jit(solution)/shard_map/all_to_all | solution.py:169
  419.4 8.3 collective-permute-done.7
  460.6 17.6 %multiply_reduce_fusion.1 = f32[4,128,768]{2,1,0:T(8,128)S(1)} fusion(f32[4,128,2,768]{3,2,1,0:T(2,128)} %reshape.500, f32[4,128,2]{2,1,0:T(8,128)S(1)} %copy.340), kind=kLoop, calls=%fused_computation.57 | loop fusion | flops 1179648 | bytes 4722688 | tf_op jit(solution)/shard_map/reduce_sum | solution.py:1123
  555.5 15.0 %reduce-scatter.21.cloned.1.call-done = bf16[128,1536]{1,0:T(8,128)(2,1)} async-done(((bf16[1024,1536]{1,0:T(8,128)(2,1)}), bf16[128,1536]{1,0:T(8,128)(2,1)}) %reduce-scatter.21.cloned.1.call-update) | async-done | bytes 393232
  576.7 39.4 %pmax.7 = f32[2,12]{1,0:T(2,128)S(1)} all-reduce(f32[2,12]{1,0:T(2,128)S(1)} %reshape_squeeze.35), channel_id=1, replica_groups=mesh['expert'=8,'shard'=4] {'expert','shard'}, use_global_device_ids=true, to_apply=%region_34.35 | all-reduce | flops 24 | bytes 192 | tf_op jit(solution)/shard_map/pmax | solution.py:1180
  618.5 10.2 %reduce-scatter.13.cloned.1.call-done = bf16[96,3072]{1,0:T(8,128)(2,1)} async-done(((bf16[768,3072]{1,0:T(8,128)(2,1)}), bf16[96,3072]{1,0:T(8,128)(2,1)}) %reduce-scatter.13.cloned.1.call-update) | async-done | bytes 589840 | tf_op jit(solution)/shard_map/reduce_scatter | solution.py:90
  637.5 8.4 collective-permute-done.16
  647.6 7.6 fusion.41
  658.8 28.2 %reduce-scatter.15.cloned.1.call-done = bf16[96,3072]{1,0:T(8,128)(2,1)} async-done(((bf16[768,3072]{1,0:T(8,128)(2,1)}), bf16[96,3072]{1,0:T(8,128)(2,1)}) %reduce-scatter.15.cloned.1.call-update) | async-done | bytes 589840 | tf_op jit(solution)/shard_map/reduce_scatter | solution.py:90
  702.6 27.4 %collective-permute-done.19 = bf16[24,3072]{1,0:T(8,128)(2,1)S(1)} collective-permute-done((bf16[24,3072]{1,0:T(8,128)(2,1)S(1)}, bf16[24,3072]{1,0:T(8,128)(2,1)S(1)}, u32[]{:S(2)}, u32[]{:S(2)}) %collective-permute-start.19) | collective-permute-done | bytes 147488 | tf_op jit(solution)/shard_map/ppermute | solution.py:45
  733.9 8.8 collective-permute-done.25
  748.5 15.8 %collective-permute-start.23 = (bf16[96,768]{1,0:T(8,128)(2,1)S(1)}, bf16[96,768]{1,0:T(8,128)(2,1)S(1)}, u32[]{:S(2)}, u32[]{:S(2)}) collective-permute-start(bf16[96,768]{1,0:T(8,128)(2,1)S(1)} %get-tuple-element.170), channel_id=1, source_target_pairs={{0,3},{1,0},{2,1},{3,2},{4,7},{5,4},{6,5},{7,6},{8,11},{9,8},{10,9... | collective-permute-start | bytes 442376 | tf_op jit(solution)/shard_map/ppermute | solution.py:45
  765.0 7.0 fusion.58
  785.2 16.6 %reduce-scatter.11.cloned.1.call-done = bf16[96,3072]{1,0:T(8,128)(2,1)} async-done(((bf16[768,3072]{1,0:T(8,128)(2,1)}), bf16[96,3072]{1,0:T(8,128)(2,1)}) %reduce-scatter.11.cloned.1.call-update) | async-done | bytes 589840 | tf_op jit(solution)/shard_map/reduce_scatter | solution.py:90
  811.1 7.8 collective-permute-done.13
  829.0 22.6 %psum.7 = f32[4032]{0:T(1024)S(1)} all-reduce(f32[4032]{0:T(1024)S(1)} %add_add_fusion.4), channel_id=1, replica_groups=mesh['expert'=8,'shard'=4] {'expert'}, use_global_device_ids=true, to_apply=%region_29.30 | all-reduce | flops 4032 | bytes 32256 | tf_op jit(solution)/shard_map/psum | solution.py:1176
  859.0 21.3 %all-gather.11.cloned.1.call-done = bf16[768,768]{1,0:T(8,128)(2,1)} async-done(((bf16[96,768]{1,0:T(8,128)(2,1)}), bf16[768,768]{1,0:T(8,128)(2,1)}) %all-gather.11.cloned.1.call-update) | async-done | bytes 1179664 | tf_op jit(solution)/shard_map/all_gather | solution.py:93
  884.6 22.2 %all-gather.5.cloned.1.call-done = bf16[192,3072]{1,0:T(8,128)(2,1)} async-done(((bf16[24,3072]{1,0:T(8,128)(2,1)}), bf16[192,3072]{1,0:T(8,128)(2,1)}) %all-gather.5.cloned.1.call-update) | async-done | bytes 1179664 | tf_op jit(solution)/shard_map/all_gather | solution.py:93
  (426 shorter events, 353.8 us)
Async XLA Ops:
  205.2 42.4 %all-to-all-start = ((bf16[8,2,4,32,768]{4,3,1,2,0:T(8,128)(2,1)}), bf16[8,2,4,32,768]{4,3,1,2,0:T(8,128)(2,1)}, u32[]{:S(2)}, u32[]{:S(2)}) async-start(bf16[8,2,4,32,768]{4,3,1,2,0:T(8,128)(2,1)} %bitcast.439), calls=%async_computation | async-start | bytes 6291456 | tf_op jit(solution)/shard_map/all_to_all | solution.py:169
  247.6 42.4 %all-to-all-start.3 = ((bf16[8,2,4,32,768]{4,3,1,2,0:T(8,128)(2,1)}), bf16[8,2,4,32,768]{4,3,1,2,0:T(8,128)(2,1)}, u32[]{:S(2)}, u32[]{:S(2)}) async-start(bf16[8,2,4,32,768]{4,3,1,2,0:T(8,128)(2,1)} %bitcast.438), calls=%async_computation.3 | async-start | bytes 6291456 | tf_op jit(solution)/shard_map/all_to_all | solution.py:169
  305.8 42.8 %all-to-all-start.4 = ((bf16[8,2,128,768]{2,3,1,0:T(8,128)(2,1)}), bf16[8,2,128,768]{2,3,1,0:T(8,128)(2,1)}, u32[]{:S(2)}, u32[]{:S(2)}) async-start(bf16[8,2,128,768]{2,3,1,0:T(8,128)(2,1)} %copy.369), calls=%async_computation.4 | async-start | bytes 6291456 | tf_op jit(solution)/shard_map/all_to_all | solution.py:169
  348.6 42.3 %all-to-all-start.1 = ((bf16[8,2,128,768]{3,2,1,0:T(8,128)(2,1)}), bf16[8,2,128,768]{3,2,1,0:T(8,128)(2,1)}, u32[]{:S(2)}, u32[]{:S(2)}) async-start(bf16[8,2,128,768]{3,2,1,0:T(8,128)(2,1)} %copy.351), calls=%async_computation.1 | async-start | bytes 6291456 | tf_op jit(solution)/shard_map/all_to_all | solution.py:169
  353.1 140.4 %reduce-scatter.19.cloned.1.call-start = ((), (), s32[]{:S(2)}) async-start(), calls=%async_computation.19 | async-start | bytes 3538944
  399.0 14.9 %collective-permute-start.5 = (f32[128,2]{0,1:T(2,128)S(1)}, f32[128,2]{0,1:T(2,128)S(1)}, u32[]{:S(2)}, u32[]{:S(2)}) collective-permute-start(f32[128,2]{0,1:T(2,128)S(1)} %bitcast.514), channel_id=1, source_target_pairs={{0,3},{1,0},{2,1},{3,2},{4,7},{5,4},{6,5},{7,6},{8,11},{9,8},{10,9... | collective-permute-start | bytes 3080 | tf_op jit(solution)/shard_map/ppermute | solution.py:45
  446.7 123.8 %reduce-scatter.21.cloned.1.call-start = ((), (), s32[]{:S(2)}) async-start(), calls=%async_computation.20 | async-start | bytes 3538944
  480.2 25.2 %collective-permute-start.2 = (bf16[128,768]{1,0:T(8,128)(2,1)}, bf16[128,768]{1,0:T(8,128)(2,1)}, u32[]{:S(2)}, u32[]{:S(2)}) collective-permute-start(bf16[128,768]{1,0:T(8,128)(2,1)} %get-tuple-element.165), channel_id=1, source_target_pairs={{0,3},{1,0},{2,1},{3,2},{4,7},{5,4},{6,5},{7,6},{8,11},{9,8},{10,9... | collective-permute-start | bytes 589832 | tf_op jit(solution)/shard_map/ppermute | solution.py:45
  480.2 25.2 %collective-permute-start.1 = (bf16[128,768]{1,0:T(8,128)(2,1)}, bf16[128,768]{1,0:T(8,128)(2,1)}, u32[]{:S(2)}, u32[]{:S(2)}) collective-permute-start(bf16[128,768]{1,0:T(8,128)(2,1)} %get-tuple-element.166), channel_id=1, source_target_pairs={{0,2},{1,3},{2,0},{3,1},{4,6},{5,7},{6,4},{7,5},{8,10},{9,11},{10,... | collective-permute-start | bytes 589832 | tf_op jit(solution)/shard_map/ppermute | solution.py:45
  481.7 23.7 %collective-permute-start = (bf16[128,768]{1,0:T(8,128)(2,1)}, bf16[128,768]{1,0:T(8,128)(2,1)}, u32[]{:S(2)}, u32[]{:S(2)}) collective-permute-start(bf16[128,768]{1,0:T(8,128)(2,1)} %get-tuple-element.164), channel_id=1, source_target_pairs={{0,1},{1,2},{2,3},{3,0},{4,5},{5,6},{6,7},{7,4},{8,9},{9,10},{10,1... | collective-permute-start | bytes 589832 | tf_op jit(solution)/shard_map/ppermute | solution.py:45
  524.2 104.6 %reduce-scatter.13.cloned.1.call-start = ((), (), s32[]{:S(2)}) async-start(), calls=%async_computation.13 | async-start | bytes 5308416 | tf_op jit(solution)/shard_map/reduce_scatter | solution.py:90
  536.8 150.1 %reduce-scatter.15.cloned.1.call-start = ((), (), s32[]{:S(2)}) async-start(), calls=%async_computation.15 | async-start | bytes 5308416 | tf_op jit(solution)/shard_map/reduce_scatter | solution.py:90
  541.7 205.7 %reduce-scatter.17.cloned.1.call-start = ((), (), s32[]{:S(2)}) async-start(), calls=%async_computation.17 | async-start | bytes 5308416 | tf_op jit(solution)/shard_map/reduce_scatter | solution.py:90
  548.7 253.1 %reduce-scatter.11.cloned.1.call-start = ((), (), s32[]{:S(2)}) async-start(), calls=%async_computation.11 | async-start | bytes 5308416 | tf_op jit(solution)/shard_map/reduce_scatter | solution.py:90
  575.8 278.7 %all-gather.7.cloned.1.call-start = ((), (), s32[]{:S(2)}) async-start(), calls=%async_computation.14 | async-start | bytes 1327104 | tf_op jit(solution)/shard_map/all_gather | solution.py:93
  647.5 208.5 %all-gather.9.cloned.1.call-start = ((), (), s32[]{:S(2)}) async-start(), calls=%async_computation.16 | async-start | bytes 1327104 | tf_op jit(solution)/shard_map/all_gather | solution.py:93
  691.4 38.6 %collective-permute-start.19 = (bf16[24,3072]{1,0:T(8,128)(2,1)S(1)}, bf16[24,3072]{1,0:T(8,128)(2,1)S(1)}, u32[]{:S(2)}, u32[]{:S(2)}) collective-permute-start(bf16[24,3072]{1,0:T(8,128)(2,1)S(1)} %get-tuple-element.174), channel_id=1, source_target_pairs={{0,2},{1,3},{2,0},{3,1},{4,6},{5,7},{6,4},{7,5},{8,10},{9,11},{10,... | collective-permute-start | bytes 442376 | tf_op jit(solution)/shard_map/ppermute | solution.py:45
  691.4 38.6 %collective-permute-start.18 = (bf16[24,3072]{1,0:T(8,128)(2,1)S(1)}, bf16[24,3072]{1,0:T(8,128)(2,1)S(1)}, u32[]{:S(2)}, u32[]{:S(2)}) collective-permute-start(bf16[24,3072]{1,0:T(8,128)(2,1)S(1)} %get-tuple-element.172), channel_id=1, source_target_pairs={{0,1},{1,2},{2,3},{3,0},{4,5},{5,6},{6,7},{7,4},{8,9},{9,10},{10,1... | collective-permute-start | bytes 442376 | tf_op jit(solution)/shard_map/ppermute | solution.py:45
  693.8 37.9 %collective-permute-start.24 = (bf16[2,192,768]{2,1,0:T(8,128)(2,1)}, bf16[2,192,768]{2,1,0:T(8,128)(2,1)}, u32[]{:S(2)}, u32[]{:S(2)}) collective-permute-start(bf16[2,192,768]{2,1,0:T(8,128)(2,1)} %get-tuple-element.160), channel_id=1, source_target_pairs={{0,1},{1,2},{2,3},{3,0},{4,5},{5,6},{6,7},{7,4},{8,9},{9,10},{10,1... | collective-permute-start | bytes 1769480 | tf_op jit(solution)/shard_map/ppermute | solution.py:45
  696.3 46.4 %collective-permute-start.25 = (bf16[2,192,768]{2,1,0:T(8,128)(2,1)}, bf16[2,192,768]{2,1,0:T(8,128)(2,1)}, u32[]{:S(2)}, u32[]{:S(2)}) collective-permute-start(bf16[2,192,768]{2,1,0:T(8,128)(2,1)} %get-tuple-element.159), channel_id=1, source_target_pairs={{0,2},{1,3},{2,0},{3,1},{4,6},{5,7},{6,4},{7,5},{8,10},{9,11},{10,... | collective-permute-start | bytes 1769480 | tf_op jit(solution)/shard_map/ppermute | solution.py:45
  701.1 43.8 %collective-permute-start.26 = (bf16[2,192,768]{2,1,0:T(8,128)(2,1)}, bf16[2,192,768]{2,1,0:T(8,128)(2,1)S(1)}, u32[]{:S(2)}, u32[]{:S(2)}) collective-permute-start(bf16[2,192,768]{2,1,0:T(8,128)(2,1)} %get-tuple-element.158), channel_id=1, source_target_pairs={{0,3},{1,0},{2,1},{3,2},{4,7},{5,4},{6,5},{7,6},{8,11},{9,8},{10,9... | collective-permute-start | bytes 1769480 | tf_op jit(solution)/shard_map/ppermute | solution.py:45
  731.7 148.7 %all-gather.11.cloned.1.call-start = ((), (), s32[]{:S(2)}) async-start(), calls=%async_computation.18 | async-start | bytes 1327104 | tf_op jit(solution)/shard_map/all_gather | solution.py:93
  748.5 23.8 %collective-permute-start.23 = (bf16[96,768]{1,0:T(8,128)(2,1)S(1)}, bf16[96,768]{1,0:T(8,128)(2,1)S(1)}, u32[]{:S(2)}, u32[]{:S(2)}) collective-permute-start(bf16[96,768]{1,0:T(8,128)(2,1)S(1)} %get-tuple-element.170), channel_id=1, source_target_pairs={{0,3},{1,0},{2,1},{3,2},{4,7},{5,4},{6,5},{7,6},{8,11},{9,8},{10,9... | collective-permute-start | bytes 442376 | tf_op jit(solution)/shard_map/ppermute | solution.py:45
  777.8 129.0 %all-gather.5.cloned.1.call-start = ((), (), s32[]{:S(2)}) async-start(), calls=%async_computation.12 | async-start | bytes 1327104 | tf_op jit(solution)/shard_map/all_gather | solution.py:93
  (80 other events, 1090.5 us)
Sparse Core Ops, SparseCore 0:
  446.9 46.5 reduce-scatter.18
  524.3 46.2 reduce-scatter.20
  574.6 54.1 reduce-scatter.12
  633.0 53.8 reduce-scatter.14
  690.2 53.8 reduce-scatter.16
  747.9 53.8 reduce-scatter.10
  803.7 24.0 all-gather.6
  829.6 24.1 all-gather.8
  856.3 23.9 all-gather.10
  882.7 24.0 all-gather.4

commit v3 on v2

--- a/solution.py
+++ b/solution.py
@@ -961,36 +961,674 @@
     )(hidden, gains, table, qkv, out, up, down, expert_up, cotangent)
 
 
-def kernel_backward(upstream, hidden, norm_gain, qkv, projection, marks, saved):
-    normalized, queries, kv, probs, attended = saved
-    rows = hidden.shape[0]
+class Plane:
+    def __init__(self):
+        self.e, self.s = place()
+        e = self.e
+        self.core = lax.rem(e, 2)
+        self.quarter = e // 2
+        self.at_x = e + 2 - 4 * lax.rem(self.quarter, 2)
+        self.at_y = lax.rem(e + 4, 8)
+        self.at_core = e + 1 - 2 * self.core
+        self.inward = jnp.where(self.core == 0, self.at_x, self.at_y)
+        self.onward = jnp.where(self.core == 0, self.at_y, self.at_x)
+        self.diagonal = self.inward + self.onward - e
+        self.others = [lax.rem(self.s + k, 4) for k in range(1, 4)]
+        self.around = [lax.rem(e + k, 8) for k in range(1, 8)]
+        self.sent = []
+
+    def push(self, source, target, send_sem, recv_sem, device):
+        return push(self.sent, source, target, send_sem, recv_sem, device)
+
+    def arrived(self, view, recv_sem):
+        pltpu.make_async_remote_copy(
+            src_ref=view,
+            dst_ref=view,
+            send_sem=recv_sem,
+            recv_sem=recv_sem,
+            device_id=(self.at_core, self.s),
+            device_id_type=MESH,
+        ).wait_recv()
+
+
+class PlaneGather:
+    def __init__(self, plane, view, send_sems, recv_sems):
+        self.plane, self.view, self.ss, self.rs = plane, view, send_sems, recv_sems
+
+    def _push(self, who, i, target):
+        p = self.plane
+        block = self.view(who)
+        p.push(block, block, self.ss.at[i], self.rs.at[i], (target, p.s))
+
+    def first(self):
+        p = self.plane
+        self._push(p.e, 0, p.at_x)
+        self._push(p.e, 1, p.at_y)
+        self._push(p.e, 3, p.at_core)
+
+    def second(self):
+        p = self.plane
+        p.arrived(self.view(p.inward), self.rs.at[p.core])
+        self._push(p.inward, 2, p.onward)
+        self._push(p.inward, 4, p.at_core)
+
+    def third(self):
+        p = self.plane
+        p.arrived(self.view(p.onward), self.rs.at[1 - p.core])
+        self._push(p.onward, 5, p.at_core)
+        p.arrived(self.view(p.diagonal), self.rs.at[2])
+        self._push(p.diagonal, 6, p.at_core)
+
+    def done(self):
+        for i in range(3, 7):
+            self.plane.arrived(self.view(self.plane.e), self.rs.at[i])
+
+
+class SmallReduce:
+    def __init__(self, plane, value, z_in, plane_in, op, sems):
+        self.plane, self.value, self.z_in, self.plane_in = plane, value, z_in, plane_in
+        self.op, self.sems = op, sems
+
+    def start(self):
+        p = self.plane
+        zs, zr, _, _ = self.sems
+        for k in range(3):
+            p.push(self.value, self.z_in.at[k], zs.at[k], zr.at[k], (p.e, p.others[k]))
+
+    def middle(self, middle):
+        p = self.plane
+        zs, zr, ps, pr = self.sems
+        total = self.value[...]
+        for k in range(3):
+            p.arrived(self.z_in.at[k], zr.at[k])
+            total = self.op(total, self.z_in[k])
+        middle[...] = total
+        for k in range(7):
+            p.push(middle, self.plane_in.at[k], ps.at[k], pr.at[k], (p.around[k], p.s))
+
+    def finish(self, middle, result):
+        p = self.plane
+        total = middle[...]
+        for k in range(7):
+            p.arrived(self.plane_in.at[k], self.sems[3].at[k])
+            total = self.op(total, self.plane_in[k])
+        result[...] = total
+
+
+def norm_pull(inputs, gain, upstream):
+    inverse = lax.rsqrt(jnp.mean(inputs * inputs, axis=-1, keepdims=True) + epsilon)
+    scaled = upstream * gain
+    inner = jnp.mean(scaled * inputs, axis=-1, keepdims=True)
+    gain_grad = jnp.sum(upstream * inputs * inverse, axis=0, keepdims=True)
+    return inverse * scaled - inputs * (inverse * inverse * inverse * inner), gain_grad
+
+
+def gelu_slope(value):
+    root = math.sqrt(2.0 / math.pi)
+    squared = value * value
+    bend = jnp.tanh(root * value * (1.0 + 0.044715 * squared))
+    return 0.5 * (1.0 + bend) + 0.5 * value * (1.0 - bend * bend) * root * (
+        1.0 + 3 * 0.044715 * squared
+    )
+
+
+def dot_columns(left, right):
+    return lax.dot_general(left, right, (((0,), (0,)), ((), ())), preferred_element_type=single)
+
+
+def backward_kernel(
+    mid_grad_ref,
+    one_ref,
+    hidden_ref,
+    mid_ref,
+    gains_ref,
+    query_ref,
+    pre_ref,
+    marks_ref,
+    small_ref,
+    peak_ref,
+    normed_hbm,
+    attended_hbm,
+    dense_normed_hbm,
+    act_hbm,
+    qkv0_hbm,
+    qkv1_hbm,
+    proj0_hbm,
+    proj1_hbm,
+    up_hbm,
+    down_hbm,
+    kv_hbm,
+    probs_hbm,
+    up_grad_hbm,
+    hidden_grad_out,
+    att_out,
+    up_out,
+    down_out,
+    small_out,
+    late_out,
+    peak_out,
+    expert_up_out,
+    w_wide,
+    w_down,
+    kv,
+    probs,
+    xg,
+    gx,
+    gsrc,
+    zb,
+    zin,
+    zb_down,
+    zin_down,
+    slopes,
+    score_low,
+    dk,
+    cin,
+    rin,
+    attended_grad,
+    layer_grad,
+    biases,
+    early,
+    early_z,
+    early_p,
+    early_m,
+    late,
+    late_z,
+    late_p,
+    late_m,
+    peak_z,
+    peak_p,
+    peak_m,
+    gs,
+    gr,
+    xs,
+    xr,
+    zs,
+    zr,
+    dcs,
+    dcr,
+    drs,
+    drr,
+    szs,
+    szr,
+    sps,
+    spr,
+    us,
+    ur,
+    loads,
+):
+    p = Plane()
+    e, s, core = p.e, p.s, p.core
+    own_rows = row_block(e, T)
+
+    def load(source, target, i):
+        copy = pltpu.make_async_copy(source, target, loads.at[i])
+        copy.start()
+        return copy
+
+    own_parts = [
+        load(source, xg.at[n, own_rows, :], 11 + n)
+        for n, source in enumerate(
+            (
+                normed_hbm.at[1],
+                attended_hbm.at[1],
+                normed_hbm.at[0],
+                attended_hbm.at[0],
+                dense_normed_hbm,
+            )
+        )
+    ]
+    own_act = load(act_hbm.at[:, lane_block(e, 384)], gx.at[3, own_rows, :], 16)
+    greet([(d, s) for d in p.around] + [(e, other) for other in p.others])
+
+    w_qkv = w_wide.at[:, : 3 * D]
+    w_out = w_wide.at[:, 3 * D :]
+    got_out = load(proj1_hbm, w_out, 0)
+    got_kv = load(kv_hbm.at[1], kv, 2)
+    got_probs = load(probs_hbm.at[1], probs, 3)
+    got_qkv = load(qkv1_hbm, w_qkv, 1)
+    got_down = load(down_hbm, w_down, 5)
+
+    peaks = SmallReduce(
+        p, peak_ref, peak_z, peak_p, jnp.maximum, (szs.at[0], szr.at[0], sps.at[0], spr.at[0])
+    )
+    peaks.start()
+
+    def rows_gather(n):
+        return PlaneGather(
+            p, lambda who: xg.at[n, row_block(who, T), :], gs.at[n], gr.at[n]
+        )
+
+    gathers = [rows_gather(n) for n in range(6)]
+    for copy in own_parts:
+        copy.wait()
+    gathers[0].first()
+    gathers[1].first()
+
+    exchanges = {}
+
+    def exchange_start(j, source):
+        if j == 3:
+            own_act.wait()
+        else:
+            gx[j, own_rows, :] = source[:, lane_block(e, 384)]
+        for k, d in enumerate(p.around):
+            p.push(
+                source.at[:, lane_block(d, 384)],
+                gx.at[j, own_rows, :],
+                xs.at[j, k],
+                xr.at[j, k],
+                (d, s),
+            )
+
+    def exchange_wait(j):
+        for k in range(7):
+            p.arrived(gx.at[j, own_rows, :], xr.at[j, k])
+
+    def out_gather(j, target, height):
+        return PlaneGather(
+            p, lambda who: target.at[pl.ds(who, 1)], gs.at[6 + j], gr.at[6 + j]
+        )
+
+    def z_start(j, tile, received, height):
+        for k in range(3):
+            p.push(
+                tile.at[row_block(p.others[k], height), :],
+                received.at[k],
+                zs.at[j, k],
+                zr.at[j, k],
+                (e, p.others[k]),
+            )
+
+    def z_finish(j, tile, received, height, target):
+        total = tile[row_block(s, height), :].astype(single)
+        for k in range(3):
+            p.arrived(received.at[k], zr.at[j, k])
+            total = total + received[k].astype(single)
+        target[pl.ds(e, 1)] = total.astype(bfloat)[None]
+
+    def tile_attention(layer):
+        j = 1 - layer
+        exchange_wait(j)
+        rows = xg[2 * j + e // 6]
+        for part in range(3):
+            lanes = slice(128 * part, 128 * (part + 1))
+            zb[j, :, lanes] = dot_columns(rows, gx[j, :, lanes]).astype(bfloat)
+        z_start(j, zb.at[j], zin.at[j], 192)
+
+    def tile_up():
+        exchange_wait(2)
+        for part in range(3):
+            lanes = slice(128 * part, 128 * (part + 1))
+            zb[2, :, lanes] = dot_columns(xg[4], gx[2, :, lanes]).astype(bfloat)
+        z_start(2, zb.at[2], zin.at[2], 192)
+
+    def tile_down():
+        exchange_wait(3)
+        for part in range(3):
+            lanes = slice(128 * part, 128 * (part + 1))
+            zb_down[lanes, :] = dot_columns(gx[3, :, lanes], xg[5]).astype(bfloat)
+        z_start(3, zb_down, zin_down, 96)
+
+    gather_att1 = out_gather(0, att_out.at[1], 192)
+    gather_att0 = out_gather(1, att_out.at[0], 192)
+    gather_up = out_gather(2, up_out, 192)
+    gather_down = out_gather(3, down_out, 96)
+
     scale = 1.0 / math.sqrt(HD)
-    branch_grad = upstream.astype(bfloat)
-    projection_grad = matmul(spread(attended).T, branch_grad)
-    attended_grad = matmul(branch_grad, projection.T).astype(bfloat)
-    queries = queries.reshape(rows, H, HD)
-    keys = kv[:, :, :256].transpose(1, 0, 2).reshape(-1, H, HD)
-    values = kv[:, :, 256:].transpose(1, 0, 2).reshape(-1, H, HD)
-    grad_heads = attended_grad.reshape(rows, H, HD)
-    probs_low = probs.reshape(H, rows, -1)
-    probs = probs_low.astype(single)
-    prob_grad = jnp.einsum("ihd,jhd->hij", grad_heads, values, preferred_element_type=single)
-    row_dot = jnp.sum(prob_grad * probs, axis=-1)
-    score_grad = (probs * (prob_grad - row_dot[..., None])).astype(bfloat)
-    query_grad = jnp.einsum("hij,jhd->ihd", score_grad, keys, preferred_element_type=single) * scale
-    query_grad = query_grad.astype(bfloat).reshape(rows, D)
-    bias_grad = jnp.einsum("hij,bij->bh", score_grad, marks, preferred_element_type=single)
-    key_grad = (
-        jnp.einsum("hij,ihd->jhd", score_grad, queries, preferred_element_type=single) * scale
-    )
-    value_grad = jnp.einsum("hij,ihd->jhd", probs_low, grad_heads, preferred_element_type=single)
-    pair = jnp.concatenate([key_grad.reshape(-1, D), value_grad.reshape(-1, D)], axis=-1)
-    pair_grad = lax.psum_scatter(pair.astype(bfloat), "expert", scatter_dimension=0, tiled=True)
-    packed_grad = jnp.concatenate([query_grad, pair_grad], axis=-1)
-    qkv_grad = matmul(spread(normalized).T, packed_grad)
-    normed_grad = matmul(packed_grad, qkv.T)
-    input_grad, gain_grad = norm_back(hidden, norm_gain, normed_grad)
-    return upstream + input_grad, gain_grad, qkv_grad, projection_grad, bias_grad
+
+    def attention(layer, upstream, work):
+        j = 1 - layer
+        grads = gsrc.at[j]
+        branch = upstream.astype(bfloat)
+        grads[:, 3 * D :] = branch
+        got_out_now = got_out if layer == 1 else reloads["out"]
+        got_out_now.wait()
+        attended_grad[...] = dot_rows(branch, w_out[...]).astype(bfloat)
+        if layer == 1:
+            got_kv.wait()
+            got_probs.wait()
+        else:
+            reloads["kv"].wait()
+            reloads["probs"].wait()
+            for copy in dk_sent:
+                copy.wait_send()
+            dk_sent.clear()
+
+        def first_step(part):
+            push(
+                dk_sent,
+                dk.at[part, 1 - core],
+                cin.at[layer, part],
+                dcs.at[layer, part],
+                dcr.at[layer, part],
+                (p.at_core, s),
+            )
+
+        def second_step(part):
+            p.arrived(cin.at[layer, part], dcr.at[layer, part])
+            for q in range(4):
+                dk[part, core, q] = (
+                    dk[part, core, q].astype(single) + cin[layer, part, q].astype(single)
+                ).astype(bfloat)
+            for k, d in enumerate((p.at_x, p.at_y, p.diagonal)):
+                push(
+                    dk_sent,
+                    dk.at[part, core, d // 2],
+                    rin.at[layer, part, k],
+                    drs.at[layer, part, k],
+                    drr.at[layer, part, k],
+                    (d, s),
+                )
+
+        def third_step(part):
+            total = dk[part, core, p.quarter].astype(single)
+            for k in range(3):
+                p.arrived(rin.at[layer, part, k], drr.at[layer, part, k])
+                total = total + rin[layer, part, k].astype(single)
+            turned = total.T.astype(bfloat)
+            grads[:, D + 256 * part : D + 256 * (part + 1)] = turned[:, :256]
+            grads[:, 2 * D + 256 * part : 2 * D + 256 * (part + 1)] = turned[:, 256:]
+
+        for part in range(3):
+
+            def one_pair(local_pair):
+                pair = 2 * part + local_pair
+                lanes = lane_block(pair, 128)
+                lane = lax.broadcasted_iota(jnp.int32, (T, 128), 1)
+
+                def split(value):
+                    zero = jnp.zeros_like(value)
+                    return jnp.concatenate(
+                        [jnp.where(lane < HD, value, zero), jnp.where(lane >= HD, value, zero)]
+                    )
+
+                queries = split(query_ref[layer, :, lanes])
+                outputs = split(attended_grad[:, lanes])
+                keys = kv[part, :, lane_block(local_pair, 128)]
+                values = kv[part, :, pl.ds(pl.multiple_of(256 + local_pair * 128, 128), 128)]
+                slopes[...] = dot_rows(outputs, values)
+                pair_rows = pl.ds(pl.multiple_of(pair * 2 * T, 2 * T), 2 * T)
+                for half in range(2):
+                    head = 2 * pair + half
+                    gathered = jnp.zeros((8, TOE), single)
+                    for rows in range(0, T, 32):
+                        at = half * T + rows
+                        prob = probs[
+                            pl.ds(pl.multiple_of(head * T + rows, 32), 32), :
+                        ].astype(single)
+                        slope = slopes[at : at + 32, :]
+                        inner = jnp.sum(prob * slope, axis=-1, keepdims=True)
+                        low = (prob * (slope - inner)).astype(bfloat)
+                        score_low[at : at + 32, :] = low
+                        fold = jnp.concatenate(
+                            [low.astype(single), jnp.zeros((32, TOE - low.shape[1]), single)],
+                            axis=1,
+                        )
+                        fold = pltpu.roll(fold[:16], 16, 1) + fold[16:]
+                        fold = pltpu.roll(fold[:8], 8, 1) + fold[8:]
+                        if rows < T - 32:
+                            fold = pltpu.roll(fold, T - 32 - rows, 1)
+                        gathered = gathered + fold
+                    fold = pltpu.roll(gathered[:4], 4, 1) + gathered[4:]
+                    fold = pltpu.roll(fold[:2], 2, 1) + fold[2:]
+                    fold = pltpu.roll(fold[:1], 1, 1) + fold[1:]
+                    biases[pl.ds(layer * H + head, 1), :] = fold
+                mixed = jnp.dot(score_low[...], keys, preferred_element_type=single) * scale
+                grads[:, lanes] = jnp.where(lane < HD, mixed[:T], mixed[T:]).astype(bfloat)
+                key_grad = dot_columns(queries, score_low[...]) * scale
+                value_grad = dot_columns(outputs, probs[pair_rows, :])
+                for d in range(8):
+                    columns = slice(128 * d, 128 * (d + 1))
+                    dk[
+                        part, d % 2, d // 2, pl.ds(pl.multiple_of(local_pair * 128, 128), 128), :
+                    ] = key_grad[:, columns].astype(bfloat)
+                    dk[
+                        part,
+                        d % 2,
+                        d // 2,
+                        pl.ds(pl.multiple_of(256 + local_pair * 128, 128), 128),
+                        :,
+                    ] = value_grad[:, columns].astype(bfloat)
+
+            loop(2, one_pair)
+            first_step(part)
+            if part > 0:
+                second_step(part - 1)
+            work[part]()
+        second_step(2)
+        third_step(0)
+        work[3]()
+        third_step(1)
+        third_step(2)
+        exchange_start(j, gsrc.at[j])
+        if layer == 1:
+            got_qkv.wait()
+        else:
+            reloads["qkv"].wait()
+        return dot_rows(gsrc[j, :, : 3 * D], w_qkv[...])
+
+    dk_sent = []
+    reloads = {}
+
+    def part0():
+        gathers[0].second()
+        gathers[1].second()
+        exchange_start(3, act_hbm)
+        gathers[4].first()
+        for k in range(3):
+            reshard.append(
+                p.push(
+                    up_grad_hbm.at[:, row_block(p.others[k], 192), :],
+                    expert_up_out.at[:, :, lane_block(s, 768)],
+                    us.at[k],
+                    ur.at[k],
+                    (e, p.others[k]),
+                )
+            )
+        reshard_own.append(
+            load(
+                up_grad_hbm.at[:, row_block(s, 192), :],
+                expert_up_out.at[:, :, lane_block(s, 768)],
+                6,
+            )
+        )
+
+    def part1():
+        gathers[0].third()
+        gathers[1].third()
+        peaks.middle(peak_m)
+
+    def part2():
+        gathers[4].second()
+        gathers[2].first()
+        gathers[3].first()
+
+    def part3():
+        gathers[4].third()
+        peaks.finish(peak_m, peak_out)
+
+    reshard, reshard_own = [], []
+    mid_grad = mid_grad_ref[...]
+    normed_grad = attention(1, mid_grad, [part0, part1, part2, part3])
+    reloads["kv"] = load(kv_hbm.at[0], kv, 7)
+    reloads["probs"] = load(probs_hbm.at[0], probs, 8)
+    got_up = load(up_hbm, w_wide, 4)
+    input_grad, gain_grad = norm_pull(one_ref[...], gains_ref[1:2, :], normed_grad)
+    early[...] = small_ref[...]
+    early[17:18, :] = gain_grad
+    layer_grad[...] = mid_grad + input_grad
+    branch = layer_grad[...].astype(bfloat)
+    xg[5, own_rows, :] = branch
+    gathers[5].first()
+    got_down.wait()
+
+    def slope_part(i):
+        lanes = lane_block(i, 512)
+        act_grad = dot_rows(xg[5, own_rows, :], w_down[row_block(i, 512), :])
+        gsrc[2, :, lanes] = (act_grad * gelu_slope(pre_ref[:, lanes])).astype(bfloat)
+
+    loop(6, slope_part)
+    exchange_start(2, gsrc.at[2])
+    gathers[2].second()
+    gathers[3].second()
+    gathers[5].second()
+    got_up.wait()
+    dense_grad = dot_rows(gsrc[2], w_wide[...])
+    reloads["out"] = load(proj0_hbm, w_out, 9)
+    reloads["qkv"] = load(qkv0_hbm, w_qkv, 10)
+    input_grad, gain_grad = norm_pull(mid_ref[...], gains_ref[2:3, :], dense_grad)
+    early[18:19, :] = gain_grad
+    layer_grad[...] = layer_grad[...] + input_grad
+    small = SmallReduce(
+        p, early, early_z, early_p, jnp.add, (szs.at[1], szr.at[1], sps.at[1], spr.at[1])
+    )
+    small.start()
+    gathers[0].done()
+    gathers[1].done()
+    tile_attention(1)
+
+    def part4():
+        gathers[5].third()
+        gathers[2].third()
+        gathers[3].third()
+        gathers[4].done()
+        tile_up()
+
+    def part5():
+        gathers[5].done()
+        tile_down()
+        z_finish(0, zb.at[0], zin.at[0], 192, att_out.at[1])
+        gather_att1.first()
+        small.middle(early_m)
+
+    def part6():
+        z_finish(2, zb.at[2], zin.at[2], 192, up_out)
+        gather_up.first()
+        gather_att1.second()
+
+    def part7():
+        z_finish(3, zb_down, zin_down, 96, down_out)
+        gather_down.first()
+        gather_up.second()
+        gather_att1.third()
+
+    normed_grad = attention(0, layer_grad[...], [part4, part5, part6, part7])
+    input_grad, gain_grad = norm_pull(
+        hidden_ref[...].astype(single), gains_ref[0:1, :], normed_grad
+    )
+    hidden_grad_out[...] = layer_grad[...] + input_grad
+    late[...] = jnp.zeros_like(late)
+    for i in range(6):
+        late[i : i + 1, :] = gain_grad[:, 128 * i : 128 * (i + 1)]
+    late[8:32, :NB] = lax.dot_general(
+        biases[...],
+        marks_ref[...].astype(single),
+        (((1,), (1,)), ((), ())),
+        precision=lax.Precision.HIGHEST,
+        preferred_element_type=single,
+    )
+    tail = SmallReduce(
+        p, late, late_z, late_p, jnp.add, (szs.at[2], szr.at[2], sps.at[2], spr.at[2])
+    )
+    tail.start()
+    gathers[2].done()
+    gathers[3].done()
+    tile_attention(0)
+    gather_down.second()
+    gather_up.third()
+    small.finish(early_m, small_out)
+    gather_down.third()
+    tail.middle(late_m)
+    z_finish(1, zb.at[1], zin.at[1], 192, att_out.at[0])
+    gather_att0.first()
+    gather_att1.done()
+    gather_up.done()
+    gather_down.done()
+    gather_att0.second()
+    gather_att0.third()
+    tail.finish(late_m, late_out)
+    for copy in reshard:
+        copy.wait_recv()
+    reshard_own[0].wait()
+    gather_att0.done()
+    for copy in p.sent + dk_sent:
+        copy.wait_send()
+
+
+def backward(
+    mid_grad, layer_one, hidden, mid, gains, normed, queries, attended, dense_normed, act, pre_act,
+    marks, small, peak_rows, weights, kv, probs, up_grad,
+):
+    length = T * lax.axis_size("expert")
+    vmem = pl.BlockSpec(memory_space=VMEM)
+    anywhere = pl.BlockSpec(memory_space=ANY)
+    shape = jax.ShapeDtypeStruct
+    ff = pre_act.shape[1]
+    sem = pltpu.SemaphoreType.DMA
+    peak_shape, early_shape, late_shape = (2 * H, 128), small.shape, (32, 128)
+    return pl.pallas_call(
+        backward_kernel,
+        name="backward_layers",
+        out_shape=(
+            shape((T, D), single),
+            shape((2, 8, 192, 384), bfloat),
+            shape((8, 192, 384), bfloat),
+            shape((8, 96, D), bfloat),
+            shape(early_shape, single),
+            shape(late_shape, single),
+            shape(peak_shape, single),
+            shape((EXP_DEV, 192, ff), bfloat),
+        ),
+        in_specs=[vmem] * 10 + [anywhere] * 13,
+        out_specs=(vmem,) * 7 + (anywhere,),
+        scratch_shapes=[
+            VMEM((D, ff), bfloat),
+            VMEM((ff, D), bfloat),
+            VMEM((3, length, 512), bfloat),
+            VMEM((H * T, length), bfloat),
+            VMEM((6, length, D), bfloat),
+            VMEM((4, length, 384), bfloat),
+            VMEM((3, T, 4 * D), bfloat),
+            VMEM((3, D, 384), bfloat),
+            VMEM((3, 3, 192, 384), bfloat),
+            VMEM((384, D), bfloat),
+            VMEM((3, 96, D), bfloat),
+            VMEM((2 * T, length), single),
+            VMEM((2 * T, length), bfloat),
+            VMEM((3, 2, 4, 512, 128), bfloat),
+            VMEM((2, 3, 4, 512, 128), bfloat),
+            VMEM((2, 3, 3, 512, 128), bfloat),
+            VMEM((T, D), bfloat),
+            VMEM((T, D), single),
+            VMEM((2 * H, TOE), single),
+            VMEM(early_shape, single),
+            VMEM((3,) + early_shape, single),
+            VMEM((7,) + early_shape, single),
+            VMEM(early_shape, single),
+            VMEM(late_shape, single),
+            VMEM((3,) + late_shape, single),
+            VMEM((7,) + late_shape, single),
+            VMEM(late_shape, single),
+            VMEM((3,) + peak_shape, single),
+            VMEM((7,) + peak_shape, single),
+            VMEM(peak_shape, single),
+            sem((10, 7)), sem((10, 7)),
+            sem((4, 7)), sem((4, 7)),
+            sem((4, 3)), sem((4, 3)),
+            sem((2, 3)), sem((2, 3)),
+            sem((2, 3, 3)), sem((2, 3, 3)),
+            sem((3, 3)), sem((3, 3)),
+            sem((3, 7)), sem((3, 7)),
+            sem((3,)), sem((3,)),
+            sem((17,)),
+        ],
+        compiler_params=pltpu.CompilerParams(
+            collective_id=3, has_side_effects=True, vmem_limit_bytes=60 * 2**20
+        ),
+    )(
+        mid_grad, layer_one, hidden, mid, gains, queries, pre_act, marks, small, peak_rows, normed,
+        attended, dense_normed, act, *weights, kv, probs, up_grad,
+    )
 
 
 def shards(
@@ -1030,7 +1668,7 @@
     cuts = [0, 4 * part, 4 * part + 2 * (NB // groups) * H, used]
     gains, bias_weights, router_full = (small[:, cuts[i] : cuts[i + 1]] for i in range(3))
     gains = gains.reshape(groups, 4, part).transpose(1, 0, 2).reshape(4, D)
-    gain_attn, gain_mlp = gains[:2], gains[2:]
+    gain_mlp = gains[2:]
     bias_weights = (
         bias_weights.reshape(groups, 2, NB // groups, H).transpose(1, 0, 2, 3).reshape(2, NB, H)
     )
@@ -1051,17 +1689,8 @@
         hidden_in.reshape(block_rows, D), gains, table, qkv_weight, out_weight, mlp_up, mlp_down,
         expert_up, out_grad.reshape(block_rows, D),
     )
-    mid_first, mid_second = mid[0], mid[1]
-    hidden_zero = hidden_in.reshape(block_rows, D).astype(single)
+    mid_second = mid[1]
     moe_normed = lax.dynamic_index_in_dim(normed_all, here, 0, keepdims=False)
-    own_positions = lax.axis_index("expert") * block_rows + jnp.arange(block_rows, dtype=jnp.int32)
-    distance = own_positions[:, None] - jnp.arange(length, dtype=jnp.int32)[None, :]
-    bounds = jnp.sum(
-        (bucket_table[:, None] < jnp.arange(NB + 1, dtype=jnp.int32)[None, :]).astype(jnp.int32),
-        axis=0,
-    )
-    attention_marks = bucket_marks(distance, bounds[:NB], bounds[1:])
-
     expert_ids = jnp.arange(expert_total, dtype=jnp.int32)
     flat_routes = route_rows.reshape(groups, -1)
     marks = (flat_routes[:, :, None] == expert_ids).astype(jnp.int32)
@@ -1134,63 +1763,43 @@
     moe_input_grad, moe_gain_grad = norm_back(mid_second, gain_mlp[1], normed_grad)
     mid_grad = upstream + moe_input_grad
 
-    up_grad = up_grad.reshape(EXP_DEV, groups, part, width)
-    expert_up_grad = jnp.zeros((EXP_DEV, part, groups * width), single)
-    for step in range(groups):
-        piece = lax.dynamic_index_in_dim(up_grad, (here + step) % groups, 1, keepdims=False)
-        if step:
-            piece = shard_shift(piece, step)
-        expert_up_grad = lax.dynamic_update_slice_in_dim(
-            expert_up_grad, piece.astype(single), ((here - step) % groups) * width, 2
+    small_in = jnp.concatenate(
+        [router_grad.T, moe_gain_grad[None], jnp.zeros((24 - expert_total - 1, D), single)]
+    )
+    hidden_grad, attention_sum, up_sum, down_sum, small_sum, late_sum, peaks, expert_up_low = (
+        backward(
+            mid_grad, layer_one, hidden_in.reshape(block_rows, D), mid[0], gains, normed, queries,
+            attended, dense_normed, spread(activation), pre_act, toeplitz_marks, small_in,
+            peak_rows, (qkv0, qkv1, projection0, projection1, dense_up, dense_down), kv, probs,
+            up_grad,
         )
-
-    layer_grad, gain_second, qkv_second, projection_second, bias_second = kernel_backward(
-        mid_grad, layer_one, gain_attn[1], qkv1, projection1, attention_marks,
-        (normed[1], queries[1], kv[1], probs[1], attended[1]),
-    )
-    second_grad = reduce_weight(jnp.concatenate([qkv_second, projection_second], axis=1))
-    dense_branch = layer_grad.astype(bfloat)
-    mlp_down_grad = reduce_weight(matmul(spread(activation).T, dense_branch))
-    hidden_act_grad = matmul(dense_branch, dense_down.T)
-    pre_act_grad = gelu_back(pre_act, hidden_act_grad).astype(bfloat)
-    mlp_up_grad = reduce_weight(matmul(spread(dense_normed).T, pre_act_grad))
-    dense_normed_grad = matmul(pre_act_grad, dense_up.T)
-    dense_input_grad, dense_gain_grad = norm_back(mid_first, gain_mlp[0], dense_normed_grad)
-    first_grad = layer_grad + dense_input_grad
-    input_grad, gain_first, qkv_first, projection_first, bias_first = kernel_backward(
-        first_grad, hidden_zero, gain_attn[0], qkv0, projection0, attention_marks,
-        (normed[0], queries[0], kv[0], probs[0], attended[0]),
-    )
-    first_weight_grad = reduce_weight(jnp.concatenate([qkv_first, projection_first], axis=1))
-
-    gains = jnp.stack([gain_first, gain_second, dense_gain_grad, moe_gain_grad])
-    biases = jnp.stack([bias_first, bias_second])
-    small_grad = jnp.concatenate(
-        [
-            gains.reshape(4, groups, part).transpose(1, 0, 2).reshape(groups, -1),
-            biases.reshape(2, groups, NB // groups, H).transpose(1, 0, 2, 3).reshape(groups, -1),
-            router_grad.reshape(groups, -1),
-        ],
-        axis=1,
-    )
-    small_grad = lax.psum(scatter_shard(small_grad, single), "expert")
-    gain_cut = 4 * part
-    bias_cut = gain_cut + 2 * (NB // groups) * H
-    own_gains = small_grad[:gain_cut].reshape(4, part)
-    peaks = lax.pmax(peak_rows[:, 0].reshape(2, H), ("expert", "shard"))
-    clip_scales = jnp.sqrt(clip_limit / jnp.maximum(peaks, clip_limit))
+    )
+    attention_sum = (
+        attention_sum.transpose(0, 2, 1, 3).reshape(2, part, 4 * D).astype(single)
+    )
+    mlp_up_grad = up_sum.transpose(1, 0, 2).reshape(part, -1).astype(single)
+    mlp_down_grad = down_sum.reshape(-1, D).astype(single)
+
+    def columns(rows):
+        return lax.dynamic_slice_in_dim(rows, here * part, part, rows.ndim - 1)
+
+    first_gain = late_sum[:6].reshape(1, D)
+    rows = columns(small_sum)
+    gain_rows = columns(first_gain)
+    biases = lax.dynamic_slice_in_dim(late_sum[8:32], here * (NB // groups), NB // groups, 1)
+    clip_scales = jnp.sqrt(clip_limit / jnp.maximum(peaks[:, 0].reshape(2, H), clip_limit))
     return (
         hidden_out,
-        input_grad.reshape(hidden_in.shape),
-        own_gains[:2],
-        jnp.stack([first_weight_grad[:, : 3 * D], second_grad[:, : 3 * D]]),
-        jnp.stack([first_weight_grad[:, 3 * D :], second_grad[:, 3 * D :]]),
-        small_grad[gain_cut:bias_cut].reshape(2, NB // groups, H),
-        own_gains[2:],
+        hidden_grad.reshape(hidden_in.shape),
+        jnp.concatenate([gain_rows, rows[expert_total + 1 : expert_total + 2]]),
+        attention_sum[:, :, : 3 * D],
+        attention_sum[:, :, 3 * D :],
+        biases.reshape(2, H, NB // groups).transpose(0, 2, 1),
+        jnp.stack([rows[expert_total + 2], rows[expert_total]]),
         mlp_up_grad,
         mlp_down_grad,
-        small_grad[bias_cut:].reshape(part, expert_total),
-        expert_up_grad,
+        rows[:expert_total].T,
+        expert_up_low.astype(single),
         expert_down_grad,
         clip_scales,
     )

time: 931 us -> 663 us (0.71)
  waiting for transfers between devices: 290 us -> 112 us
  Pallas kernels: 165 us -> 334 us
  blocking collectives: 62.1 us -> 0 us
  matrix products: 105 us -> 47.4 us
  local copies, waits for them, and re-layouts: 134 us -> 76.6 us
  starting transfers between devices: 82 us -> 41.3 us
  other arithmetic: 66.8 us -> 37.9 us
  between operations: 16 us -> 1.58 us
    pallas_call x0 -> x1, Pallas kernels: none -> 170 us  [backward(): pl.pallas_call(backward_kernel, name='backward_layers', out_shape=(shape(...]
    ppermute x27 -> x9, waiting for transfers between devices: 74.7 us -> 17.8 us  [shard_shift(): lax.ppermute(block, 'shard', [(i, (i + amount) % count) for i in range(co...]
    reduce_scatter x4 -> x0, waiting for transfers between devices: 55 us -> none  [reduce_weight(): lax.psum_scatter(grad.astype(bfloat), 'expert', scatter_dimension=0, tile...]
    all_gather x4 -> x0, waiting for transfers between devices: 43.5 us -> none  [reduce_weight(): return lax.all_gather(own, 'expert', axis=0, tiled=True).astype(single)]
    pmax x1 -> x0, blocking collectives: 39.4 us -> none  [shards(): peaks = lax.pmax(peak_rows[:, 0].reshape(2, H), ('expert', 'shard'))]
    ppermute x27 -> x9, starting transfers between devices: 55.5 us -> 16.9 us  [shard_shift(): lax.ppermute(block, 'shard', [(i, (i + amount) % count) for i in range(co...]
    dot_general x10 -> x0, matrix products: 32 us -> none  [the longest x2 14.1 us: kernel_backward(): jnp.einsum('hij,bij->bh', score_grad, marks, preferred_element_type=single)]
    dot_general x14 -> x2, matrix products: 30.2 us -> 2.7 us  [matmul(): return jnp.dot(left, right, preferred_element_type=single)]
  transfers between devices with their start and end apart: 42 -> 14, of which waited for: 20 -> 5; matrix products, arithmetic and copies ran while one was open for 23% -> 15% of each run, Pallas kernels for 0% -> 0%
where the time goes in v3:
time: 663 us; the launch traced here: 651 us
  Pallas kernels  334 us (50%)
  waiting for transfers between devices  112 us (17%)
  local copies, waits for them, and re-layouts  76.6 us (12%)
  matrix products  47.4 us (7%)
  starting transfers between devices  41.3 us (6%)
  other arithmetic  37.9 us (6%)
    pallas_call x1, Pallas kernels, backward(): pl.pallas_call(backward_kernel, name='backward_layers', out_shape=(shape(...  170 us
    pallas_call x1, Pallas kernels, forward(): pl.pallas_call(forward_kernel, name='forward_layers', out_shape=(shape((2...  156 us
    all_to_all x5, waiting for transfers between devices, exchange(): lax.all_to_all(blocks, 'expert', split_axis=0, concat_axis=0, tiled=True)  94 us
    all_to_all x5, starting transfers between devices, exchange(): lax.all_to_all(blocks, 'expert', split_axis=0, concat_axis=0, tiled=True)  24.4 us
    ppermute x9, waiting for transfers between devices, shard_shift(): lax.ppermute(block, 'shard', [(i, (i + amount) % count) for i in range(co...  17.8 us
    ppermute x9, starting transfers between devices, shard_shift(): lax.ppermute(block, 'shard', [(i, (i + amount) % count) for i in range(co...  16.9 us
    reduce_sum x1, other arithmetic, shards(): mixed = scatter_shard(jnp.sum(gates_all[..., None] * route_out, axis=2))  16.8 us
  transfers between devices with their start and end apart: 14, of which 5 were waited for; matrix products, arithmetic and copies ran while one was open for 15% of the time, Pallas kernels for 0%

profile of v3, /device:TPU:0, one launch (start us, length us, event | category | flops | bytes accessed | tf_op | source)
XLA Modules:
  0.0 651.0 jit_solution(8579082247889887781)
XLA Ops:
  6.2 9.1 %gather_small.1 = (f32[4,32,128]{2,1,0:T(8,128)}, s32[4,2,128]{2,1,0:T(2,128)}) custom-call(f32[32,128]{1,0:T(8,128)} %bitcast_convert_fusion.2.small_ref, s32[2,128]{1,0:T(2,128)} %reshape.271.routes_ref), custom_call_target="tpu_custom_call" | custom-call | tf_op jit(solution)/shard_map/gather_small/pallas_call | solution.py:442
  18.8 4.6 gather_fusion
  28.1 155.8 %forward_layers.1 = (bf16[2,128,768]{2,1,0:T(8,128)(2,1)}, bf16[2,128,768]{2,1,0:T(8,128)(2,1)}, bf16[2,128,768]{2,1,0:T(8,128)(2,1)}, f32[2,128,768]{2,1,0:T(8,...) custom-call(bf16[128,768]{1,0:T(8,128)(2,1)} %bitcast.284, ...), custom_call_target="tpu_custom_call" | custom-call | tf_op jit(solution)/shard_map/forward_layers/pallas_call | solution.py:908
  186.9 7.1 %all-to-all-start.2 = ((f32[8,1,256]{2,1,0:T(1,128)}), f32[8,1,256]{2,1,0:T(1,128)S(1)}, u32[]{:S(2)}, u32[]{:S(2)}) async-start(f32[8,1,256]{2,1,0:T(1,128)} %reshape.317), calls=%async_computation.2 | async-start | bytes 16384 | tf_op jit(solution)/shard_map/all_to_all | solution.py:169
  198.9 4.5 all-to-all-start.3
  207.6 33.7 %all-to-all-done.3 = bf16[8,2,4,32,768]{4,3,1,2,0:T(8,128)(2,1)} async-done(((bf16[8,2,4,32,768]{4,3,1,2,0:T(8,128)(2,1)}), bf16[8,2,4,32,768]{4,3,1,2,0:T(8,128)(2,1)}, u32[]{:S(2)}, u32[]{:S(2)}) %all-to-all-start.3) | async-done | bytes 3145760 | tf_op jit(solution)/shard_map/all_to_all | solution.py:169
  241.3 4.5 all-to-all-start
  251.7 32.0 %all-to-all-done = bf16[8,2,4,32,768]{4,3,1,2,0:T(8,128)(2,1)} async-done(((bf16[8,2,4,32,768]{4,3,1,2,0:T(8,128)(2,1)}), bf16[8,2,4,32,768]{4,3,1,2,0:T(8,128)(2,1)}, u32[]{:S(2)}, u32[]{:S(2)}) %all-to-all-start) | async-done | bytes 3145760 | tf_op jit(solution)/shard_map/all_to_all | solution.py:169
  289.4 6.1 fusion.7
  300.4 4.8 all-to-all-start.4
  306.1 6.7 %convert_bitcast_fusion.2 = bf16[8,2,128,768]{3,2,0,1:T(8,128)(2,1)S(1)} fusion(bf16[2,768,768]{2,1,0:T(8,128)(2,1)S(1)} %copy-done, f32[2,768,8,128]{3,1,2,0:T(8,128)} %copy-done.24), kind=kOutput, calls=%fused_computation.27 | convolution fusion | flops 2431647744 | bytes 11796480 | tf_op jit(solution)/shard_map/sjcf,jfd->sjcd/dot_general | solution.py:1730
  314.8 28.3 %all-to-all-done.4 = bf16[8,2,128,768]{2,3,1,0:T(8,128)(2,1)} async-done(((bf16[8,2,128,768]{2,3,1,0:T(8,128)(2,1)}), bf16[8,2,128,768]{2,3,1,0:T(8,128)(2,1)}, u32[]{:S(2)}, u32[]{:S(2)}) %all-to-all-start.4) | async-done | bytes 3145760 | tf_op jit(solution)/shard_map/all_to_all | solution.py:169
  343.0 3.6 all-to-all-start.1
  358.0 5.3 mul.201
  365.1 7.4 %bitcast_convert_fusion.up_grad_hbm = bf16[2,768,768]{2,1,0:T(8,128)(2,1)} fusion(bf16[8,2,128,768]{3,2,0,1:T(8,128)(2,1)} %bitcast.278, bf16[8,2,128,768]{2,3,0,1:T(8,128)(2,1)} %copy-done.25), kind=kOutput, calls=%fused_computation.20 | convolution fusion | flops 2417098752 | bytes 8650752 | tf_op jit(solution)/shard_map/sjcd,sjcf->jdf/dot_general | solution.py:1743
  372.5 8.5 %fusion.27 = f32[2,768,768]{2,1,0:T(8,128)} fusion(bf16[8,2,128,768]{3,2,1,0:T(8,128)(2,1)S(1)} %copy-done.9, f32[2,768,8,128]{3,1,2,0:T(8,128)} %copy-done.24), kind=kOutput, calls=%fused_computation.39 | convolution fusion | flops 2430074880 | bytes 14155776 | tf_op jit(solution)/shard_map/sjcf,sjcd->jfd/dot_general | solution.py:1740
  381.0 4.6 copy.268
  389.4 3.7 collective-permute-start.6
  407.8 3.9 reshape.281
  411.7 16.8 %multiply_reduce_fusion.1 = f32[4,128,768]{2,1,0:T(8,128)S(1)} fusion(f32[4,128,2,768]{3,2,1,0:T(2,128)S(1)} %reshape.281, f32[4,128,2]{2,1,0:T(8,128)} %copy.238), kind=kLoop, calls=%fused_computation.26 | loop fusion | flops 1179648 | bytes 4722688 | tf_op jit(solution)/shard_map/reduce_sum | solution.py:1752
  432.8 3.8 collective-permute-start.2
  439.2 9.0 %collective-permute-done.7 = bf16[128,768]{1,0:T(8,128)(2,1)S(1)} collective-permute-done((bf16[128,768]{1,0:T(8,128)(2,1)}, bf16[128,768]{1,0:T(8,128)(2,1)S(1)}, u32[]{:S(2)}, u32[]{:S(2)}) %collective-permute-start.7) | collective-permute-done | bytes 196640 | tf_op jit(solution)/shard_map/ppermute | solution.py:45
  450.7 8.7 %collective-permute-done.1 = bf16[128,768]{1,0:T(8,128)(2,1)S(1)} collective-permute-done((bf16[128,768]{1,0:T(8,128)(2,1)S(1)}, bf16[128,768]{1,0:T(8,128)(2,1)S(1)}, u32[]{:S(2)}, u32[]{:S(2)}) %collective-permute-start.1) | collective-permute-done | bytes 196640 | tf_op jit(solution)/shard_map/ppermute | solution.py:45
  461.4 169.5 %backward_layers.1 = (f32[128,768]{1,0:T(8,128)}, bf16[2,8,192,384]{3,2,1,0:T(8,128)(2,1)}, bf16[8,192,384]{2,1,0:T(8,128)(2,1)}, bf16[8,96,768]{2,1,0:T(8,128)(...) custom-call(f32[128,768]{1,0:T(8,128)} %get-tuple-element.161.mid_grad_ref, ...), custom_call_target="tpu_custom_call" | custom-call | tf_op jit(solution)/shard_map/backward_layers/pallas_call | solution.py:1569
  (193 shorter events, 107.3 us)
Async XLA Ops:
  0.6 288.7 %copy-start = (bf16[2,768,768]{2,1,0:T(8,128)(2,1)S(1)}, bf16[2,768,768]{2,1,0:T(8,128)(2,1)}, u32[]{:S(2)}) copy-start(bf16[2,768,768]{2,1,0:T(8,128)(2,1)} %param.25) | copy-start | bytes 7077892
  0.7 18.1 %copy-start.2 = (s32[1024]{0:T(1024)S(1)}, s32[1024]{0:T(1024)}, u32[]{:S(2)}) copy-start(s32[1024]{0:T(1024)} %param.19) | copy-start | bytes 12292
  186.9 12.0 %all-to-all-start.2 = ((f32[8,1,256]{2,1,0:T(1,128)}), f32[8,1,256]{2,1,0:T(1,128)S(1)}, u32[]{:S(2)}, u32[]{:S(2)}) async-start(f32[8,1,256]{2,1,0:T(1,128)} %reshape.317), calls=%async_computation.2 | async-start | bytes 16384 | tf_op jit(solution)/shard_map/all_to_all | solution.py:169
  194.6 8.8 %copy-start.4 = (bf16[4,128,512]{2,1,0:T(8,128)(2,1)}, bf16[4,128,512]{2,1,0:T(8,128)(2,1)S(1)}, u32[]{:S(2)}) copy-start(bf16[4,128,512]{2,1,0:T(8,128)(2,1)S(1)} %fusion.34) | copy-start | bytes 1572868
  198.9 42.4 %all-to-all-start.3 = ((bf16[8,2,4,32,768]{4,3,1,2,0:T(8,128)(2,1)}), bf16[8,2,4,32,768]{4,3,1,2,0:T(8,128)(2,1)}, u32[]{:S(2)}, u32[]{:S(2)}) async-start(bf16[8,2,4,32,768]{4,3,1,2,0:T(8,128)(2,1)} %bitcast.270), calls=%async_computation.3 | async-start | bytes 6291456 | tf_op jit(solution)/shard_map/all_to_all | solution.py:169
  241.3 42.4 %all-to-all-start = ((bf16[8,2,4,32,768]{4,3,1,2,0:T(8,128)(2,1)}), bf16[8,2,4,32,768]{4,3,1,2,0:T(8,128)(2,1)}, u32[]{:S(2)}, u32[]{:S(2)}) async-start(bf16[8,2,4,32,768]{4,3,1,2,0:T(8,128)(2,1)} %bitcast.269), calls=%async_computation | async-start | bytes 6291456 | tf_op jit(solution)/shard_map/all_to_all | solution.py:169
  300.4 42.7 %all-to-all-start.4 = ((bf16[8,2,128,768]{2,3,1,0:T(8,128)(2,1)}), bf16[8,2,128,768]{2,3,1,0:T(8,128)(2,1)}, u32[]{:S(2)}, u32[]{:S(2)}) async-start(bf16[8,2,128,768]{2,3,1,0:T(8,128)(2,1)} %copy.267), calls=%async_computation.4 | async-start | bytes 6291456 | tf_op jit(solution)/shard_map/all_to_all | solution.py:169
  305.3 7.6 %copy-start.20 = (f32[128]{0:T(128)}, f32[128]{0:T(128)S(1)}, u32[]{:S(2)}) copy-start(f32[128]{0:T(128)S(1)} %fusion.44) | copy-start | bytes 1540
  343.0 53.5 %all-to-all-start.1 = ((bf16[8,2,128,768]{3,2,1,0:T(8,128)(2,1)}), bf16[8,2,128,768]{3,2,1,0:T(8,128)(2,1)S(1)}, u32[]{:S(2)}, u32[]{:S(2)}) async-start(bf16[8,2,128,768]{3,2,1,0:T(8,128)(2,1)} %copy.249), calls=%async_computation.1 | async-start | bytes 6291456 | tf_op jit(solution)/shard_map/all_to_all | solution.py:169
  365.1 7.5 %copy-start.9 = (bf16[8,2,128,768]{3,2,1,0:T(8,128)(2,1)S(1)}, bf16[8,2,128,768]{3,2,1,0:T(8,128)(2,1)}, u32[]{:S(2)}) copy-start(bf16[8,2,128,768]{3,2,1,0:T(8,128)(2,1)} %fusion.8) | copy-start | bytes 9437188
  389.4 49.7 %collective-permute-start.6 = (bf16[128,768]{1,0:T(8,128)(2,1)}, bf16[128,768]{1,0:T(8,128)(2,1)}, u32[]{:S(2)}, u32[]{:S(2)}) collective-permute-start(bf16[128,768]{1,0:T(8,128)(2,1)} %get-tuple-element.155), channel_id=1, source_target_pairs={{0,1},{1,2},{2,3},{3,0},{4,5},{5,6},{6,7},{7,4},{8,9},{9,10},{10,1... | collective-permute-start | bytes 589832 | tf_op jit(solution)/shard_map/ppermute | solution.py:45
  393.1 46.1 %collective-permute-start.8 = (bf16[128,768]{1,0:T(8,128)(2,1)}, bf16[128,768]{1,0:T(8,128)(2,1)}, u32[]{:S(2)}, u32[]{:S(2)}) collective-permute-start(bf16[128,768]{1,0:T(8,128)(2,1)} %get-tuple-element.156), channel_id=1, source_target_pairs={{0,3},{1,0},{2,1},{3,2},{4,7},{5,4},{6,5},{7,6},{8,11},{9,8},{10,9... | collective-permute-start | bytes 589832 | tf_op jit(solution)/shard_map/ppermute | solution.py:45
  403.9 26.8 %collective-permute-start.3 = (f32[128,2]{0,1:T(2,128)}, f32[128,2]{0,1:T(2,128)}, u32[]{:S(2)}, u32[]{:S(2)}) collective-permute-start(f32[128,2]{0,1:T(2,128)} %bitcast.32), channel_id=1, source_target_pairs={{0,1},{1,2},{2,3},{3,0},{4,5},{5,6},{6,7},{7,4},{8,9},{9,10},{10,1... | collective-permute-start | bytes 3080 | tf_op jit(solution)/shard_map/ppermute | solution.py:45
  403.9 28.9 %collective-permute-start.4 = (f32[128,2]{0,1:T(2,128)}, f32[128,2]{0,1:T(2,128)}, u32[]{:S(2)}, u32[]{:S(2)}) collective-permute-start(f32[128,2]{0,1:T(2,128)} %bitcast.33), channel_id=1, source_target_pairs={{0,2},{1,3},{2,0},{3,1},{4,6},{5,7},{6,4},{7,5},{8,10},{9,11},{10,... | collective-permute-start | bytes 3080 | tf_op jit(solution)/shard_map/ppermute | solution.py:45
  406.1 26.7 %collective-permute-start.5 = (f32[128,2]{0,1:T(2,128)S(1)}, f32[128,2]{0,1:T(2,128)}, u32[]{:S(2)}, u32[]{:S(2)}) collective-permute-start(f32[128,2]{0,1:T(2,128)S(1)} %bitcast.304), channel_id=1, source_target_pairs={{0,3},{1,0},{2,1},{3,2},{4,7},{5,4},{6,5},{7,6},{8,11},{9,8},{10,9... | collective-permute-start | bytes 3080 | tf_op jit(solution)/shard_map/ppermute | solution.py:45
  411.7 47.7 %copy-start.16 = (bf16[1,128,1,768]{3,1,2,0:T(8,128)(2,1)S(1)}, bf16[1,128,1,768]{3,1,2,0:T(8,128)(2,1)}, u32[]{:S(2)}) copy-start(bf16[1,128,1,768]{3,1,2,0:T(8,128)(2,1)} %param.27) | copy-start | bytes 589828
  429.6 20.3 %copy-start.22 = (f32[24]{0:T(128)S(1)}, f32[24]{0:T(128)}, u32[]{:S(2)}) copy-start(f32[24]{0:T(128)} %pad.12.clone) | copy-start | bytes 292
  429.6 21.0 %copy-start.21 = (f32[128]{0:T(128)S(1)}, f32[128]{0:T(128)}, u32[]{:S(2)}) copy-start(f32[128]{0:T(128)} %copy-done.20) | copy-start | bytes 1540
  429.6 29.8 %copy-start.12 = (f32[2,128,768]{2,1,0:T(8,128)S(1)}, f32[2,128,768]{2,1,0:T(8,128)}, u32[]{:S(2)}) copy-start(f32[2,128,768]{2,1,0:T(8,128)} %get-tuple-element.44) | copy-start | bytes 2359300
  430.8 17.5 %collective-permute-start.7 = (bf16[128,768]{1,0:T(8,128)(2,1)}, bf16[128,768]{1,0:T(8,128)(2,1)S(1)}, u32[]{:S(2)}, u32[]{:S(2)}) collective-permute-start(bf16[128,768]{1,0:T(8,128)(2,1)} %get-tuple-element.157), channel_id=1, source_target_pairs={{0,2},{1,3},{2,0},{3,1},{4,6},{5,7},{6,4},{7,5},{8,10},{9,11},{10,... | collective-permute-start | bytes 589832 | tf_op jit(solution)/shard_map/ppermute | solution.py:45
  432.8 17.8 %collective-permute-start = (bf16[128,768]{1,0:T(8,128)(2,1)S(1)}, bf16[128,768]{1,0:T(8,128)(2,1)S(1)}, u32[]{:S(2)}, u32[]{:S(2)}) collective-permute-start(bf16[128,768]{1,0:T(8,128)(2,1)S(1)} %get-tuple-element.158), channel_id=1, source_target_pairs={{0,1},{1,2},{2,3},{3,0},{4,5},{5,6},{6,7},{7,4},{8,9},{9,10},{10,1... | collective-permute-start | bytes 589832 | tf_op jit(solution)/shard_map/ppermute | solution.py:45
  432.8 17.8 %collective-permute-start.2 = (bf16[128,768]{1,0:T(8,128)(2,1)S(1)}, bf16[128,768]{1,0:T(8,128)(2,1)S(1)}, u32[]{:S(2)}, u32[]{:S(2)}) collective-permute-start(bf16[128,768]{1,0:T(8,128)(2,1)S(1)} %get-tuple-element.159), channel_id=1, source_target_pairs={{0,3},{1,0},{2,1},{3,2},{4,7},{5,4},{6,5},{7,6},{8,11},{9,8},{10,9... | collective-permute-start | bytes 589832 | tf_op jit(solution)/shard_map/ppermute | solution.py:45
  439.1 20.3 %collective-permute-start.1 = (bf16[128,768]{1,0:T(8,128)(2,1)S(1)}, bf16[128,768]{1,0:T(8,128)(2,1)S(1)}, u32[]{:S(2)}, u32[]{:S(2)}) collective-permute-start(bf16[128,768]{1,0:T(8,128)(2,1)S(1)} %get-tuple-element.160), channel_id=1, source_target_pairs={{0,2},{1,3},{2,0},{3,1},{4,6},{5,7},{6,4},{7,5},{8,10},{9,11},{10,... | collective-permute-start | bytes 589832 | tf_op jit(solution)/shard_map/ppermute | solution.py:45
  644.6 6.3 copy-start.1
  (16 other events, 52.6 us)

commit v4 on v3

--- a/solution.py
+++ b/solution.py
@@ -416,45 +416,53 @@
     return copy
 
 
-def small_kernel(groups, small_ref, routes_ref, small_out, routes_out, ssem, rsem, lsem):
+def small_kernel(groups, small_ref, slots_ref, small_out, slots_out, zs, zr, ps, pr, lsem):
     e, s = place()
     others = [(e, lax.rem(s + k, groups)) for k in range(1, groups)]
+    around = [(lax.rem(e + k, 8), s) for k in range(1, 8)]
     local = [
         pltpu.make_async_copy(small_ref, small_out.at[s], lsem.at[0]),
-        pltpu.make_async_copy(routes_ref, routes_out.at[s], lsem.at[1]),
+        pltpu.make_async_copy(slots_ref, slots_out.at[s, e], lsem.at[1]),
     ]
     for copy in local:
         copy.start()
-    greet(others)
-    sent = []
+    greet(others + around)
+    sent, first = [], []
     for k, device in enumerate(others):
-        push(sent, small_ref, small_out.at[s], ssem.at[0, k], rsem.at[0, k], device)
-        push(sent, routes_ref, routes_out.at[s], ssem.at[1, k], rsem.at[1, k], device)
+        push(sent, small_ref, small_out.at[s], zs.at[0, k], zr.at[0, k], device)
+        first.append(
+            push(sent, slots_ref, slots_out.at[s, e], zs.at[1, k], zr.at[1, k], device)
+        )
     for copy in local:
         copy.wait()
+    for copy in first:
+        copy.wait_recv()
+    column = slots_out.at[:, e]
+    for k, device in enumerate(around):
+        push(sent, column, column, ps.at[k], pr.at[k], device)
     for copy in sent:
-        copy.wait()
-
-
-def gather_small(small, routes):
+        if all(copy is not other for other in first):
+            copy.wait_recv()
+    for copy in sent:
+        copy.wait_send()
+
+
+def gather_small(small, slots):
     groups = lax.axis_size("shard")
     vmem = pl.BlockSpec(memory_space=VMEM)
+    sem = pltpu.SemaphoreType.DMA
     return pl.pallas_call(
         functools.partial(small_kernel, groups),
         name="gather_small",
         out_shape=(
             jax.ShapeDtypeStruct((groups,) + small.shape, small.dtype),
-            jax.ShapeDtypeStruct((groups,) + routes.shape, routes.dtype),
+            jax.ShapeDtypeStruct((groups, 8) + slots.shape, slots.dtype),
         ),
         in_specs=[vmem, vmem],
         out_specs=(vmem, vmem),
-        scratch_shapes=[
-            pltpu.SemaphoreType.DMA((2, groups - 1)),
-            pltpu.SemaphoreType.DMA((2, groups - 1)),
-            pltpu.SemaphoreType.DMA((2,)),
-        ],
+        scratch_shapes=[sem((2, 3)), sem((2, 3)), sem((7,)), sem((7,)), sem((2,))],
         compiler_params=pltpu.CompilerParams(collective_id=1, has_side_effects=True),
-    )(small, routes)
+    )(small, slots)
 
 
 def norm_rows(inputs, gain):
@@ -484,6 +492,70 @@
 T = 128
 PAIRS = H // 2
 TOE = 1152
+CAP = 32
+
+
+class Plane:
+    def __init__(self):
+        self.e, self.s = place()
+        e = self.e
+        self.core = lax.rem(e, 2)
+        self.quarter = e // 2
+        self.at_x = e + 2 - 4 * lax.rem(self.quarter, 2)
+        self.at_y = lax.rem(e + 4, 8)
+        self.at_core = e + 1 - 2 * self.core
+        self.inward = jnp.where(self.core == 0, self.at_x, self.at_y)
+        self.onward = jnp.where(self.core == 0, self.at_y, self.at_x)
+        self.diagonal = self.inward + self.onward - e
+        self.others = [lax.rem(self.s + k, 4) for k in range(1, 4)]
+        self.around = [lax.rem(e + k, 8) for k in range(1, 8)]
+        self.sent = []
+
+    def push(self, source, target, send_sem, recv_sem, device):
+        return push(self.sent, source, target, send_sem, recv_sem, device)
+
+    def arrived(self, view, recv_sem):
+        pltpu.make_async_remote_copy(
+            src_ref=view,
+            dst_ref=view,
+            send_sem=recv_sem,
+            recv_sem=recv_sem,
+            device_id=(self.at_core, self.s),
+            device_id_type=MESH,
+        ).wait_recv()
+
+
+class PlaneGather:
+    def __init__(self, plane, view, send_sems, recv_sems):
+        self.plane, self.view, self.ss, self.rs = plane, view, send_sems, recv_sems
+
+    def _push(self, who, i, target):
+        p = self.plane
+        block = self.view(who)
+        p.push(block, block, self.ss.at[i], self.rs.at[i], (target, p.s))
+
+    def first(self):
+        p = self.plane
+        self._push(p.e, 0, p.at_x)
+        self._push(p.e, 1, p.at_y)
+        self._push(p.e, 3, p.at_core)
+
+    def second(self):
+        p = self.plane
+        p.arrived(self.view(p.inward), self.rs.at[p.core])
+        self._push(p.inward, 2, p.onward)
+        self._push(p.inward, 4, p.at_core)
+
+    def third(self):
+        p = self.plane
+        p.arrived(self.view(p.onward), self.rs.at[1 - p.core])
+        self._push(p.onward, 5, p.at_core)
+        p.arrived(self.view(p.diagonal), self.rs.at[2])
+        self._push(p.diagonal, 6, p.at_core)
+
+    def done(self):
+        for i in range(3, 7):
+            self.plane.arrived(self.view(self.plane.e), self.rs.at[i])
 
 
 def forward_kernel(
@@ -505,7 +577,7 @@
     act_out,
     one_out,
     peak_out,
-    normed_all,
+    moe_normed_out,
     qkv0_out,
     qkv1_out,
     proj0_out,
@@ -579,6 +651,9 @@
         rows = pl.ds(pl.multiple_of(position * 4 * height + who * height, height), height)
         return target.at[rows, lane_block(half, width)]
 
+    def cot_block(g, who):
+        return cot_all.at[g, who]
+
     stage1, stage2, stage3, stage4, own = {}, {}, {}, {}, {}
 
     def z_send(c):
@@ -644,9 +719,7 @@
         own[c].wait()
         kept.append(local(chunks[c][1], weight_outs[c], outs_sem.at[c]))
 
-    greet(
-        [(at_core, s), (at_x, s), (at_y, s)] + [(e, other) for other in others]
-    )
+    greet([(at_core, s), (at_x, s), (at_y, s)] + [(e, other) for other in others])
     z_send(0)
     z_send(1)
     z_send(2)
@@ -818,6 +891,25 @@
         core_send(2)
         plane_send(3)
 
+    plane = Plane()
+    cot_groups = [s] + sources
+    cot_gathers = []
+    for k, g in enumerate(cot_groups):
+        cot_gathers.append(
+            PlaneGather(plane, functools.partial(cot_block, g), ns.at[k], nr.at[k])
+        )
+
+    def cot_send():
+        for k in range(3):
+            push(sent, cot_hbm, cot_block(s, e), gs.at[k], gr.at[k], (e, others[k]))
+        copy = local(cot_hbm, cot_block(s, e), gs.at[3])
+        copy.wait()
+        cot_gathers[0].first()
+
+    def cot_first(k):
+        plane.arrived(cot_block(s, e), gr.at[k - 1])
+        cot_gathers[k].first()
+
     hidden = hidden_ref[...].astype(single)
     attention(0, hidden, w_qkv0, w_out0, [work0, work1, work2, work3, work4])
     ready(1)
@@ -837,9 +929,6 @@
                 (e, others[k]),
             )
         )
-        reshard.append(
-            push(sent, cot_hbm, cot_all.at[s], gs.at[k], gr.at[k], (e, others[k]))
-        )
     kept.append(
         local(
             expert_up_hbm.at[:, :, lane_block(s, 768)],
@@ -847,7 +936,7 @@
             us.at[3],
         )
     )
-    kept.append(local(cot_hbm, cot_all.at[s], gs.at[3]))
+    cot_send()
     ready(2)
 
     def up_part(i):
@@ -880,21 +969,41 @@
     loop(4, down_part)
     core_send(4)
     core_send(5)
-    attention(1, one_out[...], w_qkv1, w_out1, None)
+
+    def work5():
+        cot_first(1)
+        cot_gathers[0].second()
+
+    def work6():
+        cot_first(2)
+
+    def work7():
+        cot_gathers[0].third()
+        cot_gathers[1].second()
+
+    def work8():
+        cot_first(3)
+        cot_gathers[1].third()
+        cot_gathers[2].second()
+
+    def work9():
+        cot_gathers[2].third()
+        cot_gathers[3].second()
+
+    attention(1, one_out[...], w_qkv1, w_out1, [work5, work6, work7, work8, work9])
+    cot_gathers[3].third()
     ready(5)
     mid_out[1] = one_out[...] + jnp.dot(
         attended_out[1], w_out1[...], preferred_element_type=single
     )
-    normed_all[s] = norm_rows(mid_out[1], gains_ref[pl.ds(3, 1), :]).astype(bfloat)
-    last = [
-        push(sent, normed_all.at[s], normed_all.at[s], ns.at[k], nr.at[k], (e, others[k]))
-        for k in range(3)
-    ]
-    for copy in last + reshard:
+    moe_normed_out[...] = norm_rows(mid_out[1], gains_ref[pl.ds(3, 1), :]).astype(bfloat)
+    for gather in cot_gathers:
+        gather.done()
+    for copy in reshard:
         copy.wait_recv()
     for copy in kept:
         copy.wait()
-    for copy in sent:
+    for copy in sent + plane.sent:
         copy.wait_send()
 
 
@@ -918,7 +1027,7 @@
             shape((T, ff), bfloat),
             shape((T, D), single),
             shape((2 * H, 128), single),
-            shape((4, T, D), bfloat),
+            shape((T, D), bfloat),
             shape((D, 3 * D), bfloat),
             shape((D, 3 * D), bfloat),
             shape((D, D), bfloat),
@@ -928,7 +1037,7 @@
             shape((2, 3, length, 512), bfloat),
             shape((2, H * T, length), bfloat),
             shape((EXP_DEV, D, 768), bfloat),
-            shape((4, T, D), bfloat),
+            shape((4, 8, T, D), bfloat),
         ),
         in_specs=[vmem] * 3 + [anywhere] * 6,
         out_specs=(vmem,) * 10 + (anywhere,) * 10,
@@ -952,76 +1061,13 @@
             sem((2, 3, 4)), sem((2, 3, 4)),
             sem((4,)), sem((3,)),
             sem((4,)), sem((3,)),
-            sem((3,)), sem((3,)),
+            sem((4, 7)), sem((4, 7)),
             sem((10,)),
         ],
         compiler_params=pltpu.CompilerParams(
             collective_id=2, has_side_effects=True, vmem_limit_bytes=56 * 2**20
         ),
     )(hidden, gains, table, qkv, out, up, down, expert_up, cotangent)
-
-
-class Plane:
-    def __init__(self):
-        self.e, self.s = place()
-        e = self.e
-        self.core = lax.rem(e, 2)
-        self.quarter = e // 2
-        self.at_x = e + 2 - 4 * lax.rem(self.quarter, 2)
-        self.at_y = lax.rem(e + 4, 8)
-        self.at_core = e + 1 - 2 * self.core
-        self.inward = jnp.where(self.core == 0, self.at_x, self.at_y)
-        self.onward = jnp.where(self.core == 0, self.at_y, self.at_x)
-        self.diagonal = self.inward + self.onward - e
-        self.others = [lax.rem(self.s + k, 4) for k in range(1, 4)]
-        self.around = [lax.rem(e + k, 8) for k in range(1, 8)]
-        self.sent = []
-
-    def push(self, source, target, send_sem, recv_sem, device):
-        return push(self.sent, source, target, send_sem, recv_sem, device)
-
-    def arrived(self, view, recv_sem):
-        pltpu.make_async_remote_copy(
-            src_ref=view,
-            dst_ref=view,
-            send_sem=recv_sem,
-            recv_sem=recv_sem,
-            device_id=(self.at_core, self.s),
-            device_id_type=MESH,
-        ).wait_recv()
-
-
-class PlaneGather:
-    def __init__(self, plane, view, send_sems, recv_sems):
-        self.plane, self.view, self.ss, self.rs = plane, view, send_sems, recv_sems
-
-    def _push(self, who, i, target):
-        p = self.plane
-        block = self.view(who)
-        p.push(block, block, self.ss.at[i], self.rs.at[i], (target, p.s))
-
-    def first(self):
-        p = self.plane
-        self._push(p.e, 0, p.at_x)
-        self._push(p.e, 1, p.at_y)
-        self._push(p.e, 3, p.at_core)
-
-    def second(self):
-        p = self.plane
-        p.arrived(self.view(p.inward), self.rs.at[p.core])
-        self._push(p.inward, 2, p.onward)
-        self._push(p.inward, 4, p.at_core)
-
-    def third(self):
-        p = self.plane
-        p.arrived(self.view(p.onward), self.rs.at[1 - p.core])
-        self._push(p.onward, 5, p.at_core)
-        p.arrived(self.view(p.diagonal), self.rs.at[2])
-        self._push(p.diagonal, 6, p.at_core)
-
-    def done(self):
-        for i in range(3, 7):
-            self.plane.arrived(self.view(self.plane.e), self.rs.at[i])
 
 
 class SmallReduce:
@@ -1631,6 +1677,384 @@
     )
 
 
+def experts_kernel(
+    normed_ref,
+    mid_ref,
+    gains_ref,
+    router_ref,
+    router_turned_ref,
+    slots_ref,
+    slot_columns_ref,
+    own_cot_ref,
+    cot_hbm,
+    up_hbm,
+    down_hbm,
+    hidden_out,
+    mid_grad_out,
+    small_out,
+    up_grad_out,
+    down_grad_out,
+    normed_all,
+    cots,
+    w_up,
+    w_down,
+    rows,
+    gated,
+    gates,
+    acts,
+    pre_grads,
+    raw,
+    row_send,
+    out_send,
+    row_back,
+    out_back,
+    slot_grads,
+    slot_z,
+    slot_sum,
+    slot_plane,
+    row_part,
+    out_part,
+    row_z,
+    out_z,
+    ns,
+    nr,
+    gs,
+    gr,
+    rs,
+    rr,
+    os,
+    orr,
+    ss,
+    sr,
+    ps,
+    pr,
+    rzs,
+    rzr,
+    ozs,
+    ozr,
+    loads,
+):
+    p = Plane()
+    e, s = p.e, p.s
+    groups = [s] + [lax.rem(s + 4 - k, 4) for k in range(1, 4)]
+
+    def load(source, target, i):
+        copy = pltpu.make_async_copy(source, target, loads.at[i])
+        copy.start()
+        return copy
+
+    got_cots = [load(cot_hbm.at[groups[k]], cots.at[k], k) for k in range(2)]
+    got_up = load(up_hbm, w_up, 4)
+    got_down = load(down_hbm, w_down, 5)
+    normed_all[s, e] = normed_ref[...]
+    greet([(d, s) for d in p.around] + [(e, other) for other in p.others])
+    mine = normed_all.at[s, e]
+    for k in range(3):
+        p.push(mine, mine, ns.at[k], nr.at[k], (e, p.others[k]))
+
+    def gather(k):
+        g = groups[k]
+        return PlaneGather(p, lambda who: normed_all.at[g, who], gs.at[k], gr.at[k])
+
+    gathers = [gather(k) for k in range(4)]
+    gathers[0].first()
+
+    ids = 2 * e * CAP + lax.broadcasted_iota(jnp.int32, (2 * CAP, T), 0)
+    expert_low = CAP * lax.broadcasted_iota(jnp.int32, (16, T), 0)
+
+    def route_masks(g, who):
+        at = (g * 8 + who) * 2
+        first, second = slots_ref[pl.ds(at, 1), :], slots_ref[pl.ds(at + 1, 1), :]
+        return first, second, ids == first, ids == second
+
+    def select_cots(k):
+        g = groups[k]
+        got_cots[k].wait()
+
+        def one(who):
+            _, _, mark0, mark1 = route_masks(g, who)
+            mark = jnp.where(mark0 | mark1, 1.0, 0.0).astype(bfloat)
+            picked = jnp.dot(mark, cots[k % 2, who], preferred_element_type=single).astype(bfloat)
+            for j in range(2):
+                raw[j, g, row_block(who, CAP), :] = picked[j * CAP : (j + 1) * CAP]
+
+        loop(8, one)
+        if k < 2:
+            got_cots.append(load(cot_hbm.at[groups[k + 2]], cots.at[k], k + 2))
+
+    def select_rows(k):
+        g = groups[k]
+
+        def one(who):
+            slot0, slot1, mark0, mark1 = route_masks(g, who)
+            block = normed_all[g, who]
+            mark = jnp.where(mark0 | mark1, 1.0, 0.0).astype(bfloat)
+            picked = jnp.dot(mark, block, preferred_element_type=single).astype(bfloat)
+            logits = dot_rows(router_turned_ref[...], block)
+            chosen = [
+                jnp.sum(
+                    jnp.where((slot >= expert_low) & (slot < expert_low + CAP), logits, 0.0),
+                    axis=0,
+                    keepdims=True,
+                )
+                for slot in (slot0, slot1)
+            ]
+            top = jnp.maximum(chosen[0], chosen[1])
+            weight = [jnp.exp(value - top) for value in chosen]
+            total = weight[0] + weight[1]
+            gate = jnp.sum(
+                jnp.where(mark0, weight[0] / total, 0.0) + jnp.where(mark1, weight[1] / total, 0.0),
+                axis=1,
+                keepdims=True,
+            )
+            for j in range(2):
+                part = slice(j * CAP, (j + 1) * CAP)
+                rows[j, g, row_block(who, CAP), :] = picked[part]
+                gates[j, g, row_block(who, CAP), :] = jnp.broadcast_to(gate[part], (CAP, 128))
+
+        loop(8, one)
+
+    def compute(k):
+        g = groups[k]
+
+        def one(j):
+            before = jnp.dot(rows[j, g], w_up[j], preferred_element_type=single)
+            act = jax.nn.gelu(before).astype(bfloat)
+            acts[j, g] = act
+            gate = gates[j, g][:, :1]
+            cot = raw[j, g].astype(single)
+            weighted = (gate * cot).astype(bfloat)
+            gated[j, g] = weighted
+            act_grad = dot_rows(weighted, w_down[j])
+            pre_grad = (act_grad * gelu_slope(before)).astype(bfloat)
+            pre_grads[j, g] = pre_grad
+            row_grad = dot_rows(pre_grad, w_up[j])
+            row_send[g, j] = row_grad.astype(bfloat).reshape(8, CAP, D)
+            out = jnp.dot(act, w_down[j], preferred_element_type=single)
+            out_send[g, j] = (gate * out).astype(bfloat).reshape(8, CAP, D)
+            slot_grads[g, pl.ds(j, 1), :] = lax.dot_general(
+                jnp.ones((8, D), single),
+                out * cot,
+                (((1,), (1,)), ((), ())),
+                precision=lax.Precision.HIGHEST,
+                preferred_element_type=single,
+            )[:1]
+
+        loop(2, one)
+
+    def give_back(k, source, target, send_sems, recv_sems):
+        g = groups[k]
+        target[g, e] = source[g, :, e]
+        for i, d in enumerate(p.around):
+            p.push(
+                source.at[g, :, d], target.at[g, e], send_sems.at[k, i], recv_sems.at[k, i], (d, s)
+            )
+
+    def step(k):
+        select_rows(k)
+        compute(k)
+        give_back(k, row_send, row_back, rs, rr)
+
+    def arrive(k):
+        p.arrived(mine, nr.at[k - 1])
+        gathers[k].first()
+
+    slot_grads[...] = jnp.zeros_like(slot_grads)
+    select_cots(0)
+    gathers[0].second()
+    arrive(1)
+    gathers[0].third()
+    gathers[1].second()
+    arrive(2)
+    gathers[0].done()
+    gathers[1].third()
+    gathers[2].second()
+    arrive(3)
+    got_up.wait()
+    got_down.wait()
+    step(0)
+    gathers[2].third()
+    gathers[3].second()
+    select_cots(1)
+    gathers[1].done()
+    step(1)
+    gathers[3].third()
+    select_cots(2)
+    gathers[2].done()
+    step(2)
+    select_cots(3)
+    gathers[3].done()
+    step(3)
+    for k in range(4):
+        give_back(k, out_send, out_back, os, orr)
+    for k in range(3):
+        p.push(
+            slot_grads.at[p.others[k]], slot_z.at[k], ss.at[k], sr.at[k], (e, p.others[k])
+        )
+
+    def weight_grads(i):
+        j = i // 3
+        lanes = lane_block(lax.rem(i, 3), 256)
+        inputs = rows[j].reshape(4 * 8 * CAP, D)
+        up_grad_out[j, :, lanes] = dot_columns(
+            inputs, pre_grads[j, :, :, lanes].reshape(4 * 8 * CAP, 256)
+        ).astype(bfloat)
+        inputs = acts[j].reshape(4 * 8 * CAP, -1)
+        down_grad_out[j, :, lanes] = dot_columns(
+            inputs, gated[j, :, :, lanes].reshape(4 * 8 * CAP, 256)
+        )
+
+    loop(3, weight_grads)
+    total = slot_grads[s]
+    for k in range(3):
+        p.arrived(slot_z.at[k], sr.at[k])
+        total = total + slot_z[k]
+    slot_sum[...] = total
+    slot_plane[e] = total
+    for i, d in enumerate(p.around):
+        p.push(slot_sum, slot_plane.at[e], ps.at[i], pr.at[i], (d, s))
+
+    slot_lanes = lax.broadcasted_iota(jnp.int32, (T, 16 * CAP), 1)
+
+    def collect(k, back, recv_sems, part, z_in, z_send, z_recv):
+        g = groups[k]
+        for i in range(7):
+            p.arrived(back.at[g, e], recv_sems.at[k, i])
+        columns = slot_columns_ref[g]
+        marks = jnp.where(
+            (columns[:, :1] == slot_lanes) | (columns[:, 1:2] == slot_lanes), 1.0, 0.0
+        ).astype(bfloat)
+        combined = jnp.dot(
+            marks, back[g].reshape(16 * CAP, D), preferred_element_type=single
+        )
+        part[g] = combined.astype(bfloat)
+        if k:
+            p.push(part.at[g], z_in.at[k - 1], z_send.at[k - 1], z_recv.at[k - 1], (e, g))
+
+    for k in (1, 2, 3, 0):
+        collect(k, row_back, rr, row_part, row_z, rzs, rzr)
+
+    def weight_later(i):
+        weight_grads(i + 3)
+
+    loop(3, weight_later)
+
+    for i in range(7):
+        p.arrived(slot_sum, pr.at[i])
+    turned = pltpu.roll(
+        slot_plane[...].reshape(64, 8 * CAP), lax.rem(8 * CAP - CAP * e, 8 * CAP), 1
+    )
+    logits = jnp.dot(normed_ref[...], router_ref[...], preferred_element_type=single)
+    columns = slot_columns_ref[s]
+    expert_lanes = CAP * lax.broadcasted_iota(jnp.int32, (T, 16), 1)
+    picks, chosen, grads = [], [], []
+    small_lanes = lax.broadcasted_iota(jnp.int32, (T, CAP), 1)
+    for r in range(2):
+        slot = columns[:, r : r + 1]
+        picks.append((slot >= expert_lanes) & (slot < expert_lanes + CAP))
+        chosen.append(jnp.sum(jnp.where(picks[r], logits, 0.0), axis=1, keepdims=True))
+        found = jnp.zeros((T, CAP), single)
+        for who in range(8):
+            for j in range(2):
+                values = turned[8 * who + j : 8 * who + j + 1, :CAP]
+                found = found + jnp.where(slot - (2 * who + j) * CAP == small_lanes, values, 0.0)
+        grads.append(jnp.sum(found, axis=1, keepdims=True))
+    top = jnp.maximum(chosen[0], chosen[1])
+    weight = [jnp.exp(value - top) for value in chosen]
+    total = weight[0] + weight[1]
+    weight = [value / total for value in weight]
+    mean = weight[0] * grads[0] + weight[1] * grads[1]
+    logit_grad = jnp.zeros((T, 16), single)
+    for r in range(2):
+        logit_grad = logit_grad + jnp.where(picks[r], weight[r] * (grads[r] - mean), 0.0)
+    logit_grad = logit_grad.astype(bfloat)
+    small_out[...] = jnp.zeros_like(small_out)
+    small_out[:16, :] = dot_columns(logit_grad, normed_ref[...])
+    normed_grad = jnp.dot(logit_grad, router_turned_ref[...], preferred_element_type=single)
+    normed_grad = normed_grad + row_part[s].astype(single)
+    for k in range(3):
+        p.arrived(row_z.at[k], rzr.at[k])
+        normed_grad = normed_grad + row_z[k].astype(single)
+    input_grad, gain_grad = norm_pull(mid_ref[...], gains_ref[3:4, :], normed_grad)
+    small_out[16:17, :] = gain_grad
+    mid_grad_out[...] = own_cot_ref[...].astype(single) + input_grad
+
+    for k in (1, 2, 3, 0):
+        collect(k, out_back, orr, out_part, out_z, ozs, ozr)
+    result = mid_ref[...] + out_part[s].astype(single)
+    for k in range(3):
+        p.arrived(out_z.at[k], ozr.at[k])
+        result = result + out_z[k].astype(single)
+    hidden_out[...] = result.astype(bfloat)
+    for copy in p.sent:
+        copy.wait_send()
+
+
+def run_experts(
+    normed, mid, gains, router, slots, slot_columns, own_cot, cots, up_own, expert_down
+):
+    vmem = pl.BlockSpec(memory_space=VMEM)
+    anywhere = pl.BlockSpec(memory_space=ANY)
+    shape = jax.ShapeDtypeStruct
+    width = expert_down.shape[1]
+    sem = pltpu.SemaphoreType.DMA
+    per_expert = (EXP_DEV, 4, 8 * CAP)
+    sends = (4, EXP_DEV, 8, CAP, D)
+    backs = (4, 8, EXP_DEV, CAP, D)
+    return pl.pallas_call(
+        experts_kernel,
+        name="experts",
+        out_shape=(
+            shape((T, D), bfloat),
+            shape((T, D), single),
+            shape((24, D), single),
+            shape((EXP_DEV, D, width), bfloat),
+            shape((EXP_DEV, width, D), single),
+        ),
+        in_specs=[vmem] * 8 + [anywhere] * 3,
+        out_specs=(vmem,) * 5,
+        scratch_shapes=[
+            VMEM((4, 8, T, D), bfloat),
+            VMEM((2, 8, T, D), bfloat),
+            VMEM((EXP_DEV, D, width), bfloat),
+            VMEM((EXP_DEV, width, D), bfloat),
+            VMEM(per_expert + (D,), bfloat),
+            VMEM(per_expert + (D,), bfloat),
+            VMEM(per_expert + (128,), single),
+            VMEM(per_expert + (width,), bfloat),
+            VMEM(per_expert + (width,), bfloat),
+            VMEM(per_expert + (D,), bfloat),
+            VMEM(sends, bfloat),
+            VMEM(sends, bfloat),
+            VMEM(backs, bfloat),
+            VMEM(backs, bfloat),
+            VMEM((4, 8, 8 * CAP), single),
+            VMEM((3, 8, 8 * CAP), single),
+            VMEM((8, 8 * CAP), single),
+            VMEM((8, 8, 8 * CAP), single),
+            VMEM((4, T, D), bfloat),
+            VMEM((4, T, D), bfloat),
+            VMEM((3, T, D), bfloat),
+            VMEM((3, T, D), bfloat),
+            sem((3,)), sem((3,)),
+            sem((4, 7)), sem((4, 7)),
+            sem((4, 7)), sem((4, 7)),
+            sem((4, 7)), sem((4, 7)),
+            sem((3,)), sem((3,)),
+            sem((7,)), sem((7,)),
+            sem((3,)), sem((3,)),
+            sem((3,)), sem((3,)),
+            sem((6,)),
+        ],
+        compiler_params=pltpu.CompilerParams(
+            collective_id=4, has_side_effects=True, vmem_limit_bytes=60 * 2**20
+        ),
+    )(
+        normed, mid, gains, router, router.T, slots, slot_columns, own_cot, cots, up_own,
+        expert_down,
+    )
+
+
 def shards(
     hidden_in,
     attn_gain,
@@ -1654,7 +2078,13 @@
     here = lax.axis_index("shard")
     expert_total = EXP_DEV * experts
     capacity = 4 * block_rows // expert_total
-    width = expert_down.shape[1]
+
+    expert_ids = jnp.arange(expert_total, dtype=jnp.int32)
+    flat_routes = routes.reshape(-1)
+    marks = (flat_routes[:, None] == expert_ids).astype(bfloat)
+    earlier = jnp.tri(2 * block_rows, k=-1, dtype=bfloat)
+    rank = jnp.sum(matmul(earlier, marks) * marks.astype(single), axis=1).astype(jnp.int32)
+    slots = (flat_routes * capacity + rank).reshape(block_rows, 2).T
 
     small = jnp.concatenate(
         [attn_gain.reshape(-1), mlp_gain.reshape(-1), rel_bias.reshape(-1), router_weight.reshape(-1)]
@@ -1662,13 +2092,14 @@
     part = D // groups
     used = small.shape[0]
     small = jnp.pad(small, (0, -used % 1024)).reshape(-1, 128)
-    small, route_rows = gather_small(small, routes.reshape(-1, 128))
+    small, slots_all = gather_small(small, slots)
+    slot_columns = lax.dynamic_index_in_dim(
+        slots_all, lax.axis_index("expert"), 1, keepdims=False
+    ).transpose(0, 2, 1)
     small = small.reshape(groups, -1)
-    route_rows = route_rows.reshape(groups, block_rows, 2)
     cuts = [0, 4 * part, 4 * part + 2 * (NB // groups) * H, used]
     gains, bias_weights, router_full = (small[:, cuts[i] : cuts[i + 1]] for i in range(3))
     gains = gains.reshape(groups, 4, part).transpose(1, 0, 2).reshape(4, D)
-    gain_mlp = gains[2:]
     bias_weights = (
         bias_weights.reshape(groups, 2, NB // groups, H).transpose(1, 0, 2, 3).reshape(2, NB, H)
     )
@@ -1683,88 +2114,15 @@
 
     (
         normed, queries, attended, mid, dense_normed, pre_act, activation, layer_one, peak_rows,
-        normed_all, qkv0, qkv1, projection0, projection1, dense_up, dense_down, kv, probs, up_own,
+        moe_normed, qkv0, qkv1, projection0, projection1, dense_up, dense_down, kv, probs, up_own,
         upstream_all,
     ) = forward(
         hidden_in.reshape(block_rows, D), gains, table, qkv_weight, out_weight, mlp_up, mlp_down,
         expert_up, out_grad.reshape(block_rows, D),
     )
-    mid_second = mid[1]
-    moe_normed = lax.dynamic_index_in_dim(normed_all, here, 0, keepdims=False)
-    expert_ids = jnp.arange(expert_total, dtype=jnp.int32)
-    flat_routes = route_rows.reshape(groups, -1)
-    marks = (flat_routes[:, :, None] == expert_ids).astype(jnp.int32)
-    rank = jnp.sum((jnp.cumsum(marks, axis=1) - marks) * marks, axis=2)
-    slot_of_route = flat_routes * capacity + rank
-    slot_ids = jnp.arange(expert_total * capacity, dtype=jnp.int32)
-    slot_marks = (slot_of_route[:, :, None] == slot_ids).astype(bfloat)
-    token_marks = jnp.sum(
-        slot_marks.reshape(groups, block_rows, 2, -1).astype(single), axis=2
-    ).astype(bfloat)
-
-    def dispatch(rows):
-        slots = jnp.einsum("gts,gtd->gsd", token_marks, rows, preferred_element_type=single)
-        slots = slots.astype(bfloat).reshape(groups, experts, EXP_DEV, capacity, D)
-        return exchange(slots.transpose(1, 2, 0, 3, 4)).reshape(
-            experts, EXP_DEV, groups * capacity, D
-        )
-
-    def collect(blocks):
-        back = exchange(blocks.astype(bfloat)).reshape(experts, EXP_DEV, groups, capacity, D)
-        return back.transpose(2, 0, 1, 3, 4).reshape(groups, expert_total * capacity, D)
-
-    owner_rows = dispatch(upstream_all)
-    received = dispatch(normed_all)
-    router_logits = jnp.einsum("gtd,de->gte", normed_all, router_full, preferred_element_type=single)
-    selected = (route_rows[..., None] == expert_ids).astype(single)
-    gates_all = jax.nn.softmax(jnp.sum(selected * router_logits[:, :, None, :], axis=-1), axis=-1)
-    slot_gates = jnp.sum(
-        gates_all.reshape(groups, -1)[:, :, None] * (slot_of_route[:, :, None] == slot_ids), axis=1
-    )
-    owner_gates = exchange(
-        slot_gates.reshape(groups, experts, EXP_DEV, capacity).transpose(1, 2, 0, 3)
-    ).reshape(experts, EXP_DEV, groups * capacity)
-
-    expert_pre = jnp.einsum("sjcd,jdf->sjcf", received, up_own, preferred_element_type=single)
-    expert_act = jax.nn.gelu(expert_pre).astype(bfloat)
-    expert_out = jnp.einsum(
-        "sjcf,jfd->sjcd", expert_act, expert_down, preferred_element_type=single
-    )
-    owner_grad = (owner_gates[..., None] * owner_rows.astype(single)).astype(bfloat)
-    act_grad = jnp.einsum("sjcd,jfd->sjcf", owner_grad, expert_down, preferred_element_type=single)
-    pre_grad = gelu_back(expert_pre, act_grad).astype(bfloat)
-    row_grad = jnp.einsum("sjcf,jdf->sjcd", pre_grad, up_own, preferred_element_type=single)
-
-    returned = collect(expert_out)
-    back_rows = collect(row_grad)
-    expert_down_grad = jnp.einsum(
-        "sjcf,sjcd->jfd", expert_act, owner_grad, preferred_element_type=single
-    )
-    up_grad = jnp.einsum(
-        "sjcd,sjcf->jdf", received, pre_grad, preferred_element_type=single
-    ).astype(bfloat)
-
-    route_out = jnp.einsum("grs,gsd->grd", slot_marks, returned, preferred_element_type=single)
-    route_out = route_out.reshape(groups, block_rows, 2, D)
-    gate_grad = scatter_shard(
-        jnp.sum(route_out * upstream_all[:, :, None, :].astype(single), axis=-1), single
-    )
-    mixed = scatter_shard(jnp.sum(gates_all[..., None] * route_out, axis=2))
-    hidden_out = (mid_second + mixed).astype(bfloat).reshape(hidden_in.shape)
-
-    gates = lax.dynamic_index_in_dim(gates_all, here, 0, keepdims=False)
-    own_selected = lax.dynamic_index_in_dim(selected, here, 0, keepdims=False)
-    upstream = out_grad.reshape(block_rows, D).astype(single)
-    chosen_grad = gates * (gate_grad - jnp.sum(gates * gate_grad, axis=-1, keepdims=True))
-    logit_grad = jnp.sum(chosen_grad[:, :, None] * own_selected, axis=1).astype(bfloat)
-    router_grad = matmul(moe_normed.T, logit_grad)
-    row_terms = jnp.einsum("gts,gsd->gtd", token_marks, back_rows, preferred_element_type=single)
-    normed_grad = matmul(logit_grad, router_full.T) + scatter_shard(row_terms)
-    moe_input_grad, moe_gain_grad = norm_back(mid_second, gain_mlp[1], normed_grad)
-    mid_grad = upstream + moe_input_grad
-
-    small_in = jnp.concatenate(
-        [router_grad.T, moe_gain_grad[None], jnp.zeros((24 - expert_total - 1, D), single)]
+    hidden_out, mid_grad, small_in, up_grad, expert_down_grad = run_experts(
+        moe_normed, mid[1], gains, router_full, slots_all.reshape(-1, block_rows), slot_columns,
+        out_grad.reshape(block_rows, D), upstream_all, up_own, expert_down,
     )
     hidden_grad, attention_sum, up_sum, down_sum, small_sum, late_sum, peaks, expert_up_low = (
         backward(
@@ -1789,7 +2147,7 @@
     biases = lax.dynamic_slice_in_dim(late_sum[8:32], here * (NB // groups), NB // groups, 1)
     clip_scales = jnp.sqrt(clip_limit / jnp.maximum(peaks[:, 0].reshape(2, H), clip_limit))
     return (
-        hidden_out,
+        hidden_out.reshape(hidden_in.shape),
         hidden_grad.reshape(hidden_in.shape),
         jnp.concatenate([gain_rows, rows[expert_total + 1 : expert_total + 2]]),
         attention_sum[:, :, : 3 * D],

time: 663 us -> 554 us (0.84)
  the two profiles are of different devices: /device:TPU:0 before, /device:TPU:29 now
where the time goes in v4:
time: 554 us; the launch traced here: 545 us
  Pallas kernels  499 us (90%)
  local copies, waits for them, and re-layouts  33.2 us (6%)
  other arithmetic  9.91 us (2%)
    pallas_call x1, Pallas kernels, backward(): pl.pallas_call(backward_kernel, name='backward_layers', out_shape=(shape(...  179 us
    pallas_call x1, Pallas kernels, forward(): pl.pallas_call(forward_kernel, name='forward_layers', out_shape=(shape((2...  168 us
    pallas_call x1, Pallas kernels, run_experts(): pl.pallas_call(experts_kernel, name='experts', out_shape=(shape((T, D), b...  142 us
    unnamed x42, local copies, waits for them, and re-layouts  12.1 us

profile of v4, /device:TPU:29, one launch (start us, length us, event | category | flops | bytes accessed | tf_op | source)
XLA Modules:
  0.0 545.0 jit_solution(11927954793794876216)
XLA Ops:
  1.4 4.6 gather_fusion
  8.5 11.0 %gather_small.1 = (f32[4,32,128]{2,1,0:T(8,128)}, s32[4,8,2,128]{3,2,1,0:T(2,128)}) custom-call(f32[32,128]{1,0:T(8,128)} %bitcast_convert_fusion.1.small_ref, s32[2,128]{1,0:T(2,128)} %fusion.12.slots_ref), custom_call_target="tpu_custom_call" | custom-call | tf_op jit(solution)/shard_map/gather_small/pallas_call | solution.py:454
  19.6 0.9 copy.59
  20.7 0.8 fusion.2.table_ref
  21.5 0.9 copy.56
  22.5 0.7 reshape.158.gains_ref
  23.2 167.5 %forward_layers.1 = (bf16[2,128,768]{2,1,0:T(8,128)(2,1)}, bf16[2,128,768]{2,1,0:T(8,128)(2,1)}, bf16[2,128,768]{2,1,0:T(8,128)(2,1)}, f32[2,128,768]{2,1,0:T(8,...) custom-call(bf16[128,768]{1,0:T(8,128)(2,1)} %bitcast.74, ...), custom_call_target="tpu_custom_call" | custom-call | tf_op jit(solution)/shard_map/forward_layers/pallas_call | solution.py:1017
  190.7 2.0 slice_bitcast_fusion
  193.4 0.9 copy.38
  194.6 0.7 copy.37
  195.3 141.9 %experts.1 = (bf16[128,768]{1,0:T(8,128)(2,1)}, f32[128,768]{1,0:T(8,128)}, f32[24,768]{1,0:T(8,128)}, bf16[2,768,768]{2,1,0:T(8,128)(2,1)}, f32[2,768,768]{2,1,0:T(8,128)}) custom-call(bf16[128,768]{1,0:T(8,128)(2,1)} %get-tuple-element.49.normed_ref, f32[128,768]{1,0:T(8,128)} %get-tuple-element.110.mid_ref, f32[4,768]{1,0:T(4,128)} %reshape.158.gains_ref, ...), custom_call_target="tpu_custom_call" | custom-call | tf_op jit(solution)/shard_map/experts/pallas_call | solution.py:2004
  337.6 1.2 copy.41.act_hbm
  339.5 179.0 %backward_layers.1 = (f32[128,768]{1,0:T(8,128)}, bf16[2,8,192,384]{3,2,1,0:T(8,128)(2,1)}, bf16[8,192,384]{2,1,0:T(8,128)(2,1)}, bf16[8,96,768]{2,1,0:T(8,128)(...) custom-call(f32[128,768]{1,0:T(8,128)} %get-tuple-element.55.mid_grad_ref, ...), custom_call_target="tpu_custom_call" | custom-call | tf_op jit(solution)/shard_map/backward_layers/pallas_call | solution.py:1615
  519.2 0.9 fusion.14
  520.7 2.1 convert_bitcast_fusion
  523.4 2.1 slice.63
  525.5 1.1 slice.64
  527.4 1.7 copy.48
  529.1 0.8 copy-done.2
  529.9 2.8 convert_element_type.77
  532.7 1.7 bitcast_convert_fusion
  534.9 1.2 copy.45
  536.9 1.4 dynamic-slice_bitcast_fusion
  539.8 4.8 copy.63
  (77 shorter events, 11.1 us)
Async XLA Ops:
  0.6 0.7 copy-start
  1.3 4.6 copy-start.12
  1.3 6.0 %copy-start.11 = (bf16[192,16]{0,1:T(8,128)(2,1)S(1)}, bf16[192,16]{0,1:T(8,128)(2,1)}, u32[]{:S(2)}) copy-start(bf16[192,16]{0,1:T(8,128)(2,1)} %param.23) | copy-start | bytes 18436
  1.3 6.2 %copy-start.14 = (bf16[2,192]{1,0:T(2,128)(2,1)S(1)}, bf16[2,192]{1,0:T(2,128)(2,1)}, u32[]{:S(2)}) copy-start(bf16[2,192]{1,0:T(2,128)(2,1)} %param.15) | copy-start | bytes 2308
  1.3 6.3 %copy-start.15 = (bf16[2,192]{1,0:T(2,128)(2,1)S(1)}, bf16[2,192]{1,0:T(2,128)(2,1)}, u32[]{:S(2)}) copy-start(bf16[2,192]{1,0:T(2,128)(2,1)} %param.20) | copy-start | bytes 2308
  1.3 6.4 %copy-start.13 = (bf16[2,8,12]{2,1,0:T(8,128)(2,1)S(1)}, bf16[2,8,12]{2,1,0:T(8,128)(2,1)}, u32[]{:S(2)}) copy-start(bf16[2,8,12]{2,1,0:T(8,128)(2,1)} %param.18) | copy-start | bytes 1156
  194.6 0.7 copy-start.3
  195.3 141.9 %copy-start.6 = (bf16[128,3072]{1,0:T(8,128)(2,1)S(1)}, bf16[128,3072]{1,0:T(8,128)(2,1)}, u32[]{:S(2)}) copy-start(bf16[128,3072]{1,0:T(8,128)(2,1)} %get-tuple-element.64) | copy-start | bytes 2359300
  525.5 1.7 copy-start.5
  527.4 2.5 copy-start.2
  529.9 2.8 copy-start.4
  532.7 2.3 copy-start.7
  532.7 3.4 copy-start.9
  532.7 5.6 %copy-start.10 = (f32[24,128]{1,0:T(8,128)S(1)}, f32[24,128]{1,0:T(8,128)}, u32[]{:S(2)}) copy-start(f32[24,128]{1,0:T(8,128)} %get-tuple-element.82) | copy-start | bytes 36868
  532.7 6.4 %copy-start.8 = (bf16[128,768]{1,0:T(8,128)(2,1)S(1)}, bf16[128,768]{1,0:T(8,128)(2,1)}, u32[]{:S(2)}) copy-start(bf16[128,768]{1,0:T(8,128)(2,1)} %get-tuple-element.54) | copy-start | bytes 589828
  539.8 4.8 copy-start.1

commit v5 on v4

--- a/solution.py
+++ b/solution.py
@@ -416,61 +416,16 @@
     return copy
 
 
-def small_kernel(groups, small_ref, slots_ref, small_out, slots_out, zs, zr, ps, pr, lsem):
-    e, s = place()
-    others = [(e, lax.rem(s + k, groups)) for k in range(1, groups)]
-    around = [(lax.rem(e + k, 8), s) for k in range(1, 8)]
-    local = [
-        pltpu.make_async_copy(small_ref, small_out.at[s], lsem.at[0]),
-        pltpu.make_async_copy(slots_ref, slots_out.at[s, e], lsem.at[1]),
-    ]
-    for copy in local:
-        copy.start()
-    greet(others + around)
-    sent, first = [], []
-    for k, device in enumerate(others):
-        push(sent, small_ref, small_out.at[s], zs.at[0, k], zr.at[0, k], device)
-        first.append(
-            push(sent, slots_ref, slots_out.at[s, e], zs.at[1, k], zr.at[1, k], device)
-        )
-    for copy in local:
-        copy.wait()
-    for copy in first:
-        copy.wait_recv()
-    column = slots_out.at[:, e]
-    for k, device in enumerate(around):
-        push(sent, column, column, ps.at[k], pr.at[k], device)
-    for copy in sent:
-        if all(copy is not other for other in first):
-            copy.wait_recv()
-    for copy in sent:
-        copy.wait_send()
-
-
-def gather_small(small, slots):
-    groups = lax.axis_size("shard")
-    vmem = pl.BlockSpec(memory_space=VMEM)
-    sem = pltpu.SemaphoreType.DMA
-    return pl.pallas_call(
-        functools.partial(small_kernel, groups),
-        name="gather_small",
-        out_shape=(
-            jax.ShapeDtypeStruct((groups,) + small.shape, small.dtype),
-            jax.ShapeDtypeStruct((groups, 8) + slots.shape, slots.dtype),
-        ),
-        in_specs=[vmem, vmem],
-        out_specs=(vmem, vmem),
-        scratch_shapes=[sem((2, 3)), sem((2, 3)), sem((7,)), sem((7,)), sem((2,))],
-        compiler_params=pltpu.CompilerParams(collective_id=1, has_side_effects=True),
-    )(small, slots)
-
-
 def norm_rows(inputs, gain):
     return inputs * lax.rsqrt(jnp.mean(inputs * inputs, axis=-1, keepdims=True) + epsilon) * gain
 
 
 def dot_rows(left, right):
     return lax.dot_general(left, right, (((1,), (1,)), ((), ())), preferred_element_type=single)
+
+
+def dot_columns(left, right):
+    return lax.dot_general(left, right, (((0,), (0,)), ((), ())), preferred_element_type=single)
 
 
 def loop(count, body):
@@ -560,8 +515,9 @@
 
 def forward_kernel(
     hidden_ref,
-    gains_ref,
-    table_ref,
+    small_ref,
+    buckets_ref,
+    routes_ref,
     qkv_hbm,
     out_hbm,
     up_hbm,
@@ -571,13 +527,17 @@
     normed_out,
     query_out,
     attended_out,
-    mid_out,
+    mid_first_out,
+    mid_second_out,
     dense_normed_out,
     pre_out,
     act_out,
     one_out,
     peak_out,
     moe_normed_out,
+    gains_ref,
+    router_out,
+    slots_out,
     qkv0_out,
     qkv1_out,
     proj0_out,
@@ -588,6 +548,10 @@
     probs_out,
     up_own,
     cot_all,
+    small_all,
+    table_ref,
+    slots_own,
+    act,
     w_qkv0,
     w_qkv1,
     w_out0,
@@ -619,6 +583,12 @@
     ns,
     nr,
     outs_sem,
+    small_s,
+    small_r,
+    slot_zs,
+    slot_zr,
+    slot_ps,
+    slot_pr,
 ):
     e, s = place()
     core = lax.rem(e, 2)
@@ -719,10 +689,91 @@
         own[c].wait()
         kept.append(local(chunks[c][1], weight_outs[c], outs_sem.at[c]))
 
-    greet([(at_core, s), (at_x, s), (at_y, s)] + [(e, other) for other in others])
+    plane = Plane()
+    cot_groups = [s] + sources
+    cot_gathers = [
+        PlaneGather(plane, functools.partial(cot_block, g), ns.at[k], nr.at[k])
+        for k, g in enumerate(cot_groups)
+    ]
+
+    def cot_first(k):
+        plane.arrived(cot_block(s, e), gr.at[k - 1])
+        cot_gathers[k].first()
+
+    experts = lax.broadcasted_iota(jnp.int32, (16, T), 0)
+    chosen = [experts == routes_ref[r : r + 1, :] for r in range(2)]
+    marks = jnp.where(chosen[0] | chosen[1], 1.0, 0.0).astype(bfloat)
+    earlier = jnp.where(
+        lax.broadcasted_iota(jnp.int32, (T, T), 0) < lax.broadcasted_iota(jnp.int32, (T, T), 1),
+        1.0,
+        0.0,
+    ).astype(bfloat)
+    before = jnp.dot(marks, earlier, preferred_element_type=single)
+    slots_own[...] = jnp.zeros_like(slots_own)
+    for r in range(2):
+        rank = jnp.sum(jnp.where(chosen[r], before, 0.0), axis=0, keepdims=True)
+        slots_own[r : r + 1, :] = routes_ref[r : r + 1, :] * CAP + rank.astype(jnp.int32)
+    slots_out[s, e] = slots_own[...]
+    own_cot = local(cot_hbm, cot_block(s, e), gs.at[3])
+    small_all[s] = small_ref[...]
+
+    greet([(d, s) for d in plane.around] + [(e, other) for other in others])
+    smalls = [
+        push(sent, small_ref, small_all.at[s], small_s.at[k], small_r.at[k], (e, others[k]))
+        for k in range(3)
+    ]
     z_send(0)
+    for k in range(3):
+        push(sent, slots_own, slots_out.at[s, e], slot_zs.at[k], slot_zr.at[k], (e, others[k]))
+    own_cot.wait()
+    cot_gathers[0].first()
     z_send(1)
     z_send(2)
+    reshard = []
+
+    def bulk():
+        for c in range(3, 6):
+            z_send(c)
+        for k in range(3):
+            push(sent, cot_hbm, cot_block(s, e), gs.at[k], gr.at[k], (e, others[k]))
+        reshard.extend([
+            push(
+                sent,
+                expert_up_hbm.at[:, :, lane_block(others[k], 768)],
+                up_own.at[:, row_block(s, 192), :],
+                us.at[k],
+                ur.at[k],
+                (e, others[k]),
+            )
+            for k in range(3)
+        ])
+        kept.append(
+            local(
+                expert_up_hbm.at[:, :, lane_block(s, 768)],
+                up_own.at[:, row_block(s, 192), :],
+                us.at[3],
+            )
+        )
+
+    def slots_plane():
+        for k in range(3):
+            plane.arrived(slots_own, slot_zr.at[k])
+        column = slots_out.at[:, e]
+        for k, d in enumerate(plane.around):
+            push(sent, column, column, slot_ps.at[k], slot_pr.at[k], (d, s))
+
+    for copy in smalls:
+        copy.wait_recv()
+    biases = []
+    for z in range(4):
+        lanes = slice(192 * z, 192 * (z + 1))
+        gains_ref[:, lanes] = small_all[z, :4, :192]
+        router_out[:, lanes] = small_all[z, 16:32, :192].astype(bfloat)
+        biases.append(small_all[z, 8:16, : 2 * H])
+    bucket_marks_here = jnp.where(
+        lax.broadcasted_iota(jnp.int32, (NB, TOE), 0) == buckets_ref[...], 1.0, 0.0
+    ).astype(bfloat)
+    table_ref[...] = dot_columns(jnp.concatenate(biases).astype(bfloat), bucket_marks_here)
 
     def attention(layer, inputs, w_qkv, w_out, work):
         normed = norm_rows(inputs, gains_ref[pl.ds(layer, 1), :]).astype(bfloat)
@@ -730,8 +781,11 @@
         if layer == 0:
             plane_send(0)
             plane_forward(0)
+            plane_send(1)
             core_send(0)
+            plane_forward(1)
             ready(0)
+            bulk()
         else:
             ready(4)
         own_rows = row_block(e, T)
@@ -868,102 +922,58 @@
         kept.append(local(kv.at[layer], kv_out.at[layer], outs_sem.at[6 + layer]))
         kept.append(local(probs.at[layer], probs_out.at[layer], outs_sem.at[8 + layer]))
 
-    def nothing():
-        pass
-
     def work0():
-        plane_send(1)
-        z_send(3)
+        plane_send(2)
+        slots_plane()
 
     def work1():
-        plane_forward(1)
+        cot_gathers[0].second()
 
     def work2():
         core_send(1)
-        plane_send(2)
+        plane_send(3)
 
     def work3():
+        cot_gathers[0].third()
+
+    def work4():
         plane_forward(2)
-        z_send(4)
-        z_send(5)
-
-    def work4():
-        core_send(2)
-        plane_send(3)
-
-    plane = Plane()
-    cot_groups = [s] + sources
-    cot_gathers = []
-    for k, g in enumerate(cot_groups):
-        cot_gathers.append(
-            PlaneGather(plane, functools.partial(cot_block, g), ns.at[k], nr.at[k])
-        )
-
-    def cot_send():
-        for k in range(3):
-            push(sent, cot_hbm, cot_block(s, e), gs.at[k], gr.at[k], (e, others[k]))
-        copy = local(cot_hbm, cot_block(s, e), gs.at[3])
-        copy.wait()
-        cot_gathers[0].first()
-
-    def cot_first(k):
-        plane.arrived(cot_block(s, e), gr.at[k - 1])
-        cot_gathers[k].first()
 
     hidden = hidden_ref[...].astype(single)
     attention(0, hidden, w_qkv0, w_out0, [work0, work1, work2, work3, work4])
     ready(1)
-    mid_out[0] = hidden + jnp.dot(
+    mid_first_out[...] = hidden + jnp.dot(
         attended_out[0], w_out0[...], preferred_element_type=single
     )
-    dense_normed_out[...] = norm_rows(mid_out[0], gains_ref[pl.ds(2, 1), :]).astype(bfloat)
-    reshard = []
-    for k in range(3):
-        reshard.append(
-            push(
-                sent,
-                expert_up_hbm.at[:, :, lane_block(others[k], 768)],
-                up_own.at[:, row_block(s, 192), :],
-                us.at[k],
-                ur.at[k],
-                (e, others[k]),
-            )
-        )
-    kept.append(
-        local(
-            expert_up_hbm.at[:, :, lane_block(s, 768)],
-            up_own.at[:, row_block(s, 192), :],
-            us.at[3],
-        )
-    )
-    cot_send()
+    dense_normed_out[...] = norm_rows(mid_first_out[...], gains_ref[pl.ds(2, 1), :]).astype(bfloat)
+    core_send(2)
+    plane_forward(3)
+    plane_send(4)
+    plane_send(5)
     ready(2)
 
     def up_part(i):
-        lanes = lane_block(i, 512)
+        lanes = slice(768 * i, 768 * (i + 1))
         before = jnp.dot(dense_normed_out[...], w_up[:, lanes], preferred_element_type=single)
         pre_out[:, lanes] = before
-        act_out[:, lanes] = jax.nn.gelu(before).astype(bfloat)
-
-    plane_forward(3)
-    loop(3, up_part)
+        value = jax.nn.gelu(before).astype(bfloat)
+        act[:, lanes] = value
+        for b in range(8):
+            act_out[:, 384 * b + 96 * i : 384 * b + 96 * (i + 1)] = value[:, 96 * b : 96 * (b + 1)]
+
+    for i in range(4):
+        up_part(i)
     core_send(3)
-    plane_send(4)
-    plane_send(5)
-
-    def up_later(i):
-        up_part(i + 3)
-
-    loop(3, up_later)
     plane_forward(4)
     plane_forward(5)
+    cot_first(1)
     ready(3)
-    one_out[...] = mid_out[0]
+    one_out[...] = mid_first_out[...]
 
     def down_part(i):
         rows = row_block(i, 768)
         one_out[...] += jnp.dot(
-            act_out[:, lane_block(i, 768)], w_down[rows, :], preferred_element_type=single
+            act[:, lane_block(i, 768)], w_down[rows, :], preferred_element_type=single
         )
 
     loop(4, down_part)
@@ -971,32 +981,32 @@
     core_send(5)
 
     def work5():
-        cot_first(1)
-        cot_gathers[0].second()
+        cot_first(2)
+        cot_first(3)
+        cot_gathers[1].second()
 
     def work6():
-        cot_first(2)
+        pass
 
     def work7():
-        cot_gathers[0].third()
-        cot_gathers[1].second()
-
-    def work8():
-        cot_first(3)
         cot_gathers[1].third()
         cot_gathers[2].second()
 
-    def work9():
+    def work8():
         cot_gathers[2].third()
         cot_gathers[3].second()
 
+    def work9():
+        cot_gathers[3].third()
+
     attention(1, one_out[...], w_qkv1, w_out1, [work5, work6, work7, work8, work9])
-    cot_gathers[3].third()
     ready(5)
-    mid_out[1] = one_out[...] + jnp.dot(
+    mid_second_out[...] = one_out[...] + jnp.dot(
         attended_out[1], w_out1[...], preferred_element_type=single
     )
-    moe_normed_out[...] = norm_rows(mid_out[1], gains_ref[pl.ds(3, 1), :]).astype(bfloat)
+    moe_normed_out[...] = norm_rows(mid_second_out[...], gains_ref[pl.ds(3, 1), :]).astype(bfloat)
+    for k in range(7):
+        plane.arrived(slots_out.at[:, e], slot_pr.at[k])
     for gather in cot_gathers:
         gather.done()
     for copy in reshard:
@@ -1007,7 +1017,7 @@
         copy.wait_send()
 
 
-def forward(hidden, gains, table, qkv, out, up, down, expert_up, cotangent):
+def forward(hidden, small, buckets, routes, qkv, out, up, down, expert_up, cotangent):
     length = T * lax.axis_size("expert")
     vmem = pl.BlockSpec(memory_space=VMEM)
     anywhere = pl.BlockSpec(memory_space=ANY)
@@ -1021,13 +1031,17 @@
             shape((2, T, D), bfloat),
             shape((2, T, D), bfloat),
             shape((2, T, D), bfloat),
-            shape((2, T, D), single),
+            shape((T, D), single),
+            shape((T, D), single),
             shape((T, D), bfloat),
             shape((T, ff), single),
             shape((T, ff), bfloat),
             shape((T, D), single),
             shape((2 * H, 128), single),
             shape((T, D), bfloat),
+            shape((4, D), single),
+            shape((16, D), bfloat),
+            shape((4, 8, 8, T), jnp.int32),
             shape((D, 3 * D), bfloat),
             shape((D, 3 * D), bfloat),
             shape((D, D), bfloat),
@@ -1039,9 +1053,13 @@
             shape((EXP_DEV, D, 768), bfloat),
             shape((4, 8, T, D), bfloat),
         ),
-        in_specs=[vmem] * 3 + [anywhere] * 6,
-        out_specs=(vmem,) * 10 + (anywhere,) * 10,
+        in_specs=[vmem] * 4 + [anywhere] * 6,
+        out_specs=(vmem,) * 14 + (anywhere,) * 10,
         scratch_shapes=[
+            VMEM((4,) + small.shape, single),
+            VMEM((2 * H, TOE), single),
+            VMEM((8, T), jnp.int32),
+            VMEM((T, ff), bfloat),
             VMEM((D, 3 * D), bfloat),
             VMEM((D, 3 * D), bfloat),
             VMEM((D, D), bfloat),
@@ -1063,11 +1081,14 @@
             sem((4,)), sem((3,)),
             sem((4, 7)), sem((4, 7)),
             sem((10,)),
+            sem((3,)), sem((3,)),
+            sem((3,)), sem((3,)),
+            sem((7,)), sem((7,)),
         ],
         compiler_params=pltpu.CompilerParams(
             collective_id=2, has_side_effects=True, vmem_limit_bytes=56 * 2**20
         ),
-    )(hidden, gains, table, qkv, out, up, down, expert_up, cotangent)
+    )(hidden, small, buckets, routes, qkv, out, up, down, expert_up, cotangent)
 
 
 class SmallReduce:
@@ -1109,6 +1130,15 @@
     return inverse * scaled - inputs * (inverse * inverse * inverse * inner), gain_grad
 
 
+def gelu_both(value):
+    root = math.sqrt(2.0 / math.pi)
+    squared = value * value
+    bend = jnp.tanh(root * value * (1.0 + 0.044715 * squared))
+    half = 0.5 * (1.0 + bend)
+    slope = half + 0.5 * value * (1.0 - bend * bend) * (root * (1.0 + 3 * 0.044715 * squared))
+    return value * half, slope
+
+
 def gelu_slope(value):
     root = math.sqrt(2.0 / math.pi)
     squared = value * value
@@ -1116,10 +1146,6 @@
     return 0.5 * (1.0 + bend) + 0.5 * value * (1.0 - bend * bend) * root * (
         1.0 + 3 * 0.044715 * squared
     )
-
-
-def dot_columns(left, right):
-    return lax.dot_general(left, right, (((0,), (0,)), ((), ())), preferred_element_type=single)
 
 
 def backward_kernel(
@@ -1130,9 +1156,10 @@
     gains_ref,
     query_ref,
     pre_ref,
-    marks_ref,
+    buckets_ref,
     small_ref,
     peak_ref,
+    early_hbm,
     normed_hbm,
     attended_hbm,
     dense_normed_hbm,
@@ -1213,16 +1240,9 @@
 
     own_parts = [
         load(source, xg.at[n, own_rows, :], 11 + n)
-        for n, source in enumerate(
-            (
-                normed_hbm.at[1],
-                attended_hbm.at[1],
-                normed_hbm.at[0],
-                attended_hbm.at[0],
-                dense_normed_hbm,
-            )
-        )
+        for n, source in ((2, normed_hbm.at[0]), (3, attended_hbm.at[0]), (4, dense_normed_hbm))
     ]
+    got_early = load(early_hbm, xg.at[0:2], 12)
     own_act = load(act_hbm.at[:, lane_block(e, 384)], gx.at[3, own_rows, :], 16)
     greet([(d, s) for d in p.around] + [(e, other) for other in p.others])
 
@@ -1244,14 +1264,7 @@
             p, lambda who: xg.at[n, row_block(who, T), :], gs.at[n], gr.at[n]
         )
 
-    gathers = [rows_gather(n) for n in range(6)]
-    for copy in own_parts:
-        copy.wait()
-    gathers[0].first()
-    gathers[1].first()
-
-    exchanges = {}
-
+    gathers = {n: rows_gather(n) for n in range(2, 6)}
     def exchange_start(j, source):
         if j == 3:
             own_act.wait()
@@ -1374,6 +1387,9 @@
             turned = total.T.astype(bfloat)
             grads[:, D + 256 * part : D + 256 * (part + 1)] = turned[:, :256]
             grads[:, 2 * D + 256 * part : 2 * D + 256 * (part + 1)] = turned[:, 256:]
+
+        if layer == 1:
+            exchange_start(3, act_hbm)
 
         for part in range(3):
 
@@ -1457,10 +1473,6 @@
     reloads = {}
 
     def part0():
-        gathers[0].second()
-        gathers[1].second()
-        exchange_start(3, act_hbm)
-        gathers[4].first()
         for k in range(3):
             reshard.append(
                 p.push(
@@ -1480,17 +1492,14 @@
         )
 
     def part1():
-        gathers[0].third()
-        gathers[1].third()
         peaks.middle(peak_m)
 
     def part2():
-        gathers[4].second()
-        gathers[2].first()
-        gathers[3].first()
+        for copy in own_parts:
+            copy.wait()
 
     def part3():
-        gathers[4].third()
+        gathers[4].first()
         peaks.finish(peak_m, peak_out)
 
     reshard, reshard_own = [], []
@@ -1515,8 +1524,7 @@
 
     loop(6, slope_part)
     exchange_start(2, gsrc.at[2])
-    gathers[2].second()
-    gathers[3].second()
+    gathers[4].second()
     gathers[5].second()
     got_up.wait()
     dense_grad = dot_rows(gsrc[2], w_wide[...])
@@ -1529,34 +1537,27 @@
         p, early, early_z, early_p, jnp.add, (szs.at[1], szr.at[1], sps.at[1], spr.at[1])
     )
     small.start()
-    gathers[0].done()
-    gathers[1].done()
+    gathers[4].third()
+    gathers[5].third()
+    got_early.wait()
     tile_attention(1)
 
     def part4():
-        gathers[5].third()
-        gathers[2].third()
-        gathers[3].third()
         gathers[4].done()
         tile_up()
 
     def part5():
         gathers[5].done()
         tile_down()
+
+    def part6():
+        small.middle(early_m)
+
+    def part7():
+        gathers[2].first()
+        gathers[3].first()
         z_finish(0, zb.at[0], zin.at[0], 192, att_out.at[1])
         gather_att1.first()
-        small.middle(early_m)
-
-    def part6():
-        z_finish(2, zb.at[2], zin.at[2], 192, up_out)
-        gather_up.first()
-        gather_att1.second()
-
-    def part7():
-        z_finish(3, zb_down, zin_down, 96, down_out)
-        gather_down.first()
-        gather_up.second()
-        gather_att1.third()
 
     normed_grad = attention(0, layer_grad[...], [part4, part5, part6, part7])
     input_grad, gain_grad = norm_pull(
@@ -1568,7 +1569,7 @@
         late[i : i + 1, :] = gain_grad[:, 128 * i : 128 * (i + 1)]
     late[8:32, :NB] = lax.dot_general(
         biases[...],
-        marks_ref[...].astype(single),
+        jnp.where(lax.broadcasted_iota(jnp.int32, (NB, TOE), 0) == buckets_ref[...], 1.0, 0.0),
         (((1,), (1,)), ((), ())),
         precision=lax.Precision.HIGHEST,
         preferred_element_type=single,
@@ -1577,14 +1578,25 @@
         p, late, late_z, late_p, jnp.add, (szs.at[2], szr.at[2], sps.at[2], spr.at[2])
     )
     tail.start()
+    gathers[2].second()
+    gathers[3].second()
+    z_finish(2, zb.at[2], zin.at[2], 192, up_out)
+    gather_up.first()
+    gather_att1.second()
+    gathers[2].third()
+    gathers[3].third()
+    z_finish(3, zb_down, zin_down, 96, down_out)
+    gather_down.first()
+    gather_att1.third()
+    gather_up.second()
     gathers[2].done()
     gathers[3].done()
     tile_attention(0)
+    tail.middle(late_m)
+    small.finish(early_m, small_out)
+    gather_up.third()
     gather_down.second()
-    gather_up.third()
-    small.finish(early_m, small_out)
     gather_down.third()
-    tail.middle(late_m)
     z_finish(1, zb.at[1], zin.at[1], 192, att_out.at[0])
     gather_att0.first()
     gather_att1.done()
@@ -1603,7 +1615,7 @@
 
 def backward(
     mid_grad, layer_one, hidden, mid, gains, normed, queries, attended, dense_normed, act, pre_act,
-    marks, small, peak_rows, weights, kv, probs, up_grad,
+    buckets, small, peak_rows, early_rows, weights, kv, probs, up_grad,
 ):
     length = T * lax.axis_size("expert")
     vmem = pl.BlockSpec(memory_space=VMEM)
@@ -1625,7 +1637,7 @@
             shape(peak_shape, single),
             shape((EXP_DEV, 192, ff), bfloat),
         ),
-        in_specs=[vmem] * 10 + [anywhere] * 13,
+        in_specs=[vmem] * 10 + [anywhere] * 14,
         out_specs=(vmem,) * 7 + (anywhere,),
         scratch_shapes=[
             VMEM((D, ff), bfloat),
@@ -1672,8 +1684,8 @@
             collective_id=3, has_side_effects=True, vmem_limit_bytes=60 * 2**20
         ),
     )(
-        mid_grad, layer_one, hidden, mid, gains, queries, pre_act, marks, small, peak_rows, normed,
-        attended, dense_normed, act, *weights, kv, probs, up_grad,
+        mid_grad, layer_one, hidden, mid, gains, queries, pre_act, buckets, small, peak_rows,
+        early_rows.reshape(2, length, D), normed, attended, dense_normed, act, *weights, kv, probs, up_grad,
     )
 
 
@@ -1681,19 +1693,20 @@
     normed_ref,
     mid_ref,
     gains_ref,
-    router_ref,
     router_turned_ref,
     slots_ref,
-    slot_columns_ref,
     own_cot_ref,
     cot_hbm,
     up_hbm,
     down_hbm,
+    normed_hbm,
+    attended_hbm,
     hidden_out,
     mid_grad_out,
     small_out,
     up_grad_out,
     down_grad_out,
+    early_rows,
     normed_all,
     cots,
     w_up,
@@ -1733,6 +1746,8 @@
     ozs,
     ozr,
     loads,
+    early_s,
+    early_r,
 ):
     p = Plane()
     e, s = p.e, p.s
@@ -1746,6 +1761,10 @@
     got_cots = [load(cot_hbm.at[groups[k]], cots.at[k], k) for k in range(2)]
     got_up = load(up_hbm, w_up, 4)
     got_down = load(down_hbm, w_down, 5)
+    own_early = [
+        load(source.at[1], early_rows.at[i, e], 6 + i)
+        for i, source in enumerate((normed_hbm, attended_hbm))
+    ]
     normed_all[s, e] = normed_ref[...]
     greet([(d, s) for d in p.around] + [(e, other) for other in p.others])
     mine = normed_all.at[s, e]
@@ -1758,13 +1777,22 @@
 
     gathers = [gather(k) for k in range(4)]
     gathers[0].first()
+    early = [
+        PlaneGather(
+            p, functools.partial(lambda i, who: early_rows.at[i, who], i), early_s.at[i], early_r.at[i]
+        )
+        for i in range(2)
+    ]
+    for i in range(2):
+        own_early[i].wait()
+        early[i].first()
 
     ids = 2 * e * CAP + lax.broadcasted_iota(jnp.int32, (2 * CAP, T), 0)
     expert_low = CAP * lax.broadcasted_iota(jnp.int32, (16, T), 0)
 
     def route_masks(g, who):
-        at = (g * 8 + who) * 2
-        first, second = slots_ref[pl.ds(at, 1), :], slots_ref[pl.ds(at + 1, 1), :]
+        both = slots_ref[g, who]
+        first, second = both[:1], both[1:2]
         return first, second, ids == first, ids == second
 
     def select_cots(k):
@@ -1778,7 +1806,8 @@
             for j in range(2):
                 raw[j, g, row_block(who, CAP), :] = picked[j * CAP : (j + 1) * CAP]
 
-        loop(8, one)
+        for who in range(8):
+            one(who)
         if k < 2:
             got_cots.append(load(cot_hbm.at[groups[k + 2]], cots.at[k], k + 2))
 
@@ -1812,35 +1841,36 @@
                 rows[j, g, row_block(who, CAP), :] = picked[part]
                 gates[j, g, row_block(who, CAP), :] = jnp.broadcast_to(gate[part], (CAP, 128))
 
-        loop(8, one)
+        for who in range(8):
+            one(who)
 
     def compute(k):
         g = groups[k]
 
         def one(j):
             before = jnp.dot(rows[j, g], w_up[j], preferred_element_type=single)
-            act = jax.nn.gelu(before).astype(bfloat)
+            act, slope = gelu_both(before)
+            act = act.astype(bfloat)
             acts[j, g] = act
             gate = gates[j, g][:, :1]
             cot = raw[j, g].astype(single)
             weighted = (gate * cot).astype(bfloat)
             gated[j, g] = weighted
             act_grad = dot_rows(weighted, w_down[j])
-            pre_grad = (act_grad * gelu_slope(before)).astype(bfloat)
+            pre_grad = (act_grad * slope).astype(bfloat)
             pre_grads[j, g] = pre_grad
             row_grad = dot_rows(pre_grad, w_up[j])
             row_send[g, j] = row_grad.astype(bfloat).reshape(8, CAP, D)
             out = jnp.dot(act, w_down[j], preferred_element_type=single)
             out_send[g, j] = (gate * out).astype(bfloat).reshape(8, CAP, D)
-            slot_grads[g, pl.ds(j, 1), :] = lax.dot_general(
-                jnp.ones((8, D), single),
-                out * cot,
-                (((1,), (1,)), ((), ())),
-                precision=lax.Precision.HIGHEST,
-                preferred_element_type=single,
-            )[:1]
-
-        loop(2, one)
+            product = out * cot
+            folded = product[:, :128]
+            for i in range(1, D // 128):
+                folded = folded + product[:, 128 * i : 128 * (i + 1)]
+            slot_grads[g, j : j + 1, :] = jnp.sum(folded.T, axis=0, keepdims=True)
+
+        for j in range(2):
+            one(j)
 
     def give_back(k, source, target, send_sems, recv_sems):
         g = groups[k]
@@ -1853,7 +1883,6 @@
     def step(k):
         select_rows(k)
         compute(k)
-        give_back(k, row_send, row_back, rs, rr)
 
     def arrive(k):
         p.arrived(mine, nr.at[k - 1])
@@ -1864,29 +1893,38 @@
     gathers[0].second()
     arrive(1)
     gathers[0].third()
+    arrive(2)
+    early[0].second()
+    early[1].second()
+    arrive(3)
+    gathers[0].done()
     gathers[1].second()
-    arrive(2)
-    gathers[0].done()
-    gathers[1].third()
-    gathers[2].second()
-    arrive(3)
     got_up.wait()
     got_down.wait()
     step(0)
-    gathers[2].third()
+    gathers[1].third()
+    gathers[2].second()
     gathers[3].second()
+    early[0].third()
+    early[1].third()
     select_cots(1)
     gathers[1].done()
     step(1)
+    give_back(1, row_send, row_back, rs, rr)
+    gathers[2].third()
     gathers[3].third()
     select_cots(2)
     gathers[2].done()
     step(2)
+    give_back(2, row_send, row_back, rs, rr)
     select_cots(3)
     gathers[3].done()
     step(3)
-    for k in range(4):
+    give_back(3, row_send, row_back, rs, rr)
+    for k in (1, 2, 3):
         give_back(k, out_send, out_back, os, orr)
+    give_back(0, row_send, row_back, rs, rr)
+    give_back(0, out_send, out_back, os, orr)
     for k in range(3):
         p.push(
             slot_grads.at[p.others[k]], slot_z.at[k], ss.at[k], sr.at[k], (e, p.others[k])
@@ -1902,7 +1940,7 @@
         inputs = acts[j].reshape(4 * 8 * CAP, -1)
         down_grad_out[j, :, lanes] = dot_columns(
             inputs, gated[j, :, :, lanes].reshape(4 * 8 * CAP, 256)
-        )
+        ).astype(bfloat)
 
     loop(3, weight_grads)
     total = slot_grads[s]
@@ -1916,11 +1954,14 @@
 
     slot_lanes = lax.broadcasted_iota(jnp.int32, (T, 16 * CAP), 1)
 
+    def slot_columns(g):
+        return slots_ref[g, e].astype(single).T.astype(jnp.int32)
+
     def collect(k, back, recv_sems, part, z_in, z_send, z_recv):
         g = groups[k]
         for i in range(7):
             p.arrived(back.at[g, e], recv_sems.at[k, i])
-        columns = slot_columns_ref[g]
+        columns = slot_columns(g)
         marks = jnp.where(
             (columns[:, :1] == slot_lanes) | (columns[:, 1:2] == slot_lanes), 1.0, 0.0
         ).astype(bfloat)
@@ -1931,7 +1972,7 @@
         if k:
             p.push(part.at[g], z_in.at[k - 1], z_send.at[k - 1], z_recv.at[k - 1], (e, g))
 
-    for k in (1, 2, 3, 0):
+    for k in (1, 2, 3):
         collect(k, row_back, rr, row_part, row_z, rzs, rzr)
 
     def weight_later(i):
@@ -1944,8 +1985,8 @@
     turned = pltpu.roll(
         slot_plane[...].reshape(64, 8 * CAP), lax.rem(8 * CAP - CAP * e, 8 * CAP), 1
     )
-    logits = jnp.dot(normed_ref[...], router_ref[...], preferred_element_type=single)
-    columns = slot_columns_ref[s]
+    logits = dot_rows(normed_ref[...], router_turned_ref[...])
+    columns = slot_columns(s)
     expert_lanes = CAP * lax.broadcasted_iota(jnp.int32, (T, 16), 1)
     picks, chosen, grads = [], [], []
     small_lanes = lax.broadcasted_iota(jnp.int32, (T, CAP), 1)
@@ -1971,6 +2012,9 @@
     small_out[...] = jnp.zeros_like(small_out)
     small_out[:16, :] = dot_columns(logit_grad, normed_ref[...])
     normed_grad = jnp.dot(logit_grad, router_turned_ref[...], preferred_element_type=single)
+    for k in (1, 2, 3):
+        collect(k, out_back, orr, out_part, out_z, ozs, ozr)
+    collect(0, row_back, rr, row_part, row_z, rzs, rzr)
     normed_grad = normed_grad + row_part[s].astype(single)
     for k in range(3):
         p.arrived(row_z.at[k], rzr.at[k])
@@ -1979,19 +2023,20 @@
     small_out[16:17, :] = gain_grad
     mid_grad_out[...] = own_cot_ref[...].astype(single) + input_grad
 
-    for k in (1, 2, 3, 0):
-        collect(k, out_back, orr, out_part, out_z, ozs, ozr)
+    collect(0, out_back, orr, out_part, out_z, ozs, ozr)
     result = mid_ref[...] + out_part[s].astype(single)
     for k in range(3):
         p.arrived(out_z.at[k], ozr.at[k])
         result = result + out_z[k].astype(single)
     hidden_out[...] = result.astype(bfloat)
+    for gather in early:
+        gather.done()
     for copy in p.sent:
         copy.wait_send()
 
 
 def run_experts(
-    normed, mid, gains, router, slots, slot_columns, own_cot, cots, up_own, expert_down
+    moe_normed, mid, gains, router, slots, own_cot, cots, up_own, expert_down, normed, attended
 ):
     vmem = pl.BlockSpec(memory_space=VMEM)
     anywhere = pl.BlockSpec(memory_space=ANY)
@@ -2009,10 +2054,11 @@
             shape((T, D), single),
             shape((24, D), single),
             shape((EXP_DEV, D, width), bfloat),
-            shape((EXP_DEV, width, D), single),
+            shape((EXP_DEV, width, D), bfloat),
+            shape((2, 8, T, D), bfloat),
         ),
-        in_specs=[vmem] * 8 + [anywhere] * 3,
-        out_specs=(vmem,) * 5,
+        in_specs=[vmem] * 6 + [anywhere] * 5,
+        out_specs=(vmem,) * 5 + (anywhere,),
         scratch_shapes=[
             VMEM((4, 8, T, D), bfloat),
             VMEM((2, 8, T, D), bfloat),
@@ -2044,15 +2090,170 @@
             sem((7,)), sem((7,)),
             sem((3,)), sem((3,)),
             sem((3,)), sem((3,)),
-            sem((6,)),
+            sem((8,)),
+            sem((2, 7)), sem((2, 7)),
         ],
         compiler_params=pltpu.CompilerParams(
             collective_id=4, has_side_effects=True, vmem_limit_bytes=60 * 2**20
         ),
     )(
-        normed, mid, gains, router, router.T, slots, slot_columns, own_cot, cots, up_own,
-        expert_down,
-    )
+        moe_normed, mid, gains, router, slots, own_cot, cots, up_own, expert_down, normed, attended
+    )
+
+
+def finish_kernel(
+    att_hbm,
+    up_hbm,
+    down_hbm,
+    expert_up_hbm,
+    expert_down_hbm,
+    small_hbm,
+    late_hbm,
+    peak_hbm,
+    grad_hbm,
+    result_hbm,
+    qkv_out,
+    out_out,
+    up_out,
+    down_out,
+    expert_up_out,
+    expert_down_out,
+    attn_gain_out,
+    mlp_gain_out,
+    bias_out,
+    router_out,
+    clip_out,
+    grad_out,
+    result_out,
+    att,
+    up,
+    down,
+    expert_up,
+    expert_down,
+    small_ref,
+    late_ref,
+    peak_ref,
+    grad,
+    qkv_wide,
+    out_wide,
+    up_wide,
+    down_wide,
+    expert_up_wide,
+    expert_down_wide,
+    turned,
+    in_sems,
+    out_sems,
+):
+    s = lax.axis_index("shard")
+
+    def start(source, target, sem):
+        copy = pltpu.make_async_copy(source, target, sem)
+        copy.start()
+        return copy
+
+    got = [
+        start(source, target, in_sems.at[i])
+        for i, (source, target) in enumerate(
+            (
+                (expert_down_hbm, expert_down),
+                (expert_up_hbm, expert_up),
+                (att_hbm, att),
+                (up_hbm, up),
+                (down_hbm, down),
+                (grad_hbm, grad),
+                (small_hbm, small_ref),
+                (late_hbm, late_ref),
+                (peak_hbm, peak_ref),
+                (result_hbm, result_out),
+            )
+        )
+    ]
+    put = []
+
+    def widen(i):
+        rows = row_block(i, 128)
+        for j in range(EXP_DEV):
+            expert_down_wide[j, rows, :] = expert_down[j, rows, :].astype(single)
+
+    def widen_up(i):
+        lanes = lane_block(i, 384)
+        for j in range(EXP_DEV):
+            expert_up_wide[j, :, lanes] = expert_up[j, :, lanes].astype(single)
+
+    def widen_down(i):
+        down_wide[row_block(i, 96), :] = down[i].astype(single)
+
+    got[0].wait()
+    loop(expert_down.shape[1] // 128, widen)
+    put.append(start(expert_down_wide, expert_down_out, out_sems.at[0]))
+    got[1].wait()
+    loop(expert_up.shape[2] // 384, widen_up)
+    put.append(start(expert_up_wide, expert_up_out, out_sems.at[1]))
+    got[2].wait()
+    for layer in range(2):
+        for b in range(6):
+            qkv_wide[layer, :, 384 * b : 384 * (b + 1)] = att[layer, b].astype(single)
+        for b in range(2):
+            out_wide[layer, :, 384 * b : 384 * (b + 1)] = att[layer, 6 + b].astype(single)
+    put.append(start(qkv_wide, qkv_out, out_sems.at[2]))
+    put.append(start(out_wide, out_out, out_sems.at[3]))
+    got[3].wait()
+    for b in range(8):
+        up_wide[:, 384 * b : 384 * (b + 1)] = up[b].astype(single)
+    put.append(start(up_wide, up_out, out_sems.at[4]))
+    got[4].wait()
+    loop(8, widen_down)
+    put.append(start(down_wide, down_out, out_sems.at[5]))
+
+    for copy in got[5:]:
+        copy.wait()
+    grad_out[...] = grad[...][:, None, :]
+    part = D // 4
+    back = lax.rem(D - part * s, D)
+    first_gain = jnp.concatenate([late_ref[i : i + 1, :] for i in range(6)], axis=1)
+    gains = jnp.concatenate([first_gain, small_ref[16:19, :], jnp.zeros((4, D), single)])
+    gains = pltpu.roll(gains, back, 1)[:, :part]
+    attn_gain_out[0:1, :] = gains[0:1]
+    attn_gain_out[1:2, :] = gains[2:3]
+    mlp_gain_out[0:1, :] = gains[3:4]
+    mlp_gain_out[1:2, :] = gains[1:2]
+    turned[:, :16] = small_ref[:16, :].T
+    router_out[...] = turned[row_block(s, part), :16].T
+    turned[:128, : 2 * H] = late_ref[8:32, :].T
+    biases = turned[row_block(s, 8), : 2 * H]
+    peaks = peak_ref[...].T[:1, :]
+    clips = jnp.sqrt(clip_limit / jnp.maximum(peaks, clip_limit))
+    for layer in range(2):
+        bias_out[layer] = biases[:, layer * H : (layer + 1) * H]
+        clip_out[layer : layer + 1, :] = clips[:, layer * H : (layer + 1) * H]
+    for copy in put:
+        copy.wait()
+
+
+def finish(att, up, down, expert_up, expert_down, small, late, peaks, grad, result):
+    vmem = pl.BlockSpec(memory_space=VMEM)
+    anywhere = pl.BlockSpec(memory_space=ANY)
+    loaded = (att, up, down, expert_up, expert_down, small, late, peaks, grad)
+    sem = pltpu.SemaphoreType.DMA
+    wide = (
+        (2, 192, 3 * D), (2, 192, D), (192, 8 * 384), (8 * 96, D), expert_up.shape,
+        expert_down.shape,
+    )
+    return pl.pallas_call(
+        finish_kernel,
+        name="finish",
+        out_shape=tuple(
+            jax.ShapeDtypeStruct(dims, single)
+            for dims in wide + ((2, 192), (2, 192), (2, 8, H), (16, 192), (2, H), (T, 1, D))
+        )
+        + (jax.ShapeDtypeStruct(result.shape, bfloat),),
+        in_specs=[anywhere] * 10,
+        out_specs=(anywhere,) * 6 + (vmem,) * 7,
+        scratch_shapes=[VMEM(item.shape, item.dtype) for item in loaded]
+        + [VMEM(dims, single) for dims in wide]
+        + [VMEM((D, 128), single), sem((10,)), sem((6,))],
+        compiler_params=pltpu.CompilerParams(vmem_limit_bytes=60 * 2**20),
+    )(*loaded, result)
 
 
 def shards(
@@ -2073,91 +2274,63 @@
 ):
     block_rows = hidden_in.shape[1]
     length = bucket_table.shape[0]
-    experts = lax.axis_size("expert")
     groups = lax.axis_size("shard")
-    here = lax.axis_index("shard")
-    expert_total = EXP_DEV * experts
-    capacity = 4 * block_rows // expert_total
-
-    expert_ids = jnp.arange(expert_total, dtype=jnp.int32)
-    flat_routes = routes.reshape(-1)
-    marks = (flat_routes[:, None] == expert_ids).astype(bfloat)
-    earlier = jnp.tri(2 * block_rows, k=-1, dtype=bfloat)
-    rank = jnp.sum(matmul(earlier, marks) * marks.astype(single), axis=1).astype(jnp.int32)
-    slots = (flat_routes * capacity + rank).reshape(block_rows, 2).T
-
+
+    def block(values):
+        return jnp.pad(values, ((0, -values.shape[0] % 8), (0, 256 - values.shape[1])))
+
+    part = D // groups
     small = jnp.concatenate(
-        [attn_gain.reshape(-1), mlp_gain.reshape(-1), rel_bias.reshape(-1), router_weight.reshape(-1)]
+        [
+            block(jnp.concatenate([attn_gain, mlp_gain])),
+            block(rel_bias.transpose(1, 0, 2).reshape(NB // groups, 2 * H)),
+            block(router_weight.T),
+        ]
     ).astype(single)
-    part = D // groups
-    used = small.shape[0]
-    small = jnp.pad(small, (0, -used % 1024)).reshape(-1, 128)
-    small, slots_all = gather_small(small, slots)
-    slot_columns = lax.dynamic_index_in_dim(
-        slots_all, lax.axis_index("expert"), 1, keepdims=False
-    ).transpose(0, 2, 1)
-    small = small.reshape(groups, -1)
-    cuts = [0, 4 * part, 4 * part + 2 * (NB // groups) * H, used]
-    gains, bias_weights, router_full = (small[:, cuts[i] : cuts[i + 1]] for i in range(3))
-    gains = gains.reshape(groups, 4, part).transpose(1, 0, 2).reshape(4, D)
-    bias_weights = (
-        bias_weights.reshape(groups, 2, NB // groups, H).transpose(1, 0, 2, 3).reshape(2, NB, H)
-    )
-    router_full = router_full.reshape(D, expert_total).astype(bfloat)
-
-    distances = lax.axis_index("expert") * block_rows + block_rows - 1 - jnp.arange(TOE)
-    buckets = jnp.take(bucket_table, jnp.clip(distances, 0, length - 1))
-    toeplitz_marks = (buckets[None] == jnp.arange(NB, dtype=jnp.int32)[:, None]).astype(bfloat)
-    table = jnp.einsum(
-        "lbh,bm->lhm", bias_weights.astype(bfloat), toeplitz_marks, preferred_element_type=single
-    ).reshape(2 * H, TOE)
-
+    backward_table = jnp.pad(bucket_table[::-1], (0, TOE))
+    buckets = lax.dynamic_slice_in_dim(
+        backward_table, length - block_rows * (lax.axis_index("expert") + 1), TOE
+    )[None]
+    cotangent = out_grad.reshape(block_rows, D)
     (
-        normed, queries, attended, mid, dense_normed, pre_act, activation, layer_one, peak_rows,
-        moe_normed, qkv0, qkv1, projection0, projection1, dense_up, dense_down, kv, probs, up_own,
-        upstream_all,
+        normed, queries, attended, mid_first, mid_second, dense_normed, pre_act, activation, layer_one, peak_rows,
+        moe_normed, gains, router, slots, qkv0, qkv1, projection0, projection1, dense_up,
+        dense_down, kv, probs, up_own, cotangents,
     ) = forward(
-        hidden_in.reshape(block_rows, D), gains, table, qkv_weight, out_weight, mlp_up, mlp_down,
-        expert_up, out_grad.reshape(block_rows, D),
-    )
-    hidden_out, mid_grad, small_in, up_grad, expert_down_grad = run_experts(
-        moe_normed, mid[1], gains, router_full, slots_all.reshape(-1, block_rows), slot_columns,
-        out_grad.reshape(block_rows, D), upstream_all, up_own, expert_down,
+        hidden_in.reshape(block_rows, D), small, buckets, routes.reshape(block_rows, 2).T,
+        qkv_weight, out_weight, mlp_up, mlp_down, expert_up, cotangent,
+    )
+    hidden_out, mid_grad, small_in, up_grad, expert_down_low, early_rows = run_experts(
+        moe_normed, mid_second, gains, router, slots, cotangent, cotangents, up_own, expert_down,
+        normed, attended,
     )
     hidden_grad, attention_sum, up_sum, down_sum, small_sum, late_sum, peaks, expert_up_low = (
         backward(
-            mid_grad, layer_one, hidden_in.reshape(block_rows, D), mid[0], gains, normed, queries,
-            attended, dense_normed, spread(activation), pre_act, toeplitz_marks, small_in,
-            peak_rows, (qkv0, qkv1, projection0, projection1, dense_up, dense_down), kv, probs,
+            mid_grad, layer_one, hidden_in.reshape(block_rows, D), mid_first, gains, normed, queries,
+            attended, dense_normed, activation, pre_act, buckets, small_in, peak_rows,
+            early_rows, (qkv0, qkv1, projection0, projection1, dense_up, dense_down), kv, probs,
             up_grad,
         )
     )
-    attention_sum = (
-        attention_sum.transpose(0, 2, 1, 3).reshape(2, part, 4 * D).astype(single)
-    )
-    mlp_up_grad = up_sum.transpose(1, 0, 2).reshape(part, -1).astype(single)
-    mlp_down_grad = down_sum.reshape(-1, D).astype(single)
-
-    def columns(rows):
-        return lax.dynamic_slice_in_dim(rows, here * part, part, rows.ndim - 1)
-
-    first_gain = late_sum[:6].reshape(1, D)
-    rows = columns(small_sum)
-    gain_rows = columns(first_gain)
-    biases = lax.dynamic_slice_in_dim(late_sum[8:32], here * (NB // groups), NB // groups, 1)
-    clip_scales = jnp.sqrt(clip_limit / jnp.maximum(peaks[:, 0].reshape(2, H), clip_limit))
+    (
+        qkv_grad, out_weight_grad, mlp_up_grad, mlp_down_grad, expert_up_grad, expert_down_grad,
+        attn_gain_grad, mlp_gain_grad, rel_bias_grad, router_grad, clip_scales, hidden_grad, hidden_out,
+    ) = finish(
+        attention_sum, up_sum, down_sum, expert_up_low, expert_down_low, small_sum, late_sum, peaks,
+        hidden_grad, hidden_out,
+    )
     return (
         hidden_out.reshape(hidden_in.shape),
         hidden_grad.reshape(hidden_in.shape),
-        jnp.concatenate([gain_rows, rows[expert_total + 1 : expert_total + 2]]),
-        attention_sum[:, :, : 3 * D],
-        attention_sum[:, :, 3 * D :],
-        biases.reshape(2, H, NB // groups).transpose(0, 2, 1),
-        jnp.stack([rows[expert_total + 2], rows[expert_total]]),
+        attn_gain_grad,
+        qkv_grad,
+        out_weight_grad,
+        rel_bias_grad,
+        mlp_gain_grad,
         mlp_up_grad,
         mlp_down_grad,
-        rows[:expert_total].T,
-        expert_up_low.astype(single),
+        router_grad.T,
+        expert_up_grad,
         expert_down_grad,
         clip_scales,
     )

time: 554 us -> 474 us (0.86)
  the two profiles are of different devices: /device:TPU:29 before, /device:TPU:0 now
where the time goes in v5:
time: 474 us; the launch traced here: 465 us
  Pallas kernels  460 us (97%)
    pallas_call x1, Pallas kernels, backward(): pl.pallas_call(backward_kernel, name='backward_layers', out_shape=(shape(...  157 us
    pallas_call x1, Pallas kernels, forward(): pl.pallas_call(forward_kernel, name='forward_layers', out_shape=(shape((2...  149 us
    pallas_call x1, Pallas kernels, run_experts(): pl.pallas_call(experts_kernel, name='experts', out_shape=(shape((T, D), b...  144 us
    pallas_call x1, Pallas kernels, finish(): pl.pallas_call(finish_kernel, name='finish', out_shape=tuple((jax.ShapeDt...  9.98 us

profile of v5, /device:TPU:0, one launch (start us, length us, event | category | flops | bytes accessed | tf_op | source)
XLA Modules:
  0.0 465.2 jit_solution(16519177682012280771)
XLA Ops:
  0.7 0.7 fusion.11
  1.4 0.7 copy.27
  2.1 0.1 reshape.49
  2.1 0.8 rev.3
  2.9 0.1 pad_dynamic-slice_fusion
  3.0 0.6 broadcast_in_dim.3.buckets_ref
  3.6 1.3 fusion.5.small_ref
  4.9 148.8 %forward_layers.1 = (bf16[2,128,768]{2,1,0:T(8,128)(2,1)}, bf16[2,128,768]{2,1,0:T(8,128)(2,1)}, bf16[2,128,768]{2,1,0:T(8,128)(2,1)}, f32[128,768]{1,0:T(8,128)...) custom-call(bf16[128,768]{1,0:T(8,128)(2,1)} %bitcast.12, ...), custom_call_target="tpu_custom_call" | custom-call | tf_op jit(solution)/shard_map/forward_layers/pallas_call | solution.py:1027
  153.7 144.4 %experts.1 = (bf16[128,768]{1,0:T(8,128)(2,1)}, f32[128,768]{1,0:T(8,128)}, f32[24,768]{1,0:T(8,128)}, bf16[2,768,768]{2,1,0:T(8,128)(2,1)}, bf16[2,768,768]{2,1...) custom-call(bf16[128,768]{1,0:T(8,128)(2,1)} %get-tuple-element.64.normed_ref, f32[128,768]{1,0:T(8,128)} %get-tuple-element.65.mid_ref, ...), custom_call_target="tpu_custom_call" | custom-call | tf_op jit(solution)/shard_map/experts/pallas_call | solution.py:2049
  298.1 156.7 %backward_layers.1 = (f32[128,768]{1,0:T(8,128)}, bf16[2,8,192,384]{3,2,1,0:T(8,128)(2,1)}, bf16[8,192,384]{2,1,0:T(8,128)(2,1)}, bf16[8,96,768]{2,1,0:T(8,128)(...) custom-call(f32[128,768]{1,0:T(8,128)} %get-tuple-element.73.mid_grad_ref, ...), custom_call_target="tpu_custom_call" | custom-call | tf_op jit(solution)/shard_map/backward_layers/pallas_call | solution.py:1627
  454.8 10.0 %finish.1 = (f32[2,192,2304]{2,1,0:T(8,128)}, f32[2,192,768]{2,1,0:T(8,128)}, f32[192,3072]{1,0:T(8,128)}, f32[768,768]{1,0:T(8,128)}, f32[2,192,3072]{2,1,0:T(8...) custom-call(bf16[2,8,192,384]{3,2,1,0:T(8,128)(2,1)} %get-tuple-elem, ...), custom_call_target="tpu_custom_call" | custom-call | tf_op jit(solution)/shard_map/finish/pallas_call | solution.py:2242

commit v6 on v5

--- a/solution.py
+++ b/solution.py
@@ -982,11 +982,10 @@
 
     def work5():
         cot_first(2)
+        cot_gathers[1].second()
+
+    def work6():
         cot_first(3)
-        cot_gathers[1].second()
-
-    def work6():
-        pass
 
     def work7():
         cot_gathers[1].third()
@@ -1524,8 +1523,9 @@
 
     loop(6, slope_part)
     exchange_start(2, gsrc.at[2])
+    gathers[2].first()
+    gathers[3].first()
     gathers[4].second()
-    gathers[5].second()
     got_up.wait()
     dense_grad = dot_rows(gsrc[2], w_wide[...])
     reloads["out"] = load(proj0_hbm, w_out, 9)
@@ -1537,27 +1537,28 @@
         p, early, early_z, early_p, jnp.add, (szs.at[1], szr.at[1], sps.at[1], spr.at[1])
     )
     small.start()
-    gathers[4].third()
-    gathers[5].third()
     got_early.wait()
     tile_attention(1)
 
     def part4():
+        gathers[5].second()
+        gathers[4].third()
+
+    def part5():
+        gathers[2].second()
+        gathers[3].second()
+        small.middle(early_m)
+
+    def part6():
+        gathers[5].third()
+
+    def part7():
         gathers[4].done()
         tile_up()
-
-    def part5():
         gathers[5].done()
         tile_down()
-
-    def part6():
-        small.middle(early_m)
-
-    def part7():
-        gathers[2].first()
-        gathers[3].first()
-        z_finish(0, zb.at[0], zin.at[0], 192, att_out.at[1])
-        gather_att1.first()
+        gathers[2].third()
+        gathers[3].third()
 
     normed_grad = attention(0, layer_grad[...], [part4, part5, part6, part7])
     input_grad, gain_grad = norm_pull(
@@ -1578,24 +1579,22 @@
         p, late, late_z, late_p, jnp.add, (szs.at[2], szr.at[2], sps.at[2], spr.at[2])
     )
     tail.start()
-    gathers[2].second()
-    gathers[3].second()
-    z_finish(2, zb.at[2], zin.at[2], 192, up_out)
-    gather_up.first()
-    gather_att1.second()
-    gathers[2].third()
-    gathers[3].third()
-    z_finish(3, zb_down, zin_down, 96, down_out)
-    gather_down.first()
-    gather_att1.third()
-    gather_up.second()
+    z_finish(0, zb.at[0], zin.at[0], 192, att_out.at[1])
+    gather_att1.first()
     gathers[2].done()
     gathers[3].done()
     tile_attention(0)
     tail.middle(late_m)
     small.finish(early_m, small_out)
+    z_finish(2, zb.at[2], zin.at[2], 192, up_out)
+    gather_up.first()
+    gather_att1.second()
+    z_finish(3, zb_down, zin_down, 96, down_out)
+    gather_down.first()
+    gather_up.second()
+    gather_att1.third()
+    gather_down.second()
     gather_up.third()
-    gather_down.second()
     gather_down.third()
     z_finish(1, zb.at[1], zin.at[1], 192, att_out.at[0])
     gather_att0.first()
@@ -1721,6 +1720,7 @@
     out_send,
     row_back,
     out_back,
+    out_ahead_in,
     slot_grads,
     slot_z,
     slot_sum,
@@ -1748,6 +1748,8 @@
     loads,
     early_s,
     early_r,
+    oas,
+    oar,
 ):
     p = Plane()
     e, s = p.e, p.s
@@ -1874,11 +1876,18 @@
 
     def give_back(k, source, target, send_sems, recv_sems):
         g = groups[k]
-        target[g, e] = source[g, :, e]
+        slot = k if source is row_send else k // 2
+        target[slot, e] = source[g, :, e]
         for i, d in enumerate(p.around):
             p.push(
-                source.at[g, :, d], target.at[g, e], send_sems.at[k, i], recv_sems.at[k, i], (d, s)
+                source.at[g, :, d], target.at[slot, e], send_sems.at[k, i], recv_sems.at[k, i],
+                (d, s),
             )
+
+    def out_ahead(k):
+        g = groups[k]
+        i = k // 2
+        p.push(out_send.at[g], out_ahead_in.at[i], oas.at[i], oar.at[i], (e, g))
 
     def step(k):
         select_rows(k)
@@ -1911,6 +1920,7 @@
     gathers[1].done()
     step(1)
     give_back(1, row_send, row_back, rs, rr)
+    out_ahead(1)
     gathers[2].third()
     gathers[3].third()
     select_cots(2)
@@ -1921,14 +1931,14 @@
     gathers[3].done()
     step(3)
     give_back(3, row_send, row_back, rs, rr)
-    for k in (1, 2, 3):
-        give_back(k, out_send, out_back, os, orr)
+    give_back(2, out_send, out_back, os, orr)
     give_back(0, row_send, row_back, rs, rr)
-    give_back(0, out_send, out_back, os, orr)
     for k in range(3):
         p.push(
             slot_grads.at[p.others[k]], slot_z.at[k], ss.at[k], sr.at[k], (e, p.others[k])
         )
+
+    out_ahead(3)
 
     def weight_grads(i):
         j = i // 3
@@ -1959,21 +1969,33 @@
 
     def collect(k, back, recv_sems, part, z_in, z_send, z_recv):
         g = groups[k]
+        slot = k if back is row_back else k // 2
         for i in range(7):
-            p.arrived(back.at[g, e], recv_sems.at[k, i])
+            p.arrived(back.at[slot, e], recv_sems.at[k, i])
         columns = slot_columns(g)
         marks = jnp.where(
             (columns[:, :1] == slot_lanes) | (columns[:, 1:2] == slot_lanes), 1.0, 0.0
         ).astype(bfloat)
         combined = jnp.dot(
-            marks, back[g].reshape(16 * CAP, D), preferred_element_type=single
+            marks, back[slot].reshape(16 * CAP, D), preferred_element_type=single
         )
-        part[g] = combined.astype(bfloat)
+        part[slot] = combined.astype(bfloat)
         if k:
-            p.push(part.at[g], z_in.at[k - 1], z_send.at[k - 1], z_recv.at[k - 1], (e, g))
+            i = k - 1 if back is row_back else 0
+            p.push(part.at[slot], z_in.at[i], z_send.at[i], z_recv.at[i], (e, g))
 
     for k in (1, 2, 3):
         collect(k, row_back, rr, row_part, row_z, rzs, rzr)
+
+    for i in range(2):
+        p.arrived(out_ahead_in.at[i], oar.at[i])
+    for j in range(2):
+        out_send[s, j] = (
+            out_send[s, j].astype(single)
+            + out_ahead_in[0, j].astype(single)
+            + out_ahead_in[1, j].astype(single)
+        ).astype(bfloat)
+    give_back(0, out_send, out_back, os, orr)
 
     def weight_later(i):
         weight_grads(i + 3)
@@ -2012,10 +2034,9 @@
     small_out[...] = jnp.zeros_like(small_out)
     small_out[:16, :] = dot_columns(logit_grad, normed_ref[...])
     normed_grad = jnp.dot(logit_grad, router_turned_ref[...], preferred_element_type=single)
-    for k in (1, 2, 3):
-        collect(k, out_back, orr, out_part, out_z, ozs, ozr)
+    collect(2, out_back, orr, out_part, out_z, ozs, ozr)
     collect(0, row_back, rr, row_part, row_z, rzs, rzr)
-    normed_grad = normed_grad + row_part[s].astype(single)
+    normed_grad = normed_grad + row_part[0].astype(single)
     for k in range(3):
         p.arrived(row_z.at[k], rzr.at[k])
         normed_grad = normed_grad + row_z[k].astype(single)
@@ -2024,10 +2045,8 @@
     mid_grad_out[...] = own_cot_ref[...].astype(single) + input_grad
 
     collect(0, out_back, orr, out_part, out_z, ozs, ozr)
-    result = mid_ref[...] + out_part[s].astype(single)
-    for k in range(3):
-        p.arrived(out_z.at[k], ozr.at[k])
-        result = result + out_z[k].astype(single)
+    p.arrived(out_z.at[0], ozr.at[0])
+    result = mid_ref[...] + out_part[0].astype(single) + out_z[0].astype(single)
     hidden_out[...] = result.astype(bfloat)
     for gather in early:
         gather.done()
@@ -2073,15 +2092,16 @@
             VMEM(sends, bfloat),
             VMEM(sends, bfloat),
             VMEM(backs, bfloat),
-            VMEM(backs, bfloat),
+            VMEM((2,) + backs[1:], bfloat),
+            VMEM((2,) + sends[1:], bfloat),
             VMEM((4, 8, 8 * CAP), single),
             VMEM((3, 8, 8 * CAP), single),
             VMEM((8, 8 * CAP), single),
             VMEM((8, 8, 8 * CAP), single),
             VMEM((4, T, D), bfloat),
-            VMEM((4, T, D), bfloat),
+            VMEM((2, T, D), bfloat),
             VMEM((3, T, D), bfloat),
-            VMEM((3, T, D), bfloat),
+            VMEM((1, T, D), bfloat),
             sem((3,)), sem((3,)),
             sem((4, 7)), sem((4, 7)),
             sem((4, 7)), sem((4, 7)),
@@ -2092,6 +2112,7 @@
             sem((3,)), sem((3,)),
             sem((8,)),
             sem((2, 7)), sem((2, 7)),
+            sem((2,)), sem((2,)),
         ],
         compiler_params=pltpu.CompilerParams(
             collective_id=4, has_side_effects=True, vmem_limit_bytes=60 * 2**20

time: 474 us -> 430 us (0.907)
  Pallas kernels: 460 us -> 417 us
    pallas_call x1, Pallas kernels: 144 us -> 116 us  [run_experts(): pl.pallas_call(experts_kernel, name='experts', out_shape=(shape((T, D), b...]
    pallas_call x1, Pallas kernels: 157 us -> 145 us  [backward(): pl.pallas_call(backward_kernel, name='backward_layers', out_shape=(shape(...]
where the time goes in v6:
time: 430 us; the launch traced here: 422 us
  Pallas kernels  417 us (97%)
    pallas_call x1, Pallas kernels, forward(): pl.pallas_call(forward_kernel, name='forward_layers', out_shape=(shape((2...  147 us
    pallas_call x1, Pallas kernels, backward(): pl.pallas_call(backward_kernel, name='backward_layers', out_shape=(shape(...  145 us
    pallas_call x1, Pallas kernels, run_experts(): pl.pallas_call(experts_kernel, name='experts', out_shape=(shape((T, D), b...  116 us
    pallas_call x1, Pallas kernels, finish(): pl.pallas_call(finish_kernel, name='finish', out_shape=tuple((jax.ShapeDt...  9.98 us

profile of v6, /device:TPU:0, one launch (start us, length us, event | category | flops | bytes accessed | tf_op | source)
XLA Modules:
  0.0 422.2 jit_solution(14467862648859325767)
XLA Ops:
  0.7 0.7 fusion.11
  1.4 0.7 copy.27
  2.1 0.1 reshape.49
  2.1 0.8 rev.3
  2.9 0.1 pad_dynamic-slice_fusion
  3.0 0.6 broadcast_in_dim.3.buckets_ref
  3.6 1.3 fusion.5.small_ref
  4.9 146.7 %forward_layers.1 = (bf16[2,128,768]{2,1,0:T(8,128)(2,1)}, bf16[2,128,768]{2,1,0:T(8,128)(2,1)}, bf16[2,128,768]{2,1,0:T(8,128)(2,1)}, f32[128,768]{1,0:T(8,128)...) custom-call(bf16[128,768]{1,0:T(8,128)(2,1)} %bitcast.12, ...), custom_call_target="tpu_custom_call" | custom-call | tf_op jit(solution)/shard_map/forward_layers/pallas_call | solution.py:1026
  151.6 115.6 %experts.1 = (bf16[128,768]{1,0:T(8,128)(2,1)}, f32[128,768]{1,0:T(8,128)}, f32[24,768]{1,0:T(8,128)}, bf16[2,768,768]{2,1,0:T(8,128)(2,1)}, bf16[2,768,768]{2,1...) custom-call(bf16[128,768]{1,0:T(8,128)(2,1)} %get-tuple-element.64.normed_ref, f32[128,768]{1,0:T(8,128)} %get-tuple-element.65.mid_ref, ...), custom_call_target="tpu_custom_call" | custom-call | tf_op jit(solution)/shard_map/experts/pallas_call | solution.py:2068
  267.2 144.5 %backward_layers.1 = (f32[128,768]{1,0:T(8,128)}, bf16[2,8,192,384]{3,2,1,0:T(8,128)(2,1)}, bf16[8,192,384]{2,1,0:T(8,128)(2,1)}, bf16[8,96,768]{2,1,0:T(8,128)(...) custom-call(f32[128,768]{1,0:T(8,128)} %get-tuple-element.73.mid_grad_ref, ...), custom_call_target="tpu_custom_call" | custom-call | tf_op jit(solution)/shard_map/backward_layers/pallas_call | solution.py:1626
  411.8 10.0 %finish.1 = (f32[2,192,2304]{2,1,0:T(8,128)}, f32[2,192,768]{2,1,0:T(8,128)}, f32[192,3072]{1,0:T(8,128)}, f32[768,768]{1,0:T(8,128)}, f32[2,192,3072]{2,1,0:T(8...) custom-call(bf16[2,8,192,384]{3,2,1,0:T(8,128)(2,1)} %get-tuple-elem, ...), custom_call_target="tpu_custom_call" | custom-call | tf_op jit(solution)/shard_map/finish/pallas_call | solution.py:2263
